TPU v7x, 32 devices: a whole 2x2x4 slice. The times are simulated.
32 devices in a mesh: seq: 16 (over z, y, x), tp: 2 (over core).
Axes of the slice: x: 2, y: 2, z: 4, core: 2. Of those that a mesh axis runs over, the one named last changes fastest.
Arguments:
- query_proj: bfloat16 [2048, 4096], P('seq', 'tp'), may hold values from -500 to 500
- key_proj: bfloat16 [2048, 4096], P('seq', 'tp'), may hold values from -500 to 500
- value_proj: bfloat16 [2048, 4096], P('seq', 'tp'), may hold values from -6 to 6
- query_gain: float32 [4096], P('tp'), may hold values from 0.5 to 1.5
- key_gain: float32 [4096], P('tp'), may hold values from 0.5 to 1.5
- live_tiles: int32 [32, 16, 4], P('tp'), may hold values from 0 to 15, as said below
- live_count: int32 [32, 16], P('tp'), may hold values from 1 to 4, as said below
Outputs:
- attended: bfloat16 [2048, 4096], P('seq', 'tp')
Inputs may be any that keep to these rules, and one draw needn't show every extreme that they name: `live_tiles`: the entries of a row are distinct tiles and the first is the row's own tile; only the first live_count of them are used. `live_count`: every head has a query tile with 4 live key tiles.
All inputs are finite; a program needn't handle non-finite values.
Results may differ from a plain program's by a relative error of at most 0.012.
The roundings to bfloat16 on the way count: a program that leaves them out, or rounds other values in their place, can miss the bound.
Values may be sent and summed in bfloat16 or wider, within the bound.
No kernel may reach another device: no remote copies, remote signals or barrier semaphores. Data moves between devices by JAX's collectives and lax.ppermute only.
A program may use at most 128 MiB of HBM per device.

v0:
```python
import math

import jax
import jax.numpy as jnp
from jax import lax
from jax.sharding import PartitionSpec as P

TILE = 128
QB = 4
SG = 4


epsilon = 1e-06


def normalize(field, gain, totals, width):
    values = field.astype(jnp.float32)
    return (values * lax.rsqrt(totals[:, None] / width + epsilon) * gain[None, :]).astype(
        jnp.bfloat16
    )


def local(query_proj, key_proj, value_proj, query_gain, key_gain, live_tiles, live_count):
    tokens_here = query_proj.shape[0]
    heads_here = live_tiles.shape[0]
    most_live = live_tiles.shape[2]
    head_width = query_proj.shape[1] // heads_here
    full_width = query_proj.shape[1] * lax.axis_size("tp")
    query_values = query_proj.astype(jnp.float32)
    key_values = key_proj.astype(jnp.float32)
    query_squares, key_squares = lax.psum(
        (jnp.sum(query_values * query_values, axis=1), jnp.sum(key_values * key_values, axis=1)),
        "tp",
    )
    normed_query = normalize(query_proj, query_gain, query_squares, full_width)
    normed_key = normalize(key_proj, key_gain, key_squares, full_width)
    stacked = jnp.concatenate(
        [
            normed_query.reshape(tokens_here, heads_here, head_width),
            normed_key.reshape(tokens_here, heads_here, head_width),
            value_proj.reshape(tokens_here, heads_here, head_width),
        ],
        axis=2,
    )
    device_count = lax.axis_size("seq")
    group_size = device_count // heads_here
    my_index = lax.axis_index("seq")
    my_head = my_index // group_size
    my_member = my_index % group_size
    triple = 3 * head_width
    outgoing = jnp.broadcast_to(
        stacked.transpose(1, 0, 2)[:, None], (heads_here, group_size, tokens_here, triple)
    )
    outgoing = outgoing.reshape(device_count, tokens_here, triple)
    incoming = lax.all_to_all(outgoing, "seq", split_axis=0, concat_axis=0, tiled=True)
    gathered = incoming.reshape(device_count * tokens_here, triple)
    tile_count = gathered.shape[0] // TILE
    query_tiles = gathered[:, :head_width].reshape(tile_count, TILE, head_width)
    key_tiles = gathered[:, head_width : 2 * head_width].reshape(tile_count, TILE, head_width)
    value_tiles = gathered[:, 2 * head_width :].reshape(tile_count, TILE, head_width)
    head_lists = lax.dynamic_index_in_dim(live_tiles, my_head, 0, keepdims=False)
    head_counts = lax.dynamic_index_in_dim(live_count, my_head, 0, keepdims=False)
    per_member = tile_count // group_size
    mine = my_member * per_member + jnp.arange(per_member, dtype=jnp.int32)
    score_scale = 1.0 / math.sqrt(head_width)
    block_count = per_member // QB
    query_block_slice = query_tiles[mine].reshape(block_count, QB, TILE, head_width)
    block_lists = head_lists[mine].reshape(block_count, QB, most_live)
    block_counts = head_counts[mine].reshape(block_count, QB)
    span = SG * TILE

    def attend(inputs):
        query_tile_rows, tile_lists, tile_counts = inputs
        turns = (jnp.max(tile_counts) + SG - 1) // SG

        def live_of(turn):
            slots = turn * SG + jnp.arange(SG, dtype=jnp.int32)
            return jnp.repeat(slots[None, :] < tile_counts[:, None], TILE, axis=1)[:, None, :]

        def score_turn(turn, stored):
            selected = lax.dynamic_slice_in_dim(tile_lists, turn * SG, SG, 1)
            collected_key_rows = key_tiles[selected].reshape(QB, span, head_width)
            logit_scores = (
                jnp.einsum(
                    "xzm,xym->xzy",
                    query_tile_rows,
                    collected_key_rows,
                    preferred_element_type=jnp.float32,
                )
                * score_scale
            )
            logit_scores = jnp.where(live_of(turn), logit_scores, -jnp.inf)
            return lax.dynamic_update_slice_in_dim(stored, logit_scores, turn * span, 2)

        stored = lax.fori_loop(
            0, turns, score_turn, jnp.full((QB, TILE, most_live * TILE), -jnp.inf, jnp.float32)
        )
        largest = jnp.max(stored, axis=-1, keepdims=True)

        def accumulate(turn, carry):
            weighted_value_sum, denominators = carry
            logit_scores = lax.dynamic_slice_in_dim(stored, turn * span, span, 2)
            selected = lax.dynamic_slice_in_dim(tile_lists, turn * SG, SG, 1)
            weights = jnp.where(live_of(turn), jnp.exp(logit_scores - largest), 0.0)
            collected_value_rows = value_tiles[selected].reshape(QB, span, head_width)
            weighted_value_sum = weighted_value_sum + jnp.einsum(
                "ihp,ipe->ihe",
                weights.astype(jnp.bfloat16),
                collected_value_rows,
                preferred_element_type=jnp.float32,
            )
            denominators = denominators + jnp.sum(weights, axis=-1, keepdims=True)
            return (weighted_value_sum, denominators)

        weighted_value_sum, denominators = lax.fori_loop(
            0,
            turns,
            accumulate,
            (jnp.zeros((QB, TILE, head_width), jnp.float32), jnp.zeros((QB, TILE, 1), jnp.float32)),
        )
        return (weighted_value_sum / denominators).astype(jnp.bfloat16)

    results = lax.map(attend, (query_block_slice, block_lists, block_counts)).reshape(
        per_member, TILE, head_width
    )
    placed = jnp.zeros((tile_count, TILE, head_width), jnp.bfloat16).at[mine].set(results)
    returned = lax.all_to_all(placed, "seq", split_axis=0, concat_axis=0, tiled=True)
    merged = (
        returned.reshape(heads_here, group_size, tokens_here, head_width)
        .astype(jnp.float32)
        .sum(axis=1)
    )
    merged = merged.astype(jnp.bfloat16).transpose(1, 0, 2)
    return merged.reshape(tokens_here, heads_here * head_width)


def solution(mesh):
    placed = (
        P("seq", "tp"),
        P("seq", "tp"),
        P("seq", "tp"),
        P("tp"),
        P("tp"),
        P("tp", None, None),
        P("tp", None),
    )
    return jax.shard_map(
        local, mesh=mesh, in_specs=placed, out_specs=P("seq", "tp"), check_vma=False
    )
```

profile of v0, /device:TPU:0, one launch (start us, length us, event | category | flops | bytes accessed | tf_op | source)
XLA Modules:
  0.0 111.4 jit_solution(18030997466334293558)
XLA Ops:
  0.0 1.4 %copy.30 = bf16[128,2048]{0,1:T(8,128)(2,1)S(1)} copy(bf16[128,2048]{1,0:T(8,128)(2,1)} %param.13) | data formatting | bytes 1048576 | tf_op args[0]
  2.6 2.6 %all-reduce = (f32[128]{0:T(128)S(1)}, f32[128]{0:T(128)S(1)}) all-reduce(f32[128]{0:T(128)S(1)} %fusion.13, f32[128]{0:T(128)S(1)} %fusion.10), channel_id=1, replica_groups=mesh['seq'=16,'tp'=2] {'tp'}, use_global_device_ids=true, to_apply=%region_3.0 | all-reduce | flops 256 | bytes 2048 | tf_op jit(solution)/shard_map/psum | solution.py:31
  6.0 1.6 %copy.33 = bf16[16,128,384]{2,1,0:T(8,128)(2,1)} copy(bf16[16,128,384]{1,2,0:T(8,128)(2,1)S(1)} %maximum_bitcast_fusion) | data formatting | bytes 3145728 | tf_op jit(solution)/shard_map/transpose | solution.py:52
  7.6 8.2 %all-to-all-start = ((bf16[16,128,384]{2,1,0:T(8,128)(2,1)}), bf16[16,128,384]{2,1,0:T(8,128)(2,1)S(1)}, u32[]{:S(2)}, u32[]{:S(2)}) async-start(bf16[16,128,384]{2,1,0:T(8,128)(2,1)} %copy.33), calls=%async_computation | async-start | bytes 3145728 | tf_op jit(solution)/shard_map/all_to_all | solution.py:55
  17.9 32.1 %all-to-all-done = bf16[16,128,384]{2,1,0:T(8,128)(2,1)S(1)} async-done(((bf16[16,128,384]{2,1,0:T(8,128)(2,1)}), bf16[16,128,384]{2,1,0:T(8,128)(2,1)S(1)}, u32[]{:S(2)}, u32[]{:S(2)}) %all-to-all-start) | async-done | bytes 1572896 | tf_op jit(solution)/shard_map/all_to_all | solution.py:55
  51.0 34.8 %while.72 = (s32[]{:T(128)}, bf16[4,4,128,128]{3,2,1,0:T(8,128)(2,1)}, s32[4,4]{1,0:T(4,128)S(1)}, s32[4,4,4]{2,1,0:T(4,128)S(1)}, bf16[4,4,128,128]{3,2,1,0:T(8...) while((s32[]{:T(128)}, ...), condition=%wide.region_12.13_spmd, body=%wide.region_4.12_spmd.sunk | while | flops 136774272 | bytes 14198653 | solution.py:123
  53.2 1.1 %broadcast.152 = f32[4,128,512]{2,1,0:T(8,128)} broadcast(f32[]{:T(128)} %constant.189.clone.1..sunk), dimensions={} | broadcast | bytes 1048580 | tf_op jit(solution)/shard_map/broadcast.96
  54.3 1.5 %while.73 = (s32[]{:T(128)}, f32[4,128,512]{2,1,0:T(8,128)}, s32[]{:T(128)}, s32[4]{0:T(128)S(1)}, bf16[4,4,128,128]{3,2,1,0:T(8,128)(2,1)S(1)}, /*index=5*/bf16[4,128,128]{2,1,0:T(8,128)(2,1)S(1)}, s32[]{:T(128)}, s32[]{:T(128)}) while((s32[]{:T(128)}, f32[4,128,512]{2,1,0:T(8,128)}, s32[]{:T(128)}, s32[4]{0:T(128)S(1)}, ...), condition=%wide.region_7.7_spmd, body=%wide.region_6.6_spmd.sunk | while | flops 67633176 | bytes 1712309 | solution.py:95
  54.5 1.3 %fusion.30 = f32[4,128,512]{2,1,0:T(8,128)} fusion(bf16[4,128,128]{2,1,0:T(8,128)(2,1)S(1)} %get-tuple-element.602, bf16[4,512,128]{2,1,0:T(8,128)(2,1)S(1)} %bitcast.90, pred[4,512]{1,0:T(4,128)(4,1)S(1)} %bitcast.100), kind=kOutput, calls=%fused_computation.7.clone.1 | convolution fusion | flops 67633152 | bytes 1705984 | tf_op jit(solution)/shard_map/while/body/eval_jaxpr/while/body/xzm,xym->xzy/dot_general | solution.py:84
  55.8 1.5 %reduce_max.34 = f32[4,128]{1,0:T(4,128)S(1)} reduce(f32[4,128,512]{2,1,0:T(8,128)} %get-tuple-element.611, f32[]{:T(128)} %constant.189.clone.1..sunk), dimensions={2}, to_apply=%region_8.8 | reduce | flops 261632 | bytes 1050628 | tf_op jit(solution)/shard_map/while/body/eval_jaxpr/reduce_max | solution.py:98
  58.0 0.9 while.74
  58.9 0.8 bitcast_dynamic-update-slice_fusion.2
  61.9 1.1 %broadcast.152 = f32[4,128,512]{2,1,0:T(8,128)} broadcast(f32[]{:T(128)} %constant.189.clone.1..sunk), dimensions={} | broadcast | bytes 1048580 | tf_op jit(solution)/shard_map/broadcast.96
  63.0 1.5 %while.73 = (s32[]{:T(128)}, f32[4,128,512]{2,1,0:T(8,128)}, s32[]{:T(128)}, s32[4]{0:T(128)S(1)}, bf16[4,4,128,128]{3,2,1,0:T(8,128)(2,1)S(1)}, /*index=5*/bf16[4,128,128]{2,1,0:T(8,128)(2,1)S(1)}, s32[]{:T(128)}, s32[]{:T(128)}) while((s32[]{:T(128)}, f32[4,128,512]{2,1,0:T(8,128)}, s32[]{:T(128)}, s32[4]{0:T(128)S(1)}, ...), condition=%wide.region_7.7_spmd, body=%wide.region_6.6_spmd.sunk | while | flops 67633176 | bytes 1712309 | solution.py:95
  63.2 1.3 %fusion.30 = f32[4,128,512]{2,1,0:T(8,128)} fusion(bf16[4,128,128]{2,1,0:T(8,128)(2,1)S(1)} %get-tuple-element.602, bf16[4,512,128]{2,1,0:T(8,128)(2,1)S(1)} %bitcast.90, pred[4,512]{1,0:T(4,128)(4,1)S(1)} %bitcast.100), kind=kOutput, calls=%fused_computation.7.clone.1 | convolution fusion | flops 67633152 | bytes 1705984 | tf_op jit(solution)/shard_map/while/body/eval_jaxpr/while/body/xzm,xym->xzy/dot_general | solution.py:84
  64.5 1.5 %reduce_max.34 = f32[4,128]{1,0:T(4,128)S(1)} reduce(f32[4,128,512]{2,1,0:T(8,128)} %get-tuple-element.611, f32[]{:T(128)} %constant.189.clone.1..sunk), dimensions={2}, to_apply=%region_8.8 | reduce | flops 261632 | bytes 1050628 | tf_op jit(solution)/shard_map/while/body/eval_jaxpr/reduce_max | solution.py:98
  66.7 0.9 while.74
  67.6 0.8 bitcast_dynamic-update-slice_fusion.2
  70.6 1.1 %broadcast.152 = f32[4,128,512]{2,1,0:T(8,128)} broadcast(f32[]{:T(128)} %constant.189.clone.1..sunk), dimensions={} | broadcast | bytes 1048580 | tf_op jit(solution)/shard_map/broadcast.96
  71.7 1.5 %while.73 = (s32[]{:T(128)}, f32[4,128,512]{2,1,0:T(8,128)}, s32[]{:T(128)}, s32[4]{0:T(128)S(1)}, bf16[4,4,128,128]{3,2,1,0:T(8,128)(2,1)S(1)}, /*index=5*/bf16[4,128,128]{2,1,0:T(8,128)(2,1)S(1)}, s32[]{:T(128)}, s32[]{:T(128)}) while((s32[]{:T(128)}, f32[4,128,512]{2,1,0:T(8,128)}, s32[]{:T(128)}, s32[4]{0:T(128)S(1)}, ...), condition=%wide.region_7.7_spmd, body=%wide.region_6.6_spmd.sunk | while | flops 67633176 | bytes 1712309 | solution.py:95
  71.9 1.3 %fusion.30 = f32[4,128,512]{2,1,0:T(8,128)} fusion(bf16[4,128,128]{2,1,0:T(8,128)(2,1)S(1)} %get-tuple-element.602, bf16[4,512,128]{2,1,0:T(8,128)(2,1)S(1)} %bitcast.90, pred[4,512]{1,0:T(4,128)(4,1)S(1)} %bitcast.100), kind=kOutput, calls=%fused_computation.7.clone.1 | convolution fusion | flops 67633152 | bytes 1705984 | tf_op jit(solution)/shard_map/while/body/eval_jaxpr/while/body/xzm,xym->xzy/dot_general | solution.py:84
  73.2 1.5 %reduce_max.34 = f32[4,128]{1,0:T(4,128)S(1)} reduce(f32[4,128,512]{2,1,0:T(8,128)} %get-tuple-element.611, f32[]{:T(128)} %constant.189.clone.1..sunk), dimensions={2}, to_apply=%region_8.8 | reduce | flops 261632 | bytes 1050628 | tf_op jit(solution)/shard_map/while/body/eval_jaxpr/reduce_max | solution.py:98
  75.4 0.9 while.74
  76.3 0.8 bitcast_dynamic-update-slice_fusion.2
  79.3 1.1 %broadcast.152 = f32[4,128,512]{2,1,0:T(8,128)} broadcast(f32[]{:T(128)} %constant.189.clone.1..sunk), dimensions={} | broadcast | bytes 1048580 | tf_op jit(solution)/shard_map/broadcast.96
  80.4 1.5 %while.73 = (s32[]{:T(128)}, f32[4,128,512]{2,1,0:T(8,128)}, s32[]{:T(128)}, s32[4]{0:T(128)S(1)}, bf16[4,4,128,128]{3,2,1,0:T(8,128)(2,1)S(1)}, /*index=5*/bf16[4,128,128]{2,1,0:T(8,128)(2,1)S(1)}, s32[]{:T(128)}, s32[]{:T(128)}) while((s32[]{:T(128)}, f32[4,128,512]{2,1,0:T(8,128)}, s32[]{:T(128)}, s32[4]{0:T(128)S(1)}, ...), condition=%wide.region_7.7_spmd, body=%wide.region_6.6_spmd.sunk | while | flops 67633176 | bytes 1712309 | solution.py:95
  80.6 1.3 %fusion.30 = f32[4,128,512]{2,1,0:T(8,128)} fusion(bf16[4,128,128]{2,1,0:T(8,128)(2,1)S(1)} %get-tuple-element.602, bf16[4,512,128]{2,1,0:T(8,128)(2,1)S(1)} %bitcast.90, pred[4,512]{1,0:T(4,128)(4,1)S(1)} %bitcast.100), kind=kOutput, calls=%fused_computation.7.clone.1 | convolution fusion | flops 67633152 | bytes 1705984 | tf_op jit(solution)/shard_map/while/body/eval_jaxpr/while/body/xzm,xym->xzy/dot_general | solution.py:84
  81.9 1.5 %reduce_max.34 = f32[4,128]{1,0:T(4,128)S(1)} reduce(f32[4,128,512]{2,1,0:T(8,128)} %get-tuple-element.611, f32[]{:T(128)} %constant.189.clone.1..sunk), dimensions={2}, to_apply=%region_8.8 | reduce | flops 261632 | bytes 1050628 | tf_op jit(solution)/shard_map/while/body/eval_jaxpr/reduce_max | solution.py:98
  84.1 0.9 while.74
  85.9 2.1 %scatter_fusion = bf16[16,128,128]{2,1,0:T(8,128)(2,1)S(1)} fusion(bf16[16,128,128]{2,1,0:T(8,128)(2,1)S(1)} %broadcast_in_dim.83, s32[16]{0:T(128)S(1)} %iota.26, bf16[16,128,128]{2,1,0:T(8,128)(2,1)} %bitcast.109), kind=kCustom, calls=%fused_computation.5 | custom fusion | bytes 1572928 | tf_op jit(solution)/shard_map/scatter | solution.py:126
  88.0 22.1 %all_to_all.10 = bf16[16,128,128]{2,1,0:T(8,128)(2,1)S(1)} all-to-all(bf16[16,128,128]{2,1,0:T(8,128)(2,1)S(1)} %scatter_fusion), channel_id=1, replica_groups=mesh['seq'=16,'tp'=2] {'seq'}, dimensions={0} | all-to-all | bytes 1048576 | tf_op jit(solution)/shard_map/all_to_all | solution.py:127
  110.4 1.0 copy.36
  (121 shorter events, 18.9 us)
Async XLA Ops:
  0.0 15.8 %copy-start = (s32[16,16,4]{1,2,0:T(4,128)S(1)}, s32[16,16,4]{1,2,0:T(4,128)}, u32[]{:S(2)}) copy-start(s32[16,16,4]{1,2,0:T(4,128)} %param.18) | copy-start | bytes 12292
  0.0 1.7 %copy-start.2 = (bf16[128,2048]{1,0:T(8,128)(2,1)S(1)}, bf16[128,2048]{1,0:T(8,128)(2,1)}, u32[]{:S(2)}) copy-start(bf16[128,2048]{1,0:T(8,128)(2,1)} %param.14) | copy-start | bytes 1572868
  0.0 2.3 %copy-start.3 = (bf16[128,2048]{1,0:T(8,128)(2,1)S(1)}, bf16[128,2048]{1,0:T(8,128)(2,1)}, u32[]{:S(2)}) copy-start(bf16[128,2048]{1,0:T(8,128)(2,1)} %param.15) | copy-start | bytes 1572868
  1.4 3.8 %copy-start.4 = (f32[2048]{0:T(1024)S(1)}, f32[2048]{0:T(1024)}, u32[]{:S(2)}) copy-start(f32[2048]{0:T(1024)} %param.16) | copy-start | bytes 24580
  2.0 3.5 %copy-start.5 = (f32[2048]{0:T(1024)S(1)}, f32[2048]{0:T(1024)}, u32[]{:S(2)}) copy-start(f32[2048]{0:T(1024)} %param.17) | copy-start | bytes 24580
  7.6 42.5 %all-to-all-start = ((bf16[16,128,384]{2,1,0:T(8,128)(2,1)}), bf16[16,128,384]{2,1,0:T(8,128)(2,1)S(1)}, u32[]{:S(2)}, u32[]{:S(2)}) async-start(bf16[16,128,384]{2,1,0:T(8,128)(2,1)} %copy.33), calls=%async_computation | async-start | bytes 3145728 | tf_op jit(solution)/shard_map/all_to_all | solution.py:55
  55.8 2.2 %copy-start.1 = (f32[4,128,512]{2,1,0:T(8,128)S(1)}, f32[4,128,512]{2,1,0:T(8,128)}, u32[]{:S(2)}) copy-start(f32[4,128,512]{2,1,0:T(8,128)} %get-tuple-element.611) | copy-start | bytes 3145732 | tf_op jit(solution)/shard_map/while
  64.5 2.2 %copy-start.1 = (f32[4,128,512]{2,1,0:T(8,128)S(1)}, f32[4,128,512]{2,1,0:T(8,128)}, u32[]{:S(2)}) copy-start(f32[4,128,512]{2,1,0:T(8,128)} %get-tuple-element.611) | copy-start | bytes 3145732 | tf_op jit(solution)/shard_map/while
  73.2 2.2 %copy-start.1 = (f32[4,128,512]{2,1,0:T(8,128)S(1)}, f32[4,128,512]{2,1,0:T(8,128)}, u32[]{:S(2)}) copy-start(f32[4,128,512]{2,1,0:T(8,128)} %get-tuple-element.611) | copy-start | bytes 3145732 | tf_op jit(solution)/shard_map/while
  81.9 2.2 %copy-start.1 = (f32[4,128,512]{2,1,0:T(8,128)S(1)}, f32[4,128,512]{2,1,0:T(8,128)}, u32[]{:S(2)}) copy-start(f32[4,128,512]{2,1,0:T(8,128)} %get-tuple-element.611) | copy-start | bytes 3145732 | tf_op jit(solution)/shard_map/while
where the time goes:
time: 112 us; the launch traced here: 111 us
  waiting for transfers between devices  32.1 us (29%)
  blocking collectives  24.7 us (22%)
  local copies, waits for them, and re-layouts  20.9 us (19%)
  other arithmetic  15.3 us (14%)
  starting transfers between devices  8.2 us (7%)
  matrix products  6.63 us (6%)
  loops' own time  3.35 us (3%)
    all_to_all x1, waiting for transfers between devices, local(): lax.all_to_all(outgoing, 'seq', split_axis=0, concat_axis=0, tiled=True)  32.1 us
    all_to_all x1, blocking collectives, local(): lax.all_to_all(placed, 'seq', split_axis=0, concat_axis=0, tiled=True)  22.1 us
    all_to_all x1, starting transfers between devices, local(): lax.all_to_all(outgoing, 'seq', split_axis=0, concat_axis=0, tiled=True)  8.2 us
    reduce_max x4, other arithmetic, attend(): largest = jnp.max(stored, axis=-1, keepdims=True)  5.84 us
    dot_general x4, matrix products, score_turn(): jnp.einsum('xzm,xym->xzy', query_tile_rows, collected_key_rows, preferred...  5.17 us
    another operation x12, local copies, waits for them, and re-layouts  4.57 us
    dynamic_update_slice x4, other arithmetic, local(): lax.map(attend, (query_block_slice, block_lists, block_counts))  3.21 us
    another operation x1, loops' own time, local(): lax.map(attend, (query_block_slice, block_lists, block_counts))  3.16 us
  transfers between devices with their start and end apart: 1, of which 1 were waited for; matrix products, arithmetic and copies ran while one was open for 2% of the time, Pallas kernels for 0%

commit v1 on v0

v1 whole, which is shorter than its diff:
```python
import functools
import math

import jax
import jax.numpy as jnp
from jax import lax
from jax.experimental import pallas as pl
from jax.experimental.pallas import tpu as pltpu
from jax.sharding import PartitionSpec as P

TILE = 128
LANES = 128
epsilon = 1e-06


def pack_kernel(query_ref, key_ref, value_ref, packed_ref, sems):
    heads, _, triple = packed_ref.shape
    width = triple // 3
    copies = []
    for place, source in enumerate((query_ref, key_ref, value_ref)):
        for head in range(heads):
            copies.append(
                pltpu.make_async_copy(
                    source.at[:, pl.ds(head * width, width)],
                    packed_ref.at[head, :, pl.ds(place * width, width)],
                    sems.at[place, head],
                )
            )
    for copy in copies:
        copy.start()
    for copy in copies:
        copy.wait()


def pack(query, key, value, heads):
    tokens, columns = query.shape
    return pl.pallas_call(
        pack_kernel,
        out_shape=jax.ShapeDtypeStruct((heads, tokens, 3 * columns // heads), query.dtype),
        in_specs=[pl.BlockSpec(memory_space=pl.ANY)] * 3,
        out_specs=pl.BlockSpec(memory_space=pl.ANY),
        scratch_shapes=[pltpu.SemaphoreType.DMA((3, heads))],
        name="pack_heads",
    )(query, key, value)


def unpack_kernel(heads_ref, out_ref, sems):
    heads, _, width = heads_ref.shape
    copies = [
        pltpu.make_async_copy(
            heads_ref.at[head], out_ref.at[:, pl.ds(head * width, width)], sems.at[head]
        )
        for head in range(heads)
    ]
    for copy in copies:
        copy.start()
    for copy in copies:
        copy.wait()


def unpack(by_head):
    heads, tokens, width = by_head.shape
    return pl.pallas_call(
        unpack_kernel,
        out_shape=jax.ShapeDtypeStruct((tokens, heads * width), by_head.dtype),
        in_specs=[pl.BlockSpec(memory_space=pl.ANY)],
        out_specs=pl.BlockSpec(memory_space=pl.ANY),
        scratch_shapes=[pltpu.SemaphoreType.DMA((heads,))],
        name="unpack_heads",
    )(by_head)


def attend_kernel(
    most_live, lists, counts, base, factors_ref, gains_ref, gathered_ref, out_ref, columns, normed_key
):
    head_width = out_ref.shape[2]
    tile_count = gathered_ref.shape[0] // TILE
    scale = math.log2(math.e) / math.sqrt(head_width)
    for block in range(columns.shape[0]):
        columns[block] = factors_ref[block * LANES : (block + 1) * LANES, :].T

    def column(which):
        lane = lax.broadcasted_iota(jnp.int32, (TILE, LANES), 1)
        block = columns[which // LANES]
        return jnp.sum(jnp.where(lane == which % LANES, block, 0.0), axis=1, keepdims=True)

    def normalize(rows, place, which):
        values = gathered_ref[rows, place * head_width : (place + 1) * head_width]
        values = values.astype(jnp.float32) * column(which) * gains_ref[place : place + 1, :]
        return values.astype(jnp.bfloat16)

    def rows_of(tile):
        return pl.ds(pl.multiple_of(tile * TILE, TILE), TILE)

    def key_step(tile, carry):
        normed_key[rows_of(tile), :] = normalize(rows_of(tile), 1, tile_count + tile)
        return carry

    lax.fori_loop(0, tile_count, key_step, 0, unroll=4)

    def query_step(step, carry):
        tile = base[0] + step
        query = normalize(rows_of(tile), 0, tile)
        live = [lists[step * most_live + slot] for slot in range(most_live)]
        count = counts[step]
        scores = []
        for slot in range(most_live):
            score = lax.dot_general(
                query,
                normed_key[rows_of(live[slot]), :],
                (((1,), (1,)), ((), ())),
                preferred_element_type=jnp.float32,
            )
            scores.append(score if slot == 0 else jnp.where(slot < count, score, -jnp.inf))
        largest = functools.reduce(jnp.maximum, scores)
        largest = jnp.max(largest, axis=1, keepdims=True)
        weights = [jnp.exp2((score - largest) * scale) for score in scores]
        denominators = jnp.sum(functools.reduce(jnp.add, weights), axis=1, keepdims=True)
        total = jnp.zeros((TILE, head_width), jnp.float32)
        for slot in range(most_live):
            total = total + jnp.dot(
                weights[slot].astype(jnp.bfloat16),
                gathered_ref[rows_of(live[slot]), 2 * head_width :],
                preferred_element_type=jnp.float32,
            )
        out_ref[step] = (total / denominators).astype(out_ref.dtype)
        return carry

    lax.fori_loop(0, out_ref.shape[0], query_step, 0, unroll=max(1, 8 // most_live))


def attend(gathered, factors, gains, lists, counts, base, tiles):
    head_width = gathered.shape[1] // 3
    most_live = lists.shape[1]
    tile_count = gathered.shape[0] // TILE
    blocks = -(-factors.shape[0] // LANES)
    factors = jnp.pad(factors, ((0, blocks * LANES - factors.shape[0]), (0, 0)))
    smem = pl.BlockSpec(memory_space=pltpu.SMEM)
    vmem = pl.BlockSpec(memory_space=pltpu.VMEM)
    return pl.pallas_call(
        functools.partial(attend_kernel, most_live),
        out_shape=jax.ShapeDtypeStruct((tiles, TILE, head_width), jnp.bfloat16),
        in_specs=[smem] * 3 + [vmem] * 3,
        out_specs=vmem,
        scratch_shapes=[
            pltpu.VMEM((blocks, LANES, LANES), jnp.float32),
            pltpu.VMEM((tile_count * TILE, head_width), jnp.bfloat16),
        ],
        compiler_params=pltpu.CompilerParams(vmem_limit_bytes=48 * 1024 * 1024),
        name="attend",
    )(lists.reshape(-1), counts, base, factors, gains, gathered)


def gather_over(values, axis):
    count = lax.axis_size(axis)
    if count & (count - 1):
        return lax.all_gather(values, axis)
    me = lax.axis_index(axis)
    held = values[None]
    reach = 1
    while reach < count:
        other = lax.ppermute(held, axis, [(i, i ^ reach) for i in range(count)])
        upper = (me & reach) != 0
        held = jnp.where(
            upper, jnp.concatenate([other, held], 0), jnp.concatenate([held, other], 0)
        )
        reach *= 2
    return held


def local(query_proj, key_proj, value_proj, query_gain, key_gain, live_tiles, live_count):
    tokens_here = query_proj.shape[0]
    heads_here = live_tiles.shape[0]
    head_width = query_proj.shape[1] // heads_here
    full_width = query_proj.shape[1] * lax.axis_size("tp")
    device_count = lax.axis_size("seq")
    group_size = device_count // heads_here
    my_index = lax.axis_index("seq")
    my_head = my_index // group_size
    my_member = my_index % group_size

    outgoing = pack(query_proj, key_proj, value_proj, heads_here)
    if group_size > 1:
        outgoing = jnp.repeat(outgoing, group_size, axis=0)
    incoming = lax.all_to_all(outgoing, "seq", split_axis=0, concat_axis=0, tiled=True)
    gathered = incoming.reshape(device_count * tokens_here, 3 * head_width)

    query_values = query_proj.astype(jnp.float32)
    key_values = key_proj.astype(jnp.float32)
    squares = jnp.stack(
        [jnp.sum(query_values * query_values, axis=1), jnp.sum(key_values * key_values, axis=1)]
    )
    squares = lax.psum(squares, "tp")
    factors = gather_over(lax.rsqrt(squares / full_width + epsilon), "seq")
    tile_count = device_count * tokens_here // TILE
    factors = factors.transpose(1, 0, 2).reshape(2 * tile_count, TILE)
    gains = jnp.stack([query_gain, key_gain]).reshape(2, heads_here, head_width)
    gains = lax.dynamic_index_in_dim(gains, my_head, 1, keepdims=False)

    per_member = tile_count // group_size
    base = my_member * per_member
    lists = lax.dynamic_index_in_dim(live_tiles, my_head, 0, keepdims=False)
    counts = lax.dynamic_index_in_dim(live_count, my_head, 0, keepdims=False)
    lists = lax.dynamic_slice_in_dim(lists, base, per_member, 0)
    counts = lax.dynamic_slice_in_dim(counts, base, per_member, 0)
    results = attend(
        gathered, factors, gains, lists, counts, base.astype(jnp.int32).reshape(1), per_member
    )
    if group_size > 1:
        placed = jnp.zeros((tile_count, TILE, head_width), jnp.bfloat16)
        results = lax.dynamic_update_slice_in_dim(placed, results, base, 0)
    results = results.reshape(device_count, tokens_here, head_width)
    returned = lax.all_to_all(results, "seq", split_axis=0, concat_axis=0, tiled=True)
    if group_size > 1:
        returned = returned.reshape(heads_here, group_size, tokens_here, head_width)
        returned = returned.astype(jnp.float32).sum(axis=1).astype(jnp.bfloat16)
    return unpack(returned)


def solution(mesh):
    placed = (
        P("seq", "tp"),
        P("seq", "tp"),
        P("seq", "tp"),
        P("tp"),
        P("tp"),
        P("tp", None, None),
        P("tp", None),
    )
    return jax.shard_map(
        local, mesh=mesh, in_specs=placed, out_specs=P("seq", "tp"), check_vma=False
    )
```

time: 112 us -> 140 us (1.25)
  Pallas kernels: 0 us -> 74.6 us
  local copies, waits for them, and re-layouts: 20.9 us -> 0.9 us
  other arithmetic: 15.3 us -> 0.43 us
  starting transfers between devices: 8.2 us -> 18.7 us
  waiting for transfers between devices: 32.1 us -> 23.2 us
  matrix products: 6.63 us -> 0 us
  loops' own time: 3.35 us -> 0 us
  blocking collectives: 24.7 us -> 21.8 us
    pallas_call x0 -> x3, Pallas kernels: none -> 74.6 us  [the longest x1 49.2 us: pack(): pl.pallas_call(pack_kernel, out_shape=jax.ShapeDtypeStruct((heads, tokens...]
    all_to_all x1, waiting for transfers between devices: 32.1 us -> 0.01 us  [local(): lax.all_to_all(outgoing, 'seq', split_axis=0, concat_axis=0, tiled=True)]
    ppermute x0 -> x4, waiting for transfers between devices: none -> 23.2 us  [gather_over(): other = lax.ppermute(held, axis, [(i, i ^ reach) for i in range(count)])]
    ppermute x0 -> x4, starting transfers between devices: none -> 10.3 us  [gather_over(): other = lax.ppermute(held, axis, [(i, i ^ reach) for i in range(count)])]
    gather x11 -> x0, local copies, waits for them, and re-layouts: 7.05 us -> none  [the longest x4 2.59 us: score_turn(): collected_key_rows = key_tiles[selected].reshape(QB, span, head_width)]
    dot_general x8 -> x0, matrix products: 6.63 us -> none  [the longest x4 5.17 us: score_turn(): jnp.einsum('xzm,xym->xzy', query_tile_rows, collected_key_rows, preferred...]
    reduce_max x4 -> x0, other arithmetic: 5.84 us -> none  [attend(): largest = jnp.max(stored, axis=-1, keepdims=True)]
    another operation x12 -> x0, local copies, waits for them, and re-layouts: 4.57 us -> none
  transfers between devices with their start and end apart: 1 -> 5, of which waited for: 1 -> 4; matrix products, arithmetic and copies ran while one was open for 2% -> 1% of each run, Pallas kernels for 0% -> 0%
where the time goes in v1:
time: 140 us
  Pallas kernels  74.6 us (53%)
  waiting for transfers between devices  23.2 us (17%)
  blocking collectives  21.8 us (16%)
  starting transfers between devices  18.7 us (13%)
    pallas_call x1, Pallas kernels, pack(): pl.pallas_call(pack_kernel, out_shape=jax.ShapeDtypeStruct((heads, tokens...  49.2 us
    ppermute x4, waiting for transfers between devices, gather_over(): other = lax.ppermute(held, axis, [(i, i ^ reach) for i in range(count)])  23.2 us
    all_to_all x1, blocking collectives, local(): lax.all_to_all(results, 'seq', split_axis=0, concat_axis=0, tiled=True)  19.3 us
    pallas_call x1, Pallas kernels, unpack(): pl.pallas_call(unpack_kernel, out_shape=jax.ShapeDtypeStruct((tokens, hea...  17.1 us
    ppermute x4, starting transfers between devices, gather_over(): other = lax.ppermute(held, axis, [(i, i ^ reach) for i in range(count)])  10.3 us
    all_to_all x1, starting transfers between devices, local(): lax.all_to_all(outgoing, 'seq', split_axis=0, concat_axis=0, tiled=True)  8.46 us
    pallas_call x1, Pallas kernels, attend(): pl.pallas_call(functools.partial(attend_kernel, most_live), out_shape=jax...  8.31 us
  transfers between devices with their start and end apart: 5, of which 4 were waited for; matrix products, arithmetic and copies ran while one was open for 1% of the time, Pallas kernels for 0%

profile of v1, /device:TPU:0, one launch (start us, length us, event | category | flops | bytes accessed | tf_op | source)
XLA Modules:
  0.0 139.7 jit_solution(3638086202625207016)
XLA Ops:
  0.0 0.0 copy-start
  0.0 49.2 %pack_heads.1 = bf16[16,128,384]{2,1,0:T(8,128)(2,1)} custom-call(bf16[128,2048]{1,0:T(8,128)(2,1)} %query_ref.1, bf16[128,2048]{1,0:T(8,128)(2,1)} %key_ref.1, bf16[128,2048]{1,0:T(8,128)(2,1)} %value_ref.1), custom_call_target="tpu_custom_call" | custom-call | tf_op jit(solution)/shard_map/pack_heads/pallas_call | solution.py:37
  49.2 0.0 copy-start.1
  49.2 0.0 copy-start.2
  49.2 0.0 copy-start.3
  49.2 0.0 copy-start.4
  49.2 8.5 %all-to-all-start = ((bf16[16,128,384]{2,1,0:T(8,128)(2,1)}), bf16[16,128,384]{2,1,0:T(8,128)(2,1)S(1)}, u32[]{:S(2)}, u32[]{:S(2)}) async-start(bf16[16,128,384]{2,1,0:T(8,128)(2,1)} %pack_heads.1), calls=%async_computation | async-start | bytes 3145728 | tf_op jit(solution)/shard_map/all_to_all | solution.py:185
  57.7 0.0 copy-done.1
  57.7 0.2 multiply_reduce_fusion.1
  57.9 0.0 copy-done.2
  57.9 0.2 multiply_reduce_fusion
  58.1 2.5 %psum.7 = f32[2,128]{1,0:T(2,128)S(1)} all-reduce(f32[2,128]{1,0:T(2,128)S(1)} %pad_maximum_fusion), channel_id=1, replica_groups=mesh['seq'=16,'tp'=2] {'tp'}, use_global_device_ids=true, to_apply=%region_2.3 | all-reduce | flops 256 | bytes 2048 | tf_op jit(solution)/shard_map/psum | solution.py:193
  60.6 1.9 %collective-permute-start = (f32[1,2,128]{2,1,0:T(2,128)S(1)}, f32[1,2,128]{2,1,0:T(2,128)S(1)}, u32[]{:S(2)}, u32[]{:S(2)}) collective-permute-start(f32[1,2,128]{2,1,0:T(2,128)S(1)} %rsqrt_bitcast_fusion), channel_id=1, source_target_pairs={{0,2},{2,0},{4,6},{6,4},{8,10},{10,8},{12,14},{14,12},{16,18},{18,... | collective-permute-start | bytes 3080 | tf_op jit(solution)/shard_map/ppermute | solution.py:162
  62.5 1.7 %collective-permute-done = f32[1,2,128]{2,1,0:T(2,128)S(1)} collective-permute-done((f32[1,2,128]{2,1,0:T(2,128)S(1)}, f32[1,2,128]{2,1,0:T(2,128)S(1)}, u32[]{:S(2)}, u32[]{:S(2)}) %collective-permute-start) | collective-permute-done | bytes 1056 | tf_op jit(solution)/shard_map/ppermute | solution.py:162
  64.2 1.9 %collective-permute-start.1 = (f32[2,2,128]{2,1,0:T(2,128)S(1)}, f32[2,2,128]{2,1,0:T(2,128)S(1)}, u32[]{:S(2)}, u32[]{:S(2)}) collective-permute-start(f32[2,2,128]{2,1,0:T(2,128)S(1)} %maximum_select_fusion.3), channel_id=1, source_target_pairs={{0,4},{2,6},{4,0},{6,2},{8,12},{10,14},{12,8},{14,10},{16,20},{18,... | collective-permute-start | bytes 6152 | tf_op jit(solution)/shard_map/ppermute | solution.py:162
  66.1 0.0 copy-done
  66.1 1.7 %collective-permute-done.1 = f32[2,2,128]{2,1,0:T(2,128)S(1)} collective-permute-done((f32[2,2,128]{2,1,0:T(2,128)S(1)}, f32[2,2,128]{2,1,0:T(2,128)S(1)}, u32[]{:S(2)}, u32[]{:S(2)}) %collective-permute-start.1) | collective-permute-done | bytes 2080 | tf_op jit(solution)/shard_map/ppermute | solution.py:162
  67.8 1.9 %collective-permute-start.2 = (f32[4,2,128]{2,1,0:T(2,128)S(1)}, f32[4,2,128]{2,1,0:T(2,128)S(1)}, u32[]{:S(2)}, u32[]{:S(2)}) collective-permute-start(f32[4,2,128]{2,1,0:T(2,128)S(1)} %maximum_select_fusion.2), channel_id=1, source_target_pairs={{0,8},{2,10},{4,12},{6,14},{8,0},{10,2},{12,4},{14,6},{16,24},{18,... | collective-permute-start | bytes 12296 | tf_op jit(solution)/shard_map/ppermute | solution.py:162
  69.7 0.0 copy-done.3
  69.7 0.0 copy-done.4
  69.7 13.6 %collective-permute-done.2 = f32[4,2,128]{2,1,0:T(2,128)S(1)} collective-permute-done((f32[4,2,128]{2,1,0:T(2,128)S(1)}, f32[4,2,128]{2,1,0:T(2,128)S(1)}, u32[]{:S(2)}, u32[]{:S(2)}) %collective-permute-start.2) | collective-permute-done | bytes 4128 | tf_op jit(solution)/shard_map/ppermute | solution.py:162
  83.3 4.6 %collective-permute-start.3 = (f32[8,2,128]{2,1,0:T(2,128)S(1)}, f32[8,2,128]{2,1,0:T(2,128)S(1)}, u32[]{:S(2)}, u32[]{:S(2)}) collective-permute-start(f32[8,2,128]{2,1,0:T(2,128)S(1)} %maximum_select_fusion.1), channel_id=1, source_target_pairs={{0,16},{2,18},{4,20},{6,22},{8,24},{10,26},{12,28},{14,30},{16,0},... | collective-permute-start | bytes 24584 | tf_op jit(solution)/shard_map/ppermute | solution.py:162
  87.9 0.7 fusion.3.counts
  88.6 0.1 copy.10
  88.7 0.1 reshape.16.lists
  88.7 6.2 %collective-permute-done.3 = f32[8,2,128]{2,1,0:T(2,128)S(1)} collective-permute-done((f32[8,2,128]{2,1,0:T(2,128)S(1)}, f32[8,2,128]{2,1,0:T(2,128)S(1)}, u32[]{:S(2)}, u32[]{:S(2)}) %collective-permute-start.3) | collective-permute-done | bytes 8224 | tf_op jit(solution)/shard_map/ppermute | solution.py:162
  95.0 0.0 all-to-all-done
  95.0 8.3 %attend.1 = bf16[16,128,128]{2,1,0:T(8,128)(2,1)S(1)} custom-call(s32[64]{0:T(128)S(1)} %reshape.16.lists, s32[16]{0:T(128)S(1)} %fusion.3.counts, s32[1]{0:T(128)} %constant.51.clone.1.base, f32[128,128]{1,0:T(8,128)S(1)} %pad.4.factors_ref, f32[2,128]{1,0:T(2,128)S(1)} %fusion.2.gains_ref, bf16[2048,384]{1,0:T(8,128)(2,1)S(1)} %bitcast.14), custom_call_target="tpu_custom_call" | custom-call | tf_op jit(solution)/shard_map/attend/pallas_call | solution.py:140
  103.3 19.3 %all_to_all.10.heads_ref = bf16[16,128,128]{2,1,0:T(8,128)(2,1)} all-to-all(bf16[16,128,128]{2,1,0:T(8,128)(2,1)S(1)} %attend.1), channel_id=1, replica_groups=mesh['seq'=16,'tp'=2] {'seq'}, dimensions={0} | all-to-all | bytes 1048576 | tf_op jit(solution)/shard_map/all_to_all | solution.py:213
  122.6 17.1 %unpack_heads.1 = bf16[128,2048]{1,0:T(8,128)(2,1)} custom-call(bf16[16,128,128]{2,1,0:T(8,128)(2,1)} %all_to_all.10.heads_ref), custom_call_target="tpu_custom_call" | custom-call | tf_op jit(solution)/shard_map/unpack_heads/pallas_call | solution.py:63
  (10 shorter events, 0.1 us)
Async XLA Ops:
  0.0 66.1 %copy-start = (s32[16,16,4]{1,2,0:T(4,128)S(1)}, s32[16,16,4]{1,2,0:T(4,128)}, u32[]{:S(2)}) copy-start(s32[16,16,4]{1,2,0:T(4,128)} %param.12) | copy-start | bytes 12292
  49.2 8.5 %copy-start.1 = (bf16[128,2048]{1,0:T(8,128)(2,1)S(1)}, bf16[128,2048]{1,0:T(8,128)(2,1)}, u32[]{:S(2)}) copy-start(bf16[128,2048]{1,0:T(8,128)(2,1)} %query_ref.1) | copy-start | bytes 1572868
  49.2 8.7 %copy-start.2 = (bf16[128,2048]{1,0:T(8,128)(2,1)S(1)}, bf16[128,2048]{1,0:T(8,128)(2,1)}, u32[]{:S(2)}) copy-start(bf16[128,2048]{1,0:T(8,128)(2,1)} %key_ref.1) | copy-start | bytes 1572868
  49.2 20.5 %copy-start.3 = (f32[2048]{0:T(1024)S(1)}, f32[2048]{0:T(1024)}, u32[]{:S(2)}) copy-start(f32[2048]{0:T(1024)} %param.11) | copy-start | bytes 24580
  49.2 20.5 %copy-start.4 = (f32[2048]{0:T(1024)S(1)}, f32[2048]{0:T(1024)}, u32[]{:S(2)}) copy-start(f32[2048]{0:T(1024)} %param.10) | copy-start | bytes 24580
  49.2 45.8 %all-to-all-start = ((bf16[16,128,384]{2,1,0:T(8,128)(2,1)}), bf16[16,128,384]{2,1,0:T(8,128)(2,1)S(1)}, u32[]{:S(2)}, u32[]{:S(2)}) async-start(bf16[16,128,384]{2,1,0:T(8,128)(2,1)} %pack_heads.1), calls=%async_computation | async-start | bytes 3145728 | tf_op jit(solution)/shard_map/all_to_all | solution.py:185
  60.6 3.6 %collective-permute-start = (f32[1,2,128]{2,1,0:T(2,128)S(1)}, f32[1,2,128]{2,1,0:T(2,128)S(1)}, u32[]{:S(2)}, u32[]{:S(2)}) collective-permute-start(f32[1,2,128]{2,1,0:T(2,128)S(1)} %rsqrt_bitcast_fusion), channel_id=1, source_target_pairs={{0,2},{2,0},{4,6},{6,4},{8,10},{10,8},{12,14},{14,12},{16,18},{18,... | collective-permute-start | bytes 3080 | tf_op jit(solution)/shard_map/ppermute | solution.py:162
  64.2 3.6 %collective-permute-start.1 = (f32[2,2,128]{2,1,0:T(2,128)S(1)}, f32[2,2,128]{2,1,0:T(2,128)S(1)}, u32[]{:S(2)}, u32[]{:S(2)}) collective-permute-start(f32[2,2,128]{2,1,0:T(2,128)S(1)} %maximum_select_fusion.3), channel_id=1, source_target_pairs={{0,4},{2,6},{4,0},{6,2},{8,12},{10,14},{12,8},{14,10},{16,20},{18,... | collective-permute-start | bytes 6152 | tf_op jit(solution)/shard_map/ppermute | solution.py:162
  67.8 15.5 %collective-permute-start.2 = (f32[4,2,128]{2,1,0:T(2,128)S(1)}, f32[4,2,128]{2,1,0:T(2,128)S(1)}, u32[]{:S(2)}, u32[]{:S(2)}) collective-permute-start(f32[4,2,128]{2,1,0:T(2,128)S(1)} %maximum_select_fusion.2), channel_id=1, source_target_pairs={{0,8},{2,10},{4,12},{6,14},{8,0},{10,2},{12,4},{14,6},{16,24},{18,... | collective-permute-start | bytes 12296 | tf_op jit(solution)/shard_map/ppermute | solution.py:162
  83.3 11.6 %collective-permute-start.3 = (f32[8,2,128]{2,1,0:T(2,128)S(1)}, f32[8,2,128]{2,1,0:T(2,128)S(1)}, u32[]{:S(2)}, u32[]{:S(2)}) collective-permute-start(f32[8,2,128]{2,1,0:T(2,128)S(1)} %maximum_select_fusion.1), channel_id=1, source_target_pairs={{0,16},{2,18},{4,20},{6,22},{8,24},{10,26},{12,28},{14,30},{16,0},... | collective-permute-start | bytes 24584 | tf_op jit(solution)/shard_map/ppermute | solution.py:162

commit v2 on v1

v2 whole, which is shorter than its diff:
```python
import functools
import math

import jax
import jax.numpy as jnp
from jax import lax
from jax.experimental import pallas as pl
from jax.experimental.pallas import tpu as pltpu
from jax.sharding import PartitionSpec as P

TILE = 128
LANES = 128
UNROLL = 16
epsilon = 1e-06


def attend_kernel(
    most_live,
    lists_hbm,
    counts_hbm,
    factors_ref,
    gains_ref,
    gathered_ref,
    out_ref,
    lists,
    counts,
    columns,
    normed_query,
    normed_key,
    scores,
    weights,
    rows_kept,
    sems,
):
    head_width = out_ref.shape[2]
    tiles = out_ref.shape[0]
    tile_count = gathered_ref.shape[0] // TILE
    together = scores.shape[0]
    scale = math.log2(math.e) / math.sqrt(head_width)
    to_smem = [
        pltpu.make_async_copy(lists_hbm, lists, sems.at[0]),
        pltpu.make_async_copy(counts_hbm, counts, sems.at[1]),
    ]
    for copy in to_smem:
        copy.start()
    for block in range(columns.shape[0]):
        columns[block] = factors_ref[block * LANES : (block + 1) * LANES, :].T

    def rows_of(tile):
        return pl.ds(pl.multiple_of(tile * TILE, TILE), TILE)

    def each(count, step):
        if count <= UNROLL:
            for index in range(count):
                step(index)
        else:

            def body(index, carry):
                step(index)
                return carry

            lax.fori_loop(0, count, body, 0)

    def normalize(tile, place, which):
        lane = lax.broadcasted_iota(jnp.int32, (TILE, LANES), 1)
        column = jnp.sum(
            jnp.where(lane == which % LANES, columns[which // LANES], 0.0), axis=1, keepdims=True
        )
        values = gathered_ref[rows_of(tile), place * head_width : (place + 1) * head_width]
        values = values.astype(jnp.float32) * column * gains_ref[place : place + 1, :]
        return values.astype(jnp.bfloat16)

    def normalize_step(tile):
        normed_query[rows_of(tile), :] = normalize(tile, 0, tile)
        normed_key[rows_of(tile), :] = normalize(tile, 1, tile_count + tile)

    each(tile_count, normalize_step)
    for copy in to_smem:
        copy.wait()
    base = counts[tiles]

    def live_of(step):
        return [lists[step * most_live + slot] for slot in range(most_live)]

    def some_tiles(first):
        for place in range(together):
            step = first + place
            keys = [normed_key[rows_of(live), :] for live in live_of(step)]
            score = lax.dot_general(
                normed_query[rows_of(base + step), :],
                jnp.concatenate(keys, axis=0),
                (((1,), (1,)), ((), ())),
                preferred_element_type=jnp.float32,
            )
            slot = lax.broadcasted_iota(jnp.int32, (1, most_live * TILE), 1) // TILE
            score = jnp.where(slot < counts[step], score, -jnp.inf)
            scores[place] = score
            largest = jnp.max(score, axis=1, keepdims=True)
            rows_kept[place] = jnp.broadcast_to(largest, (TILE, LANES))
        for place in range(together):
            largest = jnp.concatenate([rows_kept[place]] * most_live, axis=1)
            weight = jnp.exp2((scores[place] - largest) * scale)
            weights[place] = weight.astype(jnp.bfloat16)
            denominators = jnp.sum(weight, axis=1, keepdims=True)
            rows_kept[place] = jnp.broadcast_to(denominators, (TILE, LANES))
        for place in range(together):
            step = first + place
            values = [gathered_ref[rows_of(live), 2 * head_width :] for live in live_of(step)]
            total = jnp.dot(
                weights[place],
                jnp.concatenate(values, axis=0),
                preferred_element_type=jnp.float32,
            )
            out_ref[step] = (total / rows_kept[place]).astype(out_ref.dtype)

    if tiles == together:
        some_tiles(0)
    else:

        def several(index, carry):
            some_tiles(index * together)
            return carry

        lax.fori_loop(0, tiles // together, several, 0)


def attend(gathered, factors, gains, lists, counts, base, tiles):
    head_width = gathered.shape[1] // 3
    most_live = lists.shape[1]
    tile_count = gathered.shape[0] // TILE
    blocks = -(-factors.shape[0] // LANES)
    factors = jnp.pad(factors, ((0, blocks * LANES - factors.shape[0]), (0, 0)))
    lists = lists.reshape(-1)
    counts = jnp.concatenate([counts, base.reshape(1)])
    together = max(size for size in range(1, max(1, 64 // most_live) + 1) if tiles % size == 0)
    anywhere = pl.BlockSpec(memory_space=pl.ANY)
    vmem = pl.BlockSpec(memory_space=pltpu.VMEM)
    return pl.pallas_call(
        functools.partial(attend_kernel, most_live),
        out_shape=jax.ShapeDtypeStruct((tiles, TILE, head_width), jnp.bfloat16),
        in_specs=[anywhere] * 2 + [vmem] * 3,
        out_specs=vmem,
        scratch_shapes=[
            pltpu.SMEM(lists.shape, jnp.int32),
            pltpu.SMEM(counts.shape, jnp.int32),
            pltpu.VMEM((blocks, LANES, LANES), jnp.float32),
            pltpu.VMEM((tile_count * TILE, head_width), jnp.bfloat16),
            pltpu.VMEM((tile_count * TILE, head_width), jnp.bfloat16),
            pltpu.VMEM((together, TILE, most_live * TILE), jnp.float32),
            pltpu.VMEM((together, TILE, most_live * TILE), jnp.bfloat16),
            pltpu.VMEM((together, TILE, LANES), jnp.float32),
            pltpu.SemaphoreType.DMA((2,)),
        ],
        compiler_params=pltpu.CompilerParams(vmem_limit_bytes=48 * 1024 * 1024),
        name="attend",
    )(lists, counts, factors, gains, gathered)


def gather_over(values, axis):
    count = lax.axis_size(axis)
    if count & (count - 1):
        return lax.all_gather(values, axis)
    me = lax.axis_index(axis)
    held = values[None]
    block = count
    while block > 1:
        radix = 4 if block % 4 == 0 else 2
        block //= radix
        others = [
            lax.ppermute(held, axis, [(i, i ^ (turn * block)) for i in range(count)])
            for turn in range(1, radix)
        ]
        parts = [held] + others
        mine = (me // block) % radix
        ordered = []
        for place in range(radix):
            part = parts[0]
            for turn in range(1, radix):
                part = jnp.where((mine ^ place) == turn, parts[turn], part)
            ordered.append(part)
        held = jnp.stack(ordered, axis=-1 - values.ndim)
        held = held.reshape((-1,) + values.shape)
    return held


def local(query_proj, key_proj, value_proj, query_gain, key_gain, live_tiles, live_count):
    tokens_here = query_proj.shape[0]
    heads_here = live_tiles.shape[0]
    head_width = query_proj.shape[1] // heads_here
    full_width = query_proj.shape[1] * lax.axis_size("tp")
    device_count = lax.axis_size("seq")
    group_size = device_count // heads_here
    my_index = lax.axis_index("seq")
    my_head = my_index // group_size
    my_member = my_index % group_size

    outgoing = jnp.concatenate(
        [
            field.reshape(tokens_here, heads_here, head_width)
            for field in (query_proj, key_proj, value_proj)
        ],
        axis=2,
    ).transpose(1, 0, 2)
    if group_size > 1:
        outgoing = jnp.repeat(outgoing, group_size, axis=0)
    incoming = lax.all_to_all(outgoing, "seq", split_axis=0, concat_axis=0, tiled=True)
    gathered = incoming.reshape(device_count * tokens_here, 3 * head_width)

    query_values = query_proj.astype(jnp.float32)
    key_values = key_proj.astype(jnp.float32)
    squares = jnp.stack(
        [jnp.sum(query_values * query_values, axis=1), jnp.sum(key_values * key_values, axis=1)]
    )
    squares = lax.psum(squares, "tp")
    factors = gather_over(lax.rsqrt(squares / full_width + epsilon), "seq")
    tile_count = device_count * tokens_here // TILE
    factors = factors.transpose(1, 0, 2).reshape(2 * tile_count, TILE)
    gains = jnp.stack([query_gain, key_gain]).reshape(2, heads_here, head_width)
    gains = lax.dynamic_index_in_dim(gains, my_head, 1, keepdims=False)

    per_member = tile_count // group_size
    base = my_member * per_member
    lists = lax.dynamic_index_in_dim(live_tiles, my_head, 0, keepdims=False)
    counts = lax.dynamic_index_in_dim(live_count, my_head, 0, keepdims=False)
    lists = lax.dynamic_slice_in_dim(lists, base, per_member, 0)
    counts = lax.dynamic_slice_in_dim(counts, base, per_member, 0)
    results = attend(
        gathered, factors, gains, lists, counts, base.astype(jnp.int32), per_member
    )
    if group_size > 1:
        placed = jnp.zeros((tile_count, TILE, head_width), jnp.bfloat16)
        results = lax.dynamic_update_slice_in_dim(placed, results, base, 0)
    results = results.reshape(device_count, tokens_here, head_width)
    returned = lax.all_to_all(results, "seq", split_axis=0, concat_axis=0, tiled=True)
    if group_size > 1:
        returned = returned.reshape(heads_here, group_size, tokens_here, head_width)
        returned = returned.astype(jnp.float32).sum(axis=1).astype(jnp.bfloat16)
    return returned.transpose(1, 0, 2).reshape(tokens_here, heads_here * head_width)


def solution(mesh):
    placed = (
        P("seq", "tp"),
        P("seq", "tp"),
        P("seq", "tp"),
        P("tp"),
        P("tp"),
        P("tp", None, None),
        P("tp", None),
    )
    return jax.shard_map(
        local, mesh=mesh, in_specs=placed, out_specs=P("seq", "tp"), check_vma=False
    )
```

time: 140 us -> 77.3 us (0.55)
  Pallas kernels: 74.6 us -> 2.51 us
  waiting for transfers between devices: 23.2 us -> 32.2 us
  local copies, waits for them, and re-layouts: 0.9 us -> 5.51 us
  blocking collectives: 21.8 us -> 17.7 us
  starting transfers between devices: 18.7 us -> 16.9 us
  other arithmetic: 0.43 us -> 1.92 us
    pallas_call x2 -> x0, Pallas kernels: 66.3 us -> none  [the longest x1 49.2 us: pack(): pl.pallas_call(pack_kernel, out_shape=jax.ShapeDtypeStruct((heads, tokens...]
    ppermute x4 -> x6, waiting for transfers between devices: 23.2 us -> 32.2 us  [gather_over(): lax.ppermute(held, axis, [(i, i ^ turn * block) for i in range(count)])]
    pallas_call x1, Pallas kernels: 8.31 us -> 2.51 us  [attend(): pl.pallas_call(functools.partial(attend_kernel, most_live), out_shape=jax...]
    all_to_all x1, blocking collectives: 19.3 us -> 15.2 us  [local(): lax.all_to_all(results, 'seq', split_axis=0, concat_axis=0, tiled=True)]
    reshape x1 -> x4, local copies, waits for them, and re-layouts: 0.09 us -> 2.7 us  [the longest x2 1.6 us: local(): field.reshape(tokens_here, heads_here, head_width)]
    ppermute x4 -> x6, starting transfers between devices: 10.3 us -> 8.48 us  [gather_over(): lax.ppermute(held, axis, [(i, i ^ turn * block) for i in range(count)])]
  transfers between devices with their start and end apart: 5 -> 7, of which waited for: 4 -> 4; matrix products, arithmetic and copies ran while one was open for 1% -> 3% of each run, Pallas kernels for 0% -> 0%
where the time goes in v2:
time: 77.3 us; the launch traced here: 76.9 us
  waiting for transfers between devices  32.2 us (42%)
  blocking collectives  17.7 us (23%)
  starting transfers between devices  16.9 us (22%)
  local copies, waits for them, and re-layouts  5.51 us (7%)
  Pallas kernels  2.51 us (3%)
  other arithmetic  1.92 us (2%)
    ppermute x6, waiting for transfers between devices, gather_over(): lax.ppermute(held, axis, [(i, i ^ turn * block) for i in range(count)])  32.2 us
    all_to_all x1, blocking collectives, local(): lax.all_to_all(results, 'seq', split_axis=0, concat_axis=0, tiled=True)  15.2 us
    ppermute x6, starting transfers between devices, gather_over(): lax.ppermute(held, axis, [(i, i ^ turn * block) for i in range(count)])  8.48 us
    all_to_all x1, starting transfers between devices, local(): lax.all_to_all(outgoing, 'seq', split_axis=0, concat_axis=0, tiled=True)  8.46 us
    pallas_call x1, Pallas kernels, attend(): pl.pallas_call(functools.partial(attend_kernel, most_live), out_shape=jax...  2.51 us
    psum x1, blocking collectives, local(): squares = lax.psum(squares, 'tp')  2.47 us
    reshape x2, local copies, waits for them, and re-layouts, local(): field.reshape(tokens_here, heads_here, head_width)  1.6 us
  transfers between devices with their start and end apart: 7, of which 4 were waited for; matrix products, arithmetic and copies ran while one was open for 3% of the time, Pallas kernels for 0%

profile of v2, /device:TPU:0, one launch (start us, length us, event | category | flops | bytes accessed | tf_op | source)
XLA Modules:
  0.0 76.9 jit_solution(8590529899180745897)
XLA Ops:
  0.0 0.0 copy-start
  0.0 1.0 %copy-done = bf16[128,2048]{1,0:T(8,128)(2,1)S(1)} copy-done((bf16[128,2048]{1,0:T(8,128)(2,1)S(1)}, bf16[128,2048]{1,0:T(8,128)(2,1)}, u32[]{:S(2)}) %copy-start) | copy-done | bytes 524312
  1.0 0.1 copy_bitcast_fusion
  1.2 1.5 %copy_bitcast_fusion.1 = (bf16[128,16,128]{2,0,1:T(8,128)(2,1)S(1)}, bf16[128,16,128]{2,0,1:T(8,128)(2,1)S(1)}) fusion(bf16[128,2048]{1,0:T(8,128)(2,1)} %param.7, bf16[128,2048]{1,0:T(8,128)(2,1)} %param.8), kind=kLoop, calls=%fused_computation.4 | loop fusion | bytes 2097152 | tf_op jit(solution)/shard_map/reshape | solution.py:199
  2.7 1.4 %maximum_bitcast_fusion = bf16[16,128,384]{2,1,0:T(8,128)(2,1)} fusion(bf16[128,16,128]{2,0,1:T(8,128)(2,1)S(1)} %copy_bitcast_fusion, bf16[128,16,128]{2,0,1:T(8,128)(2,1)S(1)} %get-tuple-element.13, bf16[128,16,128]{2,0,1:T(8,128)(2,1)S(1)} %get-tuple-element.14), kind=kLoop, calls=%fused_computation | loop fusion | flops 4718592 | bytes 3145728 | tf_op jit(solution)/shard_map/transpose | solution.py:203
  4.1 8.5 %all-to-all-start = ((bf16[16,128,384]{2,1,0:T(8,128)(2,1)}), bf16[16,128,384]{2,1,0:T(8,128)(2,1)S(1)}, u32[]{:S(2)}, u32[]{:S(2)}) async-start(bf16[16,128,384]{2,1,0:T(8,128)(2,1)} %maximum_bitcast_fusion), calls=%async_computation | async-start | bytes 3145728 | tf_op jit(solution)/shard_map/all_to_all | solution.py:206
  12.5 0.0 copy-done.1
  12.5 0.2 multiply_reduce_fusion.1
  12.7 0.2 multiply_reduce_fusion
  12.9 2.5 %psum.7 = f32[2,128]{1,0:T(2,128)S(1)} all-reduce(f32[2,128]{1,0:T(2,128)S(1)} %pad_maximum_fusion.1), channel_id=1, replica_groups=mesh['seq'=16,'tp'=2] {'tp'}, use_global_device_ids=true, to_apply=%region_2.3 | all-reduce | flops 256 | bytes 2048 | tf_op jit(solution)/shard_map/psum | solution.py:214
  15.4 1.9 %collective-permute-start.2 = (f32[1,2,128]{2,1,0:T(2,128)S(1)}, f32[1,2,128]{2,1,0:T(2,128)S(1)}, u32[]{:S(2)}, u32[]{:S(2)}) collective-permute-start(f32[1,2,128]{2,1,0:T(2,128)S(1)} %rsqrt_bitcast_fusion), channel_id=1, source_target_pairs={{0,8},{2,10},{4,12},{6,14},{8,0},{10,2},{12,4},{14,6},{16,24},{18,... | collective-permute-start | bytes 3080 | tf_op jit(solution)/shard_map/ppermute | solution.py:170
  17.3 2.4 %collective-permute-start.1 = (f32[1,2,128]{2,1,0:T(2,128)S(1)}, f32[1,2,128]{2,1,0:T(2,128)S(1)}, u32[]{:S(2)}, u32[]{:S(2)}) collective-permute-start(f32[1,2,128]{2,1,0:T(2,128)S(1)} %rsqrt_bitcast_fusion), channel_id=1, source_target_pairs={{0,16},{2,18},{4,20},{6,22},{8,24},{10,26},{12,28},{14,30},{16,0},... | collective-permute-start | bytes 3080 | tf_op jit(solution)/shard_map/ppermute | solution.py:170
  19.7 0.1 collective-permute-start
  19.8 0.7 fusion.2
  20.5 0.7 constant_dynamic-slice_fusion.1
  21.2 16.9 %collective-permute-done.2 = f32[1,2,128]{2,1,0:T(2,128)S(1)} collective-permute-done((f32[1,2,128]{2,1,0:T(2,128)S(1)}, f32[1,2,128]{2,1,0:T(2,128)S(1)}, u32[]{:S(2)}, u32[]{:S(2)}) %collective-permute-start.2) | collective-permute-done | bytes 1056 | tf_op jit(solution)/shard_map/ppermute | solution.py:170
  38.1 11.4 %collective-permute-done.1 = f32[1,2,128]{2,1,0:T(2,128)S(1)} collective-permute-done((f32[1,2,128]{2,1,0:T(2,128)S(1)}, f32[1,2,128]{2,1,0:T(2,128)S(1)}, u32[]{:S(2)}, u32[]{:S(2)}) %collective-permute-start.1) | collective-permute-done | bytes 1056 | tf_op jit(solution)/shard_map/ppermute | solution.py:170
  49.5 0.0 collective-permute-done
  49.5 1.5 %collective-permute-start.5 = (f32[4,2,128]{2,1,0:T(2,128)S(1)}, f32[4,2,128]{2,1,0:T(2,128)S(1)}, u32[]{:S(2)}, u32[]{:S(2)}) collective-permute-start(f32[4,2,128]{2,1,0:T(2,128)S(1)} %maximum_bitcast_fusion.1), channel_id=1, source_target_pairs={{0,2},{2,0},{4,6},{6,4},{8,10},{10,8},{12,14},{14,12},{16,18},{18,... | collective-permute-start | bytes 12296 | tf_op jit(solution)/shard_map/ppermute | solution.py:170
  51.1 2.2 %collective-permute-start.4 = (f32[4,2,128]{2,1,0:T(2,128)S(1)}, f32[4,2,128]{2,1,0:T(2,128)S(1)}, u32[]{:S(2)}, u32[]{:S(2)}) collective-permute-start(f32[4,2,128]{2,1,0:T(2,128)S(1)} %maximum_bitcast_fusion.1), channel_id=1, source_target_pairs={{0,4},{2,6},{4,0},{6,2},{8,12},{10,14},{12,8},{14,10},{16,20},{18,... | collective-permute-start | bytes 12296 | tf_op jit(solution)/shard_map/ppermute | solution.py:170
  53.3 0.4 collective-permute-start.3
  53.6 0.1 pad_add_fusion.counts_hbm
  53.7 0.1 copy.12
  53.8 0.1 reshape.34.lists_hbm
  53.9 0.0 collective-permute-done.5
  53.9 1.0 %collective-permute-done.4 = f32[4,2,128]{2,1,0:T(2,128)S(1)} collective-permute-done((f32[4,2,128]{2,1,0:T(2,128)S(1)}, f32[4,2,128]{2,1,0:T(2,128)S(1)}, u32[]{:S(2)}, u32[]{:S(2)}) %collective-permute-start.4) | collective-permute-done | bytes 4128 | tf_op jit(solution)/shard_map/ppermute | solution.py:170
  54.9 2.9 %collective-permute-done.3 = f32[4,2,128]{2,1,0:T(2,128)S(1)} collective-permute-done((f32[4,2,128]{2,1,0:T(2,128)S(1)}, f32[4,2,128]{2,1,0:T(2,128)S(1)}, u32[]{:S(2)}, u32[]{:S(2)}) %collective-permute-start.3) | collective-permute-done | bytes 4128 | tf_op jit(solution)/shard_map/ppermute | solution.py:170
  57.9 0.0 all-to-all-done
  57.9 2.5 %attend.1 = bf16[16,128,128]{2,1,0:T(8,128)(2,1)S(1)} custom-call(s32[64]{0:T(128)S(1)} %reshape.34.lists_hbm, s32[17]{0:T(128)S(1)} %pad_add_fusion.counts_hbm, f32[128,128]{1,0:T(8,128)S(1)} %pad.4.factors_ref, f32[2,128]{1,0:T(2,128)S(1)} %fusion.1.gains_ref, bf16[2048,384]{1,0:T(8,128)(2,1)S(1)} %bitcast.69), custom_call_target="tpu_custom_call" | custom-call | tf_op jit(solution)/shard_map/attend/pallas_call | solution.py:138
  60.4 15.2 %all_to_all.10 = bf16[16,128,128]{2,1,0:T(8,128)(2,1)S(1)} all-to-all(bf16[16,128,128]{2,1,0:T(8,128)(2,1)S(1)} %attend.1), channel_id=1, replica_groups=mesh['seq'=16,'tp'=2] {'seq'}, dimensions={0} | all-to-all | bytes 1048576 | tf_op jit(solution)/shard_map/all_to_all | solution.py:234
  75.6 0.3 copy.17
  75.9 1.0 %copy.18 = bf16[128,2048]{1,0:T(8,128)(2,1)} copy(bf16[128,2048]{0,1:T(8,128)(2,1)S(1)} %bitcast.71) | data formatting | bytes 1048576 | tf_op jit(solution)/shard_map/reshape | solution.py:238
  (17 shorter events, 0.1 us)
Async XLA Ops:
  0.0 1.0 %copy-start = (bf16[128,2048]{1,0:T(8,128)(2,1)S(1)}, bf16[128,2048]{1,0:T(8,128)(2,1)}, u32[]{:S(2)}) copy-start(bf16[128,2048]{1,0:T(8,128)(2,1)} %param.9) | copy-start | bytes 1572868
  4.1 8.5 %copy-start.1 = (bf16[128,2048]{1,0:T(8,128)(2,1)S(1)}, bf16[128,2048]{1,0:T(8,128)(2,1)}, u32[]{:S(2)}) copy-start(bf16[128,2048]{1,0:T(8,128)(2,1)} %param.7) | copy-start | bytes 1572868
  4.1 8.7 %copy-start.2 = (bf16[128,2048]{1,0:T(8,128)(2,1)S(1)}, bf16[128,2048]{1,0:T(8,128)(2,1)}, u32[]{:S(2)}) copy-start(bf16[128,2048]{1,0:T(8,128)(2,1)} %param.8) | copy-start | bytes 1572868
  4.1 16.4 %copy-start.3 = (f32[2048]{0:T(1024)S(1)}, f32[2048]{0:T(1024)}, u32[]{:S(2)}) copy-start(f32[2048]{0:T(1024)} %param.11) | copy-start | bytes 24580
  4.1 16.4 %copy-start.4 = (f32[2048]{0:T(1024)S(1)}, f32[2048]{0:T(1024)}, u32[]{:S(2)}) copy-start(f32[2048]{0:T(1024)} %param.10) | copy-start | bytes 24580
  4.1 53.8 %all-to-all-start = ((bf16[16,128,384]{2,1,0:T(8,128)(2,1)}), bf16[16,128,384]{2,1,0:T(8,128)(2,1)S(1)}, u32[]{:S(2)}, u32[]{:S(2)}) async-start(bf16[16,128,384]{2,1,0:T(8,128)(2,1)} %maximum_bitcast_fusion), calls=%async_computation | async-start | bytes 3145728 | tf_op jit(solution)/shard_map/all_to_all | solution.py:206
  15.4 22.7 %collective-permute-start.2 = (f32[1,2,128]{2,1,0:T(2,128)S(1)}, f32[1,2,128]{2,1,0:T(2,128)S(1)}, u32[]{:S(2)}, u32[]{:S(2)}) collective-permute-start(f32[1,2,128]{2,1,0:T(2,128)S(1)} %rsqrt_bitcast_fusion), channel_id=1, source_target_pairs={{0,8},{2,10},{4,12},{6,14},{8,0},{10,2},{12,4},{14,6},{16,24},{18,... | collective-permute-start | bytes 3080 | tf_op jit(solution)/shard_map/ppermute | solution.py:170
  17.3 32.2 %collective-permute-start.1 = (f32[1,2,128]{2,1,0:T(2,128)S(1)}, f32[1,2,128]{2,1,0:T(2,128)S(1)}, u32[]{:S(2)}, u32[]{:S(2)}) collective-permute-start(f32[1,2,128]{2,1,0:T(2,128)S(1)} %rsqrt_bitcast_fusion), channel_id=1, source_target_pairs={{0,16},{2,18},{4,20},{6,22},{8,24},{10,26},{12,28},{14,30},{16,0},... | collective-permute-start | bytes 3080 | tf_op jit(solution)/shard_map/ppermute | solution.py:170
  19.7 29.8 %collective-permute-start = (f32[1,2,128]{2,1,0:T(2,128)S(1)}, f32[1,2,128]{2,1,0:T(2,128)S(1)}, u32[]{:S(2)}, u32[]{:S(2)}) collective-permute-start(f32[1,2,128]{2,1,0:T(2,128)S(1)} %rsqrt_bitcast_fusion), channel_id=1, source_target_pairs={{0,24},{2,26},{4,28},{6,30},{8,16},{10,18},{12,20},{14,22},{16,8},... | collective-permute-start | bytes 3080 | tf_op jit(solution)/shard_map/ppermute | solution.py:170
  49.5 4.3 %collective-permute-start.5 = (f32[4,2,128]{2,1,0:T(2,128)S(1)}, f32[4,2,128]{2,1,0:T(2,128)S(1)}, u32[]{:S(2)}, u32[]{:S(2)}) collective-permute-start(f32[4,2,128]{2,1,0:T(2,128)S(1)} %maximum_bitcast_fusion.1), channel_id=1, source_target_pairs={{0,2},{2,0},{4,6},{6,4},{8,10},{10,8},{12,14},{14,12},{16,18},{18,... | collective-permute-start | bytes 12296 | tf_op jit(solution)/shard_map/ppermute | solution.py:170
  51.1 3.8 %collective-permute-start.4 = (f32[4,2,128]{2,1,0:T(2,128)S(1)}, f32[4,2,128]{2,1,0:T(2,128)S(1)}, u32[]{:S(2)}, u32[]{:S(2)}) collective-permute-start(f32[4,2,128]{2,1,0:T(2,128)S(1)} %maximum_bitcast_fusion.1), channel_id=1, source_target_pairs={{0,4},{2,6},{4,0},{6,2},{8,12},{10,14},{12,8},{14,10},{16,20},{18,... | collective-permute-start | bytes 12296 | tf_op jit(solution)/shard_map/ppermute | solution.py:170
  53.3 4.5 %collective-permute-start.3 = (f32[4,2,128]{2,1,0:T(2,128)S(1)}, f32[4,2,128]{2,1,0:T(2,128)S(1)}, u32[]{:S(2)}, u32[]{:S(2)}) collective-permute-start(f32[4,2,128]{2,1,0:T(2,128)S(1)} %maximum_bitcast_fusion.1), channel_id=1, source_target_pairs={{0,6},{2,4},{4,2},{6,0},{8,14},{10,12},{12,10},{14,8},{16,22},{18,... | collective-permute-start | bytes 12296 | tf_op jit(solution)/shard_map/ppermute | solution.py:170

commit v3 on v2

v3 whole, which is shorter than its diff:
```python
import functools
import math

import jax
import jax.numpy as jnp
from jax import lax
from jax.experimental import pallas as pl
from jax.experimental.pallas import tpu as pltpu
from jax.sharding import PartitionSpec as P

TILE = 128
LANES = 128
epsilon = 1e-06


def pack_kernel(query_ref, key_ref, value_ref, factors_ref, gains_ref, packed_ref):
    heads, tokens, triple = packed_ref.shape
    width = triple // 3
    for first in range(0, tokens, LANES):
        rows = slice(first, first + LANES)
        for place, field_ref in enumerate((query_ref, key_ref)):
            factor = jnp.broadcast_to(factors_ref[place : place + 1, rows], (width, LANES)).T
            for head in range(heads):
                columns = slice(head * width, (head + 1) * width)
                values = field_ref[rows, columns].astype(jnp.float32) * factor
                values = values * gains_ref[place : place + 1, columns]
                packed_ref[head, rows, place * width : (place + 1) * width] = values.astype(
                    packed_ref.dtype
                )
    for head in range(heads):
        packed_ref[head, :, 2 * width :] = value_ref[:, head * width : (head + 1) * width]


def pack(query, key, value, factors, gains, heads):
    tokens, columns = query.shape
    vmem = pl.BlockSpec(memory_space=pltpu.VMEM)
    return pl.pallas_call(
        pack_kernel,
        out_shape=jax.ShapeDtypeStruct((heads, tokens, 3 * columns // heads), query.dtype),
        in_specs=[vmem] * 5,
        out_specs=vmem,
        compiler_params=pltpu.CompilerParams(vmem_limit_bytes=16 * 1024 * 1024),
        name="normalize_and_pack",
    )(query, key, value, factors, gains)


def attend_kernel(
    most_live,
    lists_hbm,
    counts_hbm,
    gathered_ref,
    out_ref,
    lists,
    counts,
    scores,
    weights,
    rows_kept,
    sems,
):
    head_width = out_ref.shape[2]
    tiles = out_ref.shape[0]
    together = scores.shape[0]
    scale = math.log2(math.e) / math.sqrt(head_width)
    to_smem = [
        pltpu.make_async_copy(lists_hbm, lists, sems.at[0]),
        pltpu.make_async_copy(counts_hbm, counts, sems.at[1]),
    ]
    for copy in to_smem:
        copy.start()
    for copy in to_smem:
        copy.wait()
    base = counts[tiles]

    def part(tile, place):
        rows = pl.ds(pl.multiple_of(tile * TILE, TILE), TILE)
        return gathered_ref[rows, place * head_width : (place + 1) * head_width]

    def live_parts(step, place):
        live = [lists[step * most_live + slot] for slot in range(most_live)]
        return jnp.concatenate([part(tile, place) for tile in live], axis=0)

    def some_tiles(first):
        for place in range(together):
            step = first + place
            score = lax.dot_general(
                part(base + step, 0),
                live_parts(step, 1),
                (((1,), (1,)), ((), ())),
                preferred_element_type=jnp.float32,
            )
            slot = lax.broadcasted_iota(jnp.int32, (1, most_live * TILE), 1) // TILE
            score = jnp.where(slot < counts[step], score, -jnp.inf)
            scores[place] = score
            largest = jnp.max(score, axis=1, keepdims=True)
            rows_kept[place] = jnp.broadcast_to(largest, (TILE, LANES))
        for place in range(together):
            largest = jnp.concatenate([rows_kept[place]] * most_live, axis=1)
            weight = jnp.exp2((scores[place] - largest) * scale)
            weights[place] = weight.astype(jnp.bfloat16)
            denominators = jnp.sum(weight, axis=1, keepdims=True)
            rows_kept[place] = jnp.broadcast_to(denominators, (TILE, LANES))
        for place in range(together):
            step = first + place
            total = jnp.dot(
                weights[place], live_parts(step, 2), preferred_element_type=jnp.float32
            )
            out_ref[step] = (total / rows_kept[place]).astype(out_ref.dtype)

    if tiles == together:
        some_tiles(0)
    else:

        def several(index, carry):
            some_tiles(index * together)
            return carry

        lax.fori_loop(0, tiles // together, several, 0)


def attend(gathered, lists, counts, base, tiles):
    head_width = gathered.shape[1] // 3
    most_live = lists.shape[1]
    lists = lists.reshape(-1)
    counts = jnp.concatenate([counts, base.reshape(1)])
    together = max(size for size in range(1, max(1, 64 // most_live) + 1) if tiles % size == 0)
    anywhere = pl.BlockSpec(memory_space=pl.ANY)
    vmem = pl.BlockSpec(memory_space=pltpu.VMEM)
    return pl.pallas_call(
        functools.partial(attend_kernel, most_live),
        out_shape=jax.ShapeDtypeStruct((tiles, TILE, head_width), jnp.bfloat16),
        in_specs=[anywhere] * 2 + [vmem],
        out_specs=vmem,
        scratch_shapes=[
            pltpu.SMEM(lists.shape, jnp.int32),
            pltpu.SMEM(counts.shape, jnp.int32),
            pltpu.VMEM((together, TILE, most_live * TILE), jnp.float32),
            pltpu.VMEM((together, TILE, most_live * TILE), jnp.bfloat16),
            pltpu.VMEM((together, TILE, LANES), jnp.float32),
            pltpu.SemaphoreType.DMA((2,)),
        ],
        compiler_params=pltpu.CompilerParams(vmem_limit_bytes=40 * 1024 * 1024),
        name="attend",
    )(lists, counts, gathered)


def local(query_proj, key_proj, value_proj, query_gain, key_gain, live_tiles, live_count):
    tokens_here = query_proj.shape[0]
    heads_here = live_tiles.shape[0]
    head_width = query_proj.shape[1] // heads_here
    full_width = query_proj.shape[1] * lax.axis_size("tp")
    device_count = lax.axis_size("seq")
    group_size = device_count // heads_here
    my_index = lax.axis_index("seq")
    my_head = my_index // group_size
    my_member = my_index % group_size

    query_values = query_proj.astype(jnp.float32)
    key_values = key_proj.astype(jnp.float32)
    squares = jnp.stack(
        [jnp.sum(query_values * query_values, axis=1), jnp.sum(key_values * key_values, axis=1)]
    )
    squares = lax.psum(squares, "tp")
    factors = lax.rsqrt(squares / full_width + epsilon)
    gains = jnp.stack([query_gain, key_gain])
    outgoing = pack(query_proj, key_proj, value_proj, factors, gains, heads_here)
    if group_size > 1:
        outgoing = jnp.repeat(outgoing, group_size, axis=0)
    incoming = lax.all_to_all(outgoing, "seq", split_axis=0, concat_axis=0, tiled=True)
    gathered = incoming.reshape(device_count * tokens_here, 3 * head_width)

    tile_count = device_count * tokens_here // TILE
    per_member = tile_count // group_size
    base = my_member * per_member
    lists = lax.dynamic_index_in_dim(live_tiles, my_head, 0, keepdims=False)
    counts = lax.dynamic_index_in_dim(live_count, my_head, 0, keepdims=False)
    lists = lax.dynamic_slice_in_dim(lists, base, per_member, 0)
    counts = lax.dynamic_slice_in_dim(counts, base, per_member, 0)
    results = attend(gathered, lists, counts, base.astype(jnp.int32), per_member)
    if group_size > 1:
        placed = jnp.zeros((tile_count, TILE, head_width), jnp.bfloat16)
        results = lax.dynamic_update_slice_in_dim(placed, results, base, 0)
    results = results.reshape(device_count, tokens_here, head_width)
    returned = lax.all_to_all(results, "seq", split_axis=0, concat_axis=0, tiled=True)
    if group_size > 1:
        returned = returned.reshape(heads_here, group_size, tokens_here, head_width)
        returned = returned.astype(jnp.float32).sum(axis=1).astype(jnp.bfloat16)
    return returned.transpose(1, 0, 2).reshape(tokens_here, heads_here * head_width)


def solution(mesh):
    placed = (
        P("seq", "tp"),
        P("seq", "tp"),
        P("seq", "tp"),
        P("tp"),
        P("tp"),
        P("tp", None, None),
        P("tp", None),
    )
    return jax.shard_map(
        local, mesh=mesh, in_specs=placed, out_specs=P("seq", "tp"), check_vma=False
    )
```

time: 77.3 us -> 79.3 us (1.026)
  starting transfers between devices: 16.9 us -> 8.2 us
  blocking collectives: 17.7 us -> 24.7 us
  Pallas kernels: 2.51 us -> 3.95 us
  other arithmetic: 1.92 us -> 3.3 us
  waiting for transfers between devices: 32.2 us -> 33.3 us
    all_to_all x1, waiting for transfers between devices: 0.01 us -> 33.3 us  [local(): lax.all_to_all(outgoing, 'seq', split_axis=0, concat_axis=0, tiled=True)]
    ppermute x6 -> x0, waiting for transfers between devices: 32.2 us -> none  [gather_over(): lax.ppermute(held, axis, [(i, i ^ turn * block) for i in range(count)])]
    ppermute x6 -> x0, starting transfers between devices: 8.48 us -> none  [gather_over(): lax.ppermute(held, axis, [(i, i ^ turn * block) for i in range(count)])]
    all_to_all x1, blocking collectives: 15.2 us -> 22.1 us  [local(): lax.all_to_all(results, 'seq', split_axis=0, concat_axis=0, tiled=True)]
    unnamed x10 -> x8, local copies, waits for them, and re-layouts: 1.06 us -> 3.12 us
    pallas_call x0 -> x1, Pallas kernels: none -> 1.62 us  [pack(): pl.pallas_call(pack_kernel, out_shape=jax.ShapeDtypeStruct((heads, tokens...]
    reshape x2 -> x0, local copies, waits for them, and re-layouts: 1.6 us -> none  [local(): field.reshape(tokens_here, heads_here, head_width)]
    transpose x1 -> x0, other arithmetic: 1.4 us -> none  [local(): outgoing = jnp.concatenate([field.reshape(tokens_here, heads_here, head_w...]
  transfers between devices with their start and end apart: 7 -> 1, of which waited for: 4 -> 1; matrix products, arithmetic and copies ran while one was open for 3% -> 1% of each run, Pallas kernels for 0% -> 0%
where the time goes in v3:
time: 79.3 us; the launch traced here: 78.8 us
  waiting for transfers between devices  33.3 us (42%)
  blocking collectives  24.7 us (31%)
  starting transfers between devices  8.2 us (10%)
  local copies, waits for them, and re-layouts  5.29 us (7%)
  Pallas kernels  3.95 us (5%)
  other arithmetic  3.3 us (4%)
    all_to_all x1, waiting for transfers between devices, local(): lax.all_to_all(outgoing, 'seq', split_axis=0, concat_axis=0, tiled=True)  33.3 us
    all_to_all x1, blocking collectives, local(): lax.all_to_all(results, 'seq', split_axis=0, concat_axis=0, tiled=True)  22.1 us
    all_to_all x1, starting transfers between devices, local(): lax.all_to_all(outgoing, 'seq', split_axis=0, concat_axis=0, tiled=True)  8.2 us
    unnamed x8, local copies, waits for them, and re-layouts  3.12 us
    psum x1, blocking collectives, local(): squares = lax.psum(squares, 'tp')  2.58 us
    pallas_call x1, Pallas kernels, attend(): pl.pallas_call(functools.partial(attend_kernel, most_live), out_shape=jax...  2.33 us
    pallas_call x1, Pallas kernels, pack(): pl.pallas_call(pack_kernel, out_shape=jax.ShapeDtypeStruct((heads, tokens...  1.62 us
  transfers between devices with their start and end apart: 1, of which 1 were waited for; matrix products, arithmetic and copies ran while one was open for 1% of the time, Pallas kernels for 0%

profile of v3, /device:TPU:0, one launch (start us, length us, event | category | flops | bytes accessed | tf_op | source)
XLA Modules:
  0.0 78.8 jit_solution(5375998137078615274)
XLA Ops:
  0.0 0.0 copy-start
  0.0 1.2 %multiply_reduce_fusion.1 = f32[128]{0:T(128)S(1)} fusion(bf16[128,2048]{1,0:T(8,128)(2,1)} %query_ref.1), kind=kLoop, calls=%fused_computation.1 | loop fusion | flops 786304 | bytes 524800 | tf_op jit(solution)/shard_map/reduce_sum | solution.py:160
  1.2 1.2 %multiply_reduce_fusion = f32[128]{0:T(128)S(1)} fusion(bf16[128,2048]{1,0:T(8,128)(2,1)} %key_ref.1), kind=kLoop, calls=%fused_computation | loop fusion | flops 786304 | bytes 524800 | tf_op jit(solution)/shard_map/reduce_sum | solution.py:160
  2.5 2.6 %psum.7 = f32[2,128]{1,0:T(2,128)S(1)} all-reduce(f32[2,128]{1,0:T(2,128)S(1)} %pad_maximum_fusion.1), channel_id=1, replica_groups=mesh['seq'=16,'tp'=2] {'tp'}, use_global_device_ids=true, to_apply=%region_2.3 | all-reduce | flops 256 | bytes 2048 | tf_op jit(solution)/shard_map/psum | solution.py:162
  5.1 0.7 pad_maximum_fusion.gains_ref
  5.8 0.0 copy-start.1
  5.8 1.0 %copy-done.1 = bf16[128,2048]{1,0:T(8,128)(2,1)S(1)} copy-done((bf16[128,2048]{1,0:T(8,128)(2,1)S(1)}, bf16[128,2048]{1,0:T(8,128)(2,1)}, u32[]{:S(2)}) %copy-start.1) | copy-done | bytes 524312
  6.9 0.0 copy-start.2
  6.9 1.0 %copy-done.2 = bf16[128,2048]{1,0:T(8,128)(2,1)S(1)} copy-done((bf16[128,2048]{1,0:T(8,128)(2,1)S(1)}, bf16[128,2048]{1,0:T(8,128)(2,1)}, u32[]{:S(2)}) %copy-start.2) | copy-done | bytes 524312
  7.9 0.0 copy-start.3
  7.9 1.0 %copy-done.3 = bf16[128,2048]{1,0:T(8,128)(2,1)S(1)} copy-done((bf16[128,2048]{1,0:T(8,128)(2,1)S(1)}, bf16[128,2048]{1,0:T(8,128)(2,1)}, u32[]{:S(2)}) %copy-start.3) | copy-done | bytes 524312
  8.9 1.6 %normalize_and_pack.1 = bf16[16,128,384]{2,1,0:T(8,128)(2,1)} custom-call(bf16[128,2048]{1,0:T(8,128)(2,1)S(1)} %copy-done.1, bf16[128,2048]{1,0:T(8,128)(2,1)S(1)} %copy-done.2, bf16[128,2048]{1,0:T(8,128)(2,1)S(1)} %copy-done.3, f32[2,128]{1,0:T(2,128)S(1)} %add_rsqrt_fusion.factors_ref, f32[2,2048]{1,0:T(2,128)S(1)} %pad_maximum_fusion.gains_ref), custom_call_target="tpu_custom_call" | custom-call | tf_op jit(solution)/shard_map/normalize_and_pack/pallas_call | solution.py:37
  10.6 8.2 %all-to-all-start = ((bf16[16,128,384]{2,1,0:T(8,128)(2,1)}), bf16[16,128,384]{2,1,0:T(8,128)(2,1)S(1)}, u32[]{:S(2)}, u32[]{:S(2)}) async-start(bf16[16,128,384]{2,1,0:T(8,128)(2,1)} %normalize_and_pack.1), calls=%async_computation | async-start | bytes 3145728 | tf_op jit(solution)/shard_map/all_to_all | solution.py:168
  18.8 0.0 copy-done
  18.8 0.1 copy.9
  18.9 0.1 reshape.11.lists_hbm
  19.0 0.7 dynamic-slice_bitcast_fusion
  19.7 0.1 pad_add_fusion.counts_hbm
  19.7 33.3 %all-to-all-done = bf16[16,128,384]{2,1,0:T(8,128)(2,1)S(1)} async-done(((bf16[16,128,384]{2,1,0:T(8,128)(2,1)}), bf16[16,128,384]{2,1,0:T(8,128)(2,1)S(1)}, u32[]{:S(2)}, u32[]{:S(2)}) %all-to-all-start) | async-done | bytes 1572896 | tf_op jit(solution)/shard_map/all_to_all | solution.py:168
  53.0 2.3 %attend.1 = bf16[16,128,128]{2,1,0:T(8,128)(2,1)S(1)} custom-call(s32[64]{0:T(128)S(1)} %reshape.11.lists_hbm, s32[17]{0:T(128)S(1)} %pad_add_fusion.counts_hbm, bf16[2048,384]{1,0:T(8,128)(2,1)S(1)} %bitcast.9), custom_call_target="tpu_custom_call" | custom-call | tf_op jit(solution)/shard_map/attend/pallas_call | solution.py:128
  55.4 22.1 %all_to_all.10 = bf16[16,128,128]{2,1,0:T(8,128)(2,1)S(1)} all-to-all(bf16[16,128,128]{2,1,0:T(8,128)(2,1)S(1)} %attend.1), channel_id=1, replica_groups=mesh['seq'=16,'tp'=2] {'seq'}, dimensions={0} | all-to-all | bytes 1048576 | tf_op jit(solution)/shard_map/all_to_all | solution.py:183
  77.5 0.3 copy.10
  77.8 1.0 %copy.11 = bf16[128,2048]{1,0:T(8,128)(2,1)} copy(bf16[128,2048]{0,1:T(8,128)(2,1)S(1)} %bitcast.11) | data formatting | bytes 1048576 | tf_op jit(solution)/shard_map/reshape | solution.py:187
  (3 shorter events, 0.0 us)
Async XLA Ops:
  0.0 18.8 %copy-start = (s32[16,16,4]{1,2,0:T(4,128)S(1)}, s32[16,16,4]{1,2,0:T(4,128)}, u32[]{:S(2)}) copy-start(s32[16,16,4]{1,2,0:T(4,128)} %param.12) | copy-start | bytes 12292
  5.8 1.0 %copy-start.1 = (bf16[128,2048]{1,0:T(8,128)(2,1)S(1)}, bf16[128,2048]{1,0:T(8,128)(2,1)}, u32[]{:S(2)}) copy-start(bf16[128,2048]{1,0:T(8,128)(2,1)} %query_ref.1) | copy-start | bytes 1572868
  6.9 1.0 %copy-start.2 = (bf16[128,2048]{1,0:T(8,128)(2,1)S(1)}, bf16[128,2048]{1,0:T(8,128)(2,1)}, u32[]{:S(2)}) copy-start(bf16[128,2048]{1,0:T(8,128)(2,1)} %key_ref.1) | copy-start | bytes 1572868
  7.9 1.0 %copy-start.3 = (bf16[128,2048]{1,0:T(8,128)(2,1)S(1)}, bf16[128,2048]{1,0:T(8,128)(2,1)}, u32[]{:S(2)}) copy-start(bf16[128,2048]{1,0:T(8,128)(2,1)} %value_ref.1) | copy-start | bytes 1572868
  10.6 42.5 %all-to-all-start = ((bf16[16,128,384]{2,1,0:T(8,128)(2,1)}), bf16[16,128,384]{2,1,0:T(8,128)(2,1)S(1)}, u32[]{:S(2)}, u32[]{:S(2)}) async-start(bf16[16,128,384]{2,1,0:T(8,128)(2,1)} %normalize_and_pack.1), calls=%async_computation | async-start | bytes 3145728 | tf_op jit(solution)/shard_map/all_to_all | solution.py:168

commit v4 on v2

--- a/solution.py
+++ b/solution.py
@@ -12,6 +12,38 @@
 LANES = 128
 UNROLL = 16
 epsilon = 1e-06
+
+
+def pack_kernel(query_hbm, key_hbm, value_hbm, packed_ref, query, key, value, sems):
+    heads, _, triple = packed_ref.shape
+    width = triple // 3
+    held = (query, key, value)
+    copies = [
+        pltpu.make_async_copy(source, target, sems.at[place])
+        for place, (source, target) in enumerate(zip((query_hbm, key_hbm, value_hbm), held))
+    ]
+    for copy in copies:
+        copy.start()
+    for place, field in enumerate(held):
+        copies[place].wait()
+        for head in range(heads):
+            packed_ref[head, :, place * width : (place + 1) * width] = field[
+                :, head * width : (head + 1) * width
+            ]
+
+
+def pack(query, key, value, heads):
+    tokens, columns = query.shape
+    return pl.pallas_call(
+        pack_kernel,
+        out_shape=jax.ShapeDtypeStruct((heads, tokens, 3 * columns // heads), query.dtype),
+        in_specs=[pl.BlockSpec(memory_space=pl.ANY)] * 3,
+        out_specs=pl.BlockSpec(memory_space=pltpu.VMEM),
+        scratch_shapes=[pltpu.VMEM((tokens, columns), query.dtype)] * 3
+        + [pltpu.SemaphoreType.DMA((3,))],
+        compiler_params=pltpu.CompilerParams(vmem_limit_bytes=56 * 1024 * 1024),
+        name="pack_heads",
+    )(query, key, value)
 
 
 def attend_kernel(
@@ -162,24 +194,14 @@
         return lax.all_gather(values, axis)
     me = lax.axis_index(axis)
     held = values[None]
-    block = count
-    while block > 1:
-        radix = 4 if block % 4 == 0 else 2
-        block //= radix
-        others = [
-            lax.ppermute(held, axis, [(i, i ^ (turn * block)) for i in range(count)])
-            for turn in range(1, radix)
-        ]
-        parts = [held] + others
-        mine = (me // block) % radix
-        ordered = []
-        for place in range(radix):
-            part = parts[0]
-            for turn in range(1, radix):
-                part = jnp.where((mine ^ place) == turn, parts[turn], part)
-            ordered.append(part)
-        held = jnp.stack(ordered, axis=-1 - values.ndim)
-        held = held.reshape((-1,) + values.shape)
+    reach = 1
+    while reach < count:
+        other = lax.ppermute(held, axis, [(i, i ^ reach) for i in range(count)])
+        upper = (me & reach) != 0
+        held = jnp.where(
+            upper, jnp.concatenate([other, held], 0), jnp.concatenate([held, other], 0)
+        )
+        reach *= 2
     return held
 
 
@@ -194,13 +216,7 @@
     my_head = my_index // group_size
     my_member = my_index % group_size
 
-    outgoing = jnp.concatenate(
-        [
-            field.reshape(tokens_here, heads_here, head_width)
-            for field in (query_proj, key_proj, value_proj)
-        ],
-        axis=2,
-    ).transpose(1, 0, 2)
+    outgoing = pack(query_proj, key_proj, value_proj, heads_here)
     if group_size > 1:
         outgoing = jnp.repeat(outgoing, group_size, axis=0)
     incoming = lax.all_to_all(outgoing, "seq", split_axis=0, concat_axis=0, tiled=True)

time: 77.3 us -> 71.8 us (0.929)
  waiting for transfers between devices: 32.2 us -> 23.1 us
  blocking collectives: 17.7 us -> 21.7 us
  local copies, waits for them, and re-layouts: 5.51 us -> 2.19 us
  Pallas kernels: 2.51 us -> 5.16 us
  starting transfers between devices: 16.9 us -> 18.7 us
  other arithmetic: 1.92 us -> 0.5 us
    ppermute x6 -> x4, waiting for transfers between devices: 32.2 us -> 23.1 us  [gather_over(): other = lax.ppermute(held, axis, [(i, i ^ reach) for i in range(count)])]
    all_to_all x1, blocking collectives: 15.2 us -> 19.2 us  [local(): lax.all_to_all(results, 'seq', split_axis=0, concat_axis=0, tiled=True)]
    pallas_call x0 -> x1, Pallas kernels: none -> 2.65 us  [pack(): pl.pallas_call(pack_kernel, out_shape=jax.ShapeDtypeStruct((heads, tokens...]
    ppermute x6 -> x4, starting transfers between devices: 8.48 us -> 10.3 us  [gather_over(): other = lax.ppermute(held, axis, [(i, i ^ reach) for i in range(count)])]
    reshape x2 -> x0, local copies, waits for them, and re-layouts: 1.6 us -> none  [local(): field.reshape(tokens_here, heads_here, head_width)]
    transpose x1, other arithmetic: 1.4 us -> 0.01 us  [local(): factors = factors.transpose(1, 0, 2).reshape(2 * tile_count, TILE)]
    unnamed x10, local copies, waits for them, and re-layouts: 1.06 us -> 0.03 us
  transfers between devices with their start and end apart: 7 -> 5, of which waited for: 4 -> 4; matrix products, arithmetic and copies ran while one was open for 3% -> 2% of each run, Pallas kernels for 0% -> 0%
where the time goes in v4:
time: 71.8 us; the launch traced here: 71.5 us
  waiting for transfers between devices  23.1 us (32%)
  blocking collectives  21.7 us (30%)
  starting transfers between devices  18.7 us (26%)
  Pallas kernels  5.16 us (7%)
  local copies, waits for them, and re-layouts  2.19 us (3%)
    ppermute x4, waiting for transfers between devices, gather_over(): other = lax.ppermute(held, axis, [(i, i ^ reach) for i in range(count)])  23.1 us
    all_to_all x1, blocking collectives, local(): lax.all_to_all(results, 'seq', split_axis=0, concat_axis=0, tiled=True)  19.2 us
    ppermute x4, starting transfers between devices, gather_over(): other = lax.ppermute(held, axis, [(i, i ^ reach) for i in range(count)])  10.3 us
    all_to_all x1, starting transfers between devices, local(): lax.all_to_all(outgoing, 'seq', split_axis=0, concat_axis=0, tiled=True)  8.46 us
    pallas_call x1, Pallas kernels, pack(): pl.pallas_call(pack_kernel, out_shape=jax.ShapeDtypeStruct((heads, tokens...  2.65 us
    pallas_call x1, Pallas kernels, attend(): pl.pallas_call(functools.partial(attend_kernel, most_live), out_shape=jax...  2.51 us
    psum x1, blocking collectives, local(): squares = lax.psum(squares, 'tp')  2.47 us
  transfers between devices with their start and end apart: 5, of which 4 were waited for; matrix products, arithmetic and copies ran while one was open for 2% of the time, Pallas kernels for 0%

profile of v4, /device:TPU:0, one launch (start us, length us, event | category | flops | bytes accessed | tf_op | source)
XLA Modules:
  0.0 71.5 jit_solution(11373744838282556136)
XLA Ops:
  0.0 0.0 copy-start
  0.0 2.7 %pack_heads.1 = bf16[16,128,384]{2,1,0:T(8,128)(2,1)} custom-call(bf16[128,2048]{1,0:T(8,128)(2,1)} %query_hbm.1, bf16[128,2048]{1,0:T(8,128)(2,1)} %key_hbm.1, bf16[128,2048]{1,0:T(8,128)(2,1)} %value_hbm.1), custom_call_target="tpu_custom_call" | custom-call | tf_op jit(solution)/shard_map/pack_heads/pallas_call | solution.py:37
  2.7 0.0 copy-start.1
  2.7 0.0 copy-start.2
  2.7 0.0 copy-start.3
  2.7 0.0 copy-start.4
  2.7 8.5 %all-to-all-start = ((bf16[16,128,384]{2,1,0:T(8,128)(2,1)}), bf16[16,128,384]{2,1,0:T(8,128)(2,1)S(1)}, u32[]{:S(2)}, u32[]{:S(2)}) async-start(bf16[16,128,384]{2,1,0:T(8,128)(2,1)} %pack_heads.1), calls=%async_computation | async-start | bytes 3145728 | tf_op jit(solution)/shard_map/all_to_all | solution.py:222
  11.2 0.0 copy-done.1
  11.2 0.2 multiply_reduce_fusion.1
  11.4 0.0 copy-done.2
  11.4 0.2 multiply_reduce_fusion
  11.6 2.5 %psum.7 = f32[2,128]{1,0:T(2,128)S(1)} all-reduce(f32[2,128]{1,0:T(2,128)S(1)} %pad_maximum_fusion), channel_id=1, replica_groups=mesh['seq'=16,'tp'=2] {'tp'}, use_global_device_ids=true, to_apply=%region_2.3 | all-reduce | flops 256 | bytes 2048 | tf_op jit(solution)/shard_map/psum | solution.py:230
  14.1 1.9 %collective-permute-start = (f32[1,2,128]{2,1,0:T(2,128)S(1)}, f32[1,2,128]{2,1,0:T(2,128)S(1)}, u32[]{:S(2)}, u32[]{:S(2)}) collective-permute-start(f32[1,2,128]{2,1,0:T(2,128)S(1)} %rsqrt_bitcast_fusion), channel_id=1, source_target_pairs={{0,2},{2,0},{4,6},{6,4},{8,10},{10,8},{12,14},{14,12},{16,18},{18,... | collective-permute-start | bytes 3080 | tf_op jit(solution)/shard_map/ppermute | solution.py:199
  16.0 0.0 copy-done
  16.0 1.7 %collective-permute-done = f32[1,2,128]{2,1,0:T(2,128)S(1)} collective-permute-done((f32[1,2,128]{2,1,0:T(2,128)S(1)}, f32[1,2,128]{2,1,0:T(2,128)S(1)}, u32[]{:S(2)}, u32[]{:S(2)}) %collective-permute-start) | collective-permute-done | bytes 1056 | tf_op jit(solution)/shard_map/ppermute | solution.py:199
  17.7 1.9 %collective-permute-start.1 = (f32[2,2,128]{2,1,0:T(2,128)S(1)}, f32[2,2,128]{2,1,0:T(2,128)S(1)}, u32[]{:S(2)}, u32[]{:S(2)}) collective-permute-start(f32[2,2,128]{2,1,0:T(2,128)S(1)} %maximum_select_fusion.3), channel_id=1, source_target_pairs={{0,4},{2,6},{4,0},{6,2},{8,12},{10,14},{12,8},{14,10},{16,20},{18,... | collective-permute-start | bytes 6152 | tf_op jit(solution)/shard_map/ppermute | solution.py:199
  19.6 0.0 copy-done.3
  19.6 0.0 copy-done.4
  19.6 1.7 %collective-permute-done.1 = f32[2,2,128]{2,1,0:T(2,128)S(1)} collective-permute-done((f32[2,2,128]{2,1,0:T(2,128)S(1)}, f32[2,2,128]{2,1,0:T(2,128)S(1)}, u32[]{:S(2)}, u32[]{:S(2)}) %collective-permute-start.1) | collective-permute-done | bytes 2080 | tf_op jit(solution)/shard_map/ppermute | solution.py:199
  21.3 1.9 %collective-permute-start.2 = (f32[4,2,128]{2,1,0:T(2,128)S(1)}, f32[4,2,128]{2,1,0:T(2,128)S(1)}, u32[]{:S(2)}, u32[]{:S(2)}) collective-permute-start(f32[4,2,128]{2,1,0:T(2,128)S(1)} %maximum_select_fusion.2), channel_id=1, source_target_pairs={{0,8},{2,10},{4,12},{6,14},{8,0},{10,2},{12,4},{14,6},{16,24},{18,... | collective-permute-start | bytes 12296 | tf_op jit(solution)/shard_map/ppermute | solution.py:199
  23.2 0.7 fusion.3
  23.9 12.9 %collective-permute-done.2 = f32[4,2,128]{2,1,0:T(2,128)S(1)} collective-permute-done((f32[4,2,128]{2,1,0:T(2,128)S(1)}, f32[4,2,128]{2,1,0:T(2,128)S(1)}, u32[]{:S(2)}, u32[]{:S(2)}) %collective-permute-start.2) | collective-permute-done | bytes 4128 | tf_op jit(solution)/shard_map/ppermute | solution.py:199
  36.8 4.6 %collective-permute-start.3 = (f32[8,2,128]{2,1,0:T(2,128)S(1)}, f32[8,2,128]{2,1,0:T(2,128)S(1)}, u32[]{:S(2)}, u32[]{:S(2)}) collective-permute-start(f32[8,2,128]{2,1,0:T(2,128)S(1)} %maximum_select_fusion.1), channel_id=1, source_target_pairs={{0,16},{2,18},{4,20},{6,22},{8,24},{10,26},{12,28},{14,30},{16,0},... | collective-permute-start | bytes 24584 | tf_op jit(solution)/shard_map/ppermute | solution.py:199
  41.4 0.1 pad_add_fusion.counts_hbm
  41.4 0.1 copy.10
  41.5 0.1 reshape.19.lists_hbm
  41.6 6.8 %collective-permute-done.3 = f32[8,2,128]{2,1,0:T(2,128)S(1)} collective-permute-done((f32[8,2,128]{2,1,0:T(2,128)S(1)}, f32[8,2,128]{2,1,0:T(2,128)S(1)}, u32[]{:S(2)}, u32[]{:S(2)}) %collective-permute-start.3) | collective-permute-done | bytes 8224 | tf_op jit(solution)/shard_map/ppermute | solution.py:199
  48.5 0.0 all-to-all-done
  48.5 2.5 %attend.1 = bf16[16,128,128]{2,1,0:T(8,128)(2,1)S(1)} custom-call(s32[64]{0:T(128)S(1)} %reshape.19.lists_hbm, s32[17]{0:T(128)S(1)} %pad_add_fusion.counts_hbm, f32[128,128]{1,0:T(8,128)S(1)} %pad.4.factors_ref, f32[2,128]{1,0:T(2,128)S(1)} %fusion.2.gains_ref, bf16[2048,384]{1,0:T(8,128)(2,1)S(1)} %bitcast.16), custom_call_target="tpu_custom_call" | custom-call | tf_op jit(solution)/shard_map/attend/pallas_call | solution.py:170
  51.0 19.2 %all_to_all.10 = bf16[16,128,128]{2,1,0:T(8,128)(2,1)S(1)} all-to-all(bf16[16,128,128]{2,1,0:T(8,128)(2,1)S(1)} %attend.1), channel_id=1, replica_groups=mesh['seq'=16,'tp'=2] {'seq'}, dimensions={0} | all-to-all | bytes 1048576 | tf_op jit(solution)/shard_map/all_to_all | solution.py:250
  70.2 0.3 copy.12
  70.5 1.0 %copy.13 = bf16[128,2048]{1,0:T(8,128)(2,1)} copy(bf16[128,2048]{0,1:T(8,128)(2,1)S(1)} %bitcast.18) | data formatting | bytes 1048576 | tf_op jit(solution)/shard_map/reshape | solution.py:254
  (10 shorter events, 0.1 us)
Async XLA Ops:
  0.0 16.0 %copy-start = (s32[16,16,4]{1,2,0:T(4,128)S(1)}, s32[16,16,4]{1,2,0:T(4,128)}, u32[]{:S(2)}) copy-start(s32[16,16,4]{1,2,0:T(4,128)} %param.12) | copy-start | bytes 12292
  2.7 8.5 %copy-start.1 = (bf16[128,2048]{1,0:T(8,128)(2,1)S(1)}, bf16[128,2048]{1,0:T(8,128)(2,1)}, u32[]{:S(2)}) copy-start(bf16[128,2048]{1,0:T(8,128)(2,1)} %query_hbm.1) | copy-start | bytes 1572868
  2.7 8.7 %copy-start.2 = (bf16[128,2048]{1,0:T(8,128)(2,1)S(1)}, bf16[128,2048]{1,0:T(8,128)(2,1)}, u32[]{:S(2)}) copy-start(bf16[128,2048]{1,0:T(8,128)(2,1)} %key_hbm.1) | copy-start | bytes 1572868
  2.7 16.9 %copy-start.3 = (f32[2048]{0:T(1024)S(1)}, f32[2048]{0:T(1024)}, u32[]{:S(2)}) copy-start(f32[2048]{0:T(1024)} %param.11) | copy-start | bytes 24580
  2.7 16.9 %copy-start.4 = (f32[2048]{0:T(1024)S(1)}, f32[2048]{0:T(1024)}, u32[]{:S(2)}) copy-start(f32[2048]{0:T(1024)} %param.10) | copy-start | bytes 24580
  2.7 45.8 %all-to-all-start = ((bf16[16,128,384]{2,1,0:T(8,128)(2,1)}), bf16[16,128,384]{2,1,0:T(8,128)(2,1)S(1)}, u32[]{:S(2)}, u32[]{:S(2)}) async-start(bf16[16,128,384]{2,1,0:T(8,128)(2,1)} %pack_heads.1), calls=%async_computation | async-start | bytes 3145728 | tf_op jit(solution)/shard_map/all_to_all | solution.py:222
  14.1 3.6 %collective-permute-start = (f32[1,2,128]{2,1,0:T(2,128)S(1)}, f32[1,2,128]{2,1,0:T(2,128)S(1)}, u32[]{:S(2)}, u32[]{:S(2)}) collective-permute-start(f32[1,2,128]{2,1,0:T(2,128)S(1)} %rsqrt_bitcast_fusion), channel_id=1, source_target_pairs={{0,2},{2,0},{4,6},{6,4},{8,10},{10,8},{12,14},{14,12},{16,18},{18,... | collective-permute-start | bytes 3080 | tf_op jit(solution)/shard_map/ppermute | solution.py:199
  17.7 3.6 %collective-permute-start.1 = (f32[2,2,128]{2,1,0:T(2,128)S(1)}, f32[2,2,128]{2,1,0:T(2,128)S(1)}, u32[]{:S(2)}, u32[]{:S(2)}) collective-permute-start(f32[2,2,128]{2,1,0:T(2,128)S(1)} %maximum_select_fusion.3), channel_id=1, source_target_pairs={{0,4},{2,6},{4,0},{6,2},{8,12},{10,14},{12,8},{14,10},{16,20},{18,... | collective-permute-start | bytes 6152 | tf_op jit(solution)/shard_map/ppermute | solution.py:199
  21.3 15.5 %collective-permute-start.2 = (f32[4,2,128]{2,1,0:T(2,128)S(1)}, f32[4,2,128]{2,1,0:T(2,128)S(1)}, u32[]{:S(2)}, u32[]{:S(2)}) collective-permute-start(f32[4,2,128]{2,1,0:T(2,128)S(1)} %maximum_select_fusion.2), channel_id=1, source_target_pairs={{0,8},{2,10},{4,12},{6,14},{8,0},{10,2},{12,4},{14,6},{16,24},{18,... | collective-permute-start | bytes 12296 | tf_op jit(solution)/shard_map/ppermute | solution.py:199
  36.8 11.6 %collective-permute-start.3 = (f32[8,2,128]{2,1,0:T(2,128)S(1)}, f32[8,2,128]{2,1,0:T(2,128)S(1)}, u32[]{:S(2)}, u32[]{:S(2)}) collective-permute-start(f32[8,2,128]{2,1,0:T(2,128)S(1)} %maximum_select_fusion.1), channel_id=1, source_target_pairs={{0,16},{2,18},{4,20},{6,22},{8,24},{10,26},{12,28},{14,30},{16,0},... | collective-permute-start | bytes 24584 | tf_op jit(solution)/shard_map/ppermute | solution.py:199

commit v5 on v4

--- a/solution.py
+++ b/solution.py
@@ -11,36 +11,55 @@
 TILE = 128
 LANES = 128
 UNROLL = 16
+APART = 4
 epsilon = 1e-06
 
 
-def pack_kernel(query_hbm, key_hbm, value_hbm, packed_ref, query, key, value, sems):
-    heads, _, triple = packed_ref.shape
-    width = triple // 3
-    held = (query, key, value)
-    copies = [
-        pltpu.make_async_copy(source, target, sems.at[place])
-        for place, (source, target) in enumerate(zip((query_hbm, key_hbm, value_hbm), held))
+def pack_kernel(
+    query_hbm, key_hbm, value_hbm, packed_hbm, query, key, value, packed, fetched, written
+):
+    heads, _, _, width = packed.shape
+    pieces = written.shape[1]
+    fields = ((query_hbm, query), (key_hbm, key), (value_hbm, value))
+    fetches = [
+        pltpu.make_async_copy(source, target, fetched.at[place])
+        for place, (source, target) in enumerate(fields)
     ]
-    for copy in copies:
-        copy.start()
-    for place, field in enumerate(held):
-        copies[place].wait()
-        for head in range(heads):
-            packed_ref[head, :, place * width : (place + 1) * width] = field[
-                :, head * width : (head + 1) * width
-            ]
+    for fetch in fetches:
+        fetch.start()
+    writes = []
+    for place, (_, field) in enumerate(fields):
+        fetches[place].wait()
+        for piece in range(pieces):
+            some = range(piece * heads // pieces, (piece + 1) * heads // pieces)
+            for head in some:
+                packed[head, place] = field[:, head * width : (head + 1) * width]
+            span = pl.ds(some[0], len(some))
+            writes.append(
+                pltpu.make_async_copy(
+                    packed.at[span, place], packed_hbm.at[span, place], written.at[place, piece]
+                )
+            )
+            writes[-1].start()
+    for write in writes:
+        write.wait()
 
 
 def pack(query, key, value, heads):
     tokens, columns = query.shape
+    shape = (heads, 3, tokens, columns // heads)
+    anywhere = pl.BlockSpec(memory_space=pl.ANY)
     return pl.pallas_call(
         pack_kernel,
-        out_shape=jax.ShapeDtypeStruct((heads, tokens, 3 * columns // heads), query.dtype),
-        in_specs=[pl.BlockSpec(memory_space=pl.ANY)] * 3,
-        out_specs=pl.BlockSpec(memory_space=pltpu.VMEM),
+        out_shape=jax.ShapeDtypeStruct(shape, query.dtype),
+        in_specs=[anywhere] * 3,
+        out_specs=anywhere,
         scratch_shapes=[pltpu.VMEM((tokens, columns), query.dtype)] * 3
-        + [pltpu.SemaphoreType.DMA((3,))],
+        + [
+            pltpu.VMEM(shape, query.dtype),
+            pltpu.SemaphoreType.DMA((3,)),
+            pltpu.SemaphoreType.DMA((3, 2 if heads % 2 == 0 else 1)),
+        ],
         compiler_params=pltpu.CompilerParams(vmem_limit_bytes=56 * 1024 * 1024),
         name="pack_heads",
     )(query, key, value)
@@ -66,7 +85,8 @@
 ):
     head_width = out_ref.shape[2]
     tiles = out_ref.shape[0]
-    tile_count = gathered_ref.shape[0] // TILE
+    here = gathered_ref.shape[2] // TILE
+    tile_count = gathered_ref.shape[0] * here
     together = scores.shape[0]
     scale = math.log2(math.e) / math.sqrt(head_width)
     to_smem = [
@@ -81,6 +101,10 @@
     def rows_of(tile):
         return pl.ds(pl.multiple_of(tile * TILE, TILE), TILE)
 
+    def part(tile, place):
+        rows = pl.ds(pl.multiple_of(tile % here * TILE, TILE), TILE)
+        return gathered_ref[tile // here, place, rows, :]
+
     def each(count, step):
         if count <= UNROLL:
             for index in range(count):
@@ -98,8 +122,7 @@
         column = jnp.sum(
             jnp.where(lane == which % LANES, columns[which // LANES], 0.0), axis=1, keepdims=True
         )
-        values = gathered_ref[rows_of(tile), place * head_width : (place + 1) * head_width]
-        values = values.astype(jnp.float32) * column * gains_ref[place : place + 1, :]
+        values = part(tile, place).astype(jnp.float32) * column * gains_ref[place : place + 1, :]
         return values.astype(jnp.bfloat16)
 
     def normalize_step(tile):
@@ -114,36 +137,40 @@
     def live_of(step):
         return [lists[step * most_live + slot] for slot in range(most_live)]
 
+    def score_tile(place, step):
+        keys = [normed_key[rows_of(live), :] for live in live_of(step)]
+        score = lax.dot_general(
+            normed_query[rows_of(base + step), :],
+            jnp.concatenate(keys, axis=0),
+            (((1,), (1,)), ((), ())),
+            preferred_element_type=jnp.float32,
+        )
+        slot = lax.broadcasted_iota(jnp.int32, (1, most_live * TILE), 1) // TILE
+        score = jnp.where(slot < counts[step], score, -jnp.inf)
+        scores[place] = score
+        largest = jnp.max(score, axis=1, keepdims=True)
+        rows_kept[place] = jnp.broadcast_to(largest, (TILE, LANES))
+
+    def weigh_tile(place, step):
+        largest = jnp.concatenate([rows_kept[place]] * most_live, axis=1)
+        weight = jnp.exp2((scores[place] - largest) * scale)
+        weights[place] = weight.astype(jnp.bfloat16)
+        denominators = jnp.sum(weight, axis=1, keepdims=True)
+        rows_kept[place] = jnp.broadcast_to(denominators, (TILE, LANES))
+
+    def value_tile(place, step):
+        values = [part(live, 2) for live in live_of(step)]
+        total = jnp.dot(
+            weights[place], jnp.concatenate(values, axis=0), preferred_element_type=jnp.float32
+        )
+        out_ref[step] = (total / rows_kept[place]).astype(out_ref.dtype)
+
     def some_tiles(first):
-        for place in range(together):
-            step = first + place
-            keys = [normed_key[rows_of(live), :] for live in live_of(step)]
-            score = lax.dot_general(
-                normed_query[rows_of(base + step), :],
-                jnp.concatenate(keys, axis=0),
-                (((1,), (1,)), ((), ())),
-                preferred_element_type=jnp.float32,
-            )
-            slot = lax.broadcasted_iota(jnp.int32, (1, most_live * TILE), 1) // TILE
-            score = jnp.where(slot < counts[step], score, -jnp.inf)
-            scores[place] = score
-            largest = jnp.max(score, axis=1, keepdims=True)
-            rows_kept[place] = jnp.broadcast_to(largest, (TILE, LANES))
-        for place in range(together):
-            largest = jnp.concatenate([rows_kept[place]] * most_live, axis=1)
-            weight = jnp.exp2((scores[place] - largest) * scale)
-            weights[place] = weight.astype(jnp.bfloat16)
-            denominators = jnp.sum(weight, axis=1, keepdims=True)
-            rows_kept[place] = jnp.broadcast_to(denominators, (TILE, LANES))
-        for place in range(together):
-            step = first + place
-            values = [gathered_ref[rows_of(live), 2 * head_width :] for live in live_of(step)]
-            total = jnp.dot(
-                weights[place],
-                jnp.concatenate(values, axis=0),
-                preferred_element_type=jnp.float32,
-            )
-            out_ref[step] = (total / rows_kept[place]).astype(out_ref.dtype)
+        for turn in range(together + 2 * APART):
+            for behind, stage in enumerate((score_tile, weigh_tile, value_tile)):
+                place = turn - behind * APART
+                if 0 <= place < together:
+                    stage(place, first + place)
 
     if tiles == together:
         some_tiles(0)
@@ -157,9 +184,9 @@
 
 
 def attend(gathered, factors, gains, lists, counts, base, tiles):
-    head_width = gathered.shape[1] // 3
+    device_count, _, tokens_here, head_width = gathered.shape
     most_live = lists.shape[1]
-    tile_count = gathered.shape[0] // TILE
+    tile_count = device_count * tokens_here // TILE
     blocks = -(-factors.shape[0] // LANES)
     factors = jnp.pad(factors, ((0, blocks * LANES - factors.shape[0]), (0, 0)))
     lists = lists.reshape(-1)
@@ -219,8 +246,7 @@
     outgoing = pack(query_proj, key_proj, value_proj, heads_here)
     if group_size > 1:
         outgoing = jnp.repeat(outgoing, group_size, axis=0)
-    incoming = lax.all_to_all(outgoing, "seq", split_axis=0, concat_axis=0, tiled=True)
-    gathered = incoming.reshape(device_count * tokens_here, 3 * head_width)
+    gathered = lax.all_to_all(outgoing, "seq", split_axis=0, concat_axis=0, tiled=True)
 
     query_values = query_proj.astype(jnp.float32)
     key_values = key_proj.astype(jnp.float32)
@@ -251,7 +277,8 @@
     if group_size > 1:
         returned = returned.reshape(heads_here, group_size, tokens_here, head_width)
         returned = returned.astype(jnp.float32).sum(axis=1).astype(jnp.bfloat16)
-    return returned.transpose(1, 0, 2).reshape(tokens_here, heads_here * head_width)
+    returned = returned.reshape(heads_here, tokens_here // 8, 8, head_width)
+    return returned.transpose(1, 2, 0, 3).reshape(tokens_here, heads_here * head_width)
 
 
 def solution(mesh):

time: 71.8 us -> 70.9 us (0.987)
  no operation moved by 1% of the time
where the time goes in v5:
time: 70.9 us; the launch traced here: 70.6 us
  waiting for transfers between devices  23.1 us (33%)
  blocking collectives  21.7 us (31%)
  starting transfers between devices  18.7 us (26%)
  Pallas kernels  4.72 us (7%)
  local copies, waits for them, and re-layouts  1.77 us (2%)
    ppermute x4, waiting for transfers between devices, gather_over(): other = lax.ppermute(held, axis, [(i, i ^ reach) for i in range(count)])  23.1 us
    all_to_all x1, blocking collectives, local(): lax.all_to_all(results, 'seq', split_axis=0, concat_axis=0, tiled=True)  19.2 us
    ppermute x4, starting transfers between devices, gather_over(): other = lax.ppermute(held, axis, [(i, i ^ reach) for i in range(count)])  10.3 us
    all_to_all x1, starting transfers between devices, local(): lax.all_to_all(outgoing, 'seq', split_axis=0, concat_axis=0, tiled=True)  8.46 us
    psum x1, blocking collectives, local(): squares = lax.psum(squares, 'tp')  2.47 us
    pallas_call x1, Pallas kernels, pack(): pl.pallas_call(pack_kernel, out_shape=jax.ShapeDtypeStruct(shape, query.d...  2.4 us
    pallas_call x1, Pallas kernels, attend(): pl.pallas_call(functools.partial(attend_kernel, most_live), out_shape=jax...  2.33 us
  transfers between devices with their start and end apart: 5, of which 4 were waited for; matrix products, arithmetic and copies ran while one was open for 2% of the time, Pallas kernels for 0%

profile of v5, /device:TPU:0, one launch (start us, length us, event | category | flops | bytes accessed | tf_op | source)
XLA Modules:
  0.0 70.6 jit_solution(14631519853840258161)
XLA Ops:
  0.0 0.0 copy-start
  0.0 2.4 %pack_heads.1 = bf16[16,3,128,128]{3,2,1,0:T(8,128)(2,1)} custom-call(bf16[128,2048]{1,0:T(8,128)(2,1)} %query_hbm.1, bf16[128,2048]{1,0:T(8,128)(2,1)} %key_hbm.1, bf16[128,2048]{1,0:T(8,128)(2,1)} %value_hbm.1), custom_call_target="tpu_custom_call" | custom-call | tf_op jit(solution)/shard_map/pack_heads/pallas_call | solution.py:52
  2.4 0.0 copy-start.1
  2.4 0.0 copy-start.2
  2.4 0.0 copy-start.3
  2.4 0.0 copy-start.4
  2.5 8.5 %all-to-all-start = ((bf16[16,3,128,128]{3,2,1,0:T(8,128)(2,1)}), bf16[16,3,128,128]{3,2,1,0:T(8,128)(2,1)S(1)}, u32[]{:S(2)}, u32[]{:S(2)}) async-start(bf16[16,3,128,128]{3,2,1,0:T(8,128)(2,1)} %pack_heads.1), calls=%async_computation | async-start | bytes 3145728 | tf_op jit(solution)/shard_map/all_to_all | solution.py:249
  10.9 0.0 copy-done.1
  10.9 0.2 multiply_reduce_fusion.1
  11.1 0.0 copy-done.2
  11.1 0.2 multiply_reduce_fusion
  11.3 2.5 %psum.7 = f32[2,128]{1,0:T(2,128)S(1)} all-reduce(f32[2,128]{1,0:T(2,128)S(1)} %pad_maximum_fusion), channel_id=1, replica_groups=mesh['seq'=16,'tp'=2] {'tp'}, use_global_device_ids=true, to_apply=%region_2.3 | all-reduce | flops 256 | bytes 2048 | tf_op jit(solution)/shard_map/psum | solution.py:256
  13.8 1.9 %collective-permute-start = (f32[1,2,128]{2,1,0:T(2,128)S(1)}, f32[1,2,128]{2,1,0:T(2,128)S(1)}, u32[]{:S(2)}, u32[]{:S(2)}) collective-permute-start(f32[1,2,128]{2,1,0:T(2,128)S(1)} %rsqrt_bitcast_fusion), channel_id=1, source_target_pairs={{0,2},{2,0},{4,6},{6,4},{8,10},{10,8},{12,14},{14,12},{16,18},{18,... | collective-permute-start | bytes 3080 | tf_op jit(solution)/shard_map/ppermute | solution.py:226
  15.7 0.0 copy-done
  15.7 1.7 %collective-permute-done = f32[1,2,128]{2,1,0:T(2,128)S(1)} collective-permute-done((f32[1,2,128]{2,1,0:T(2,128)S(1)}, f32[1,2,128]{2,1,0:T(2,128)S(1)}, u32[]{:S(2)}, u32[]{:S(2)}) %collective-permute-start) | collective-permute-done | bytes 1056 | tf_op jit(solution)/shard_map/ppermute | solution.py:226
  17.5 1.9 %collective-permute-start.1 = (f32[2,2,128]{2,1,0:T(2,128)S(1)}, f32[2,2,128]{2,1,0:T(2,128)S(1)}, u32[]{:S(2)}, u32[]{:S(2)}) collective-permute-start(f32[2,2,128]{2,1,0:T(2,128)S(1)} %maximum_select_fusion.3), channel_id=1, source_target_pairs={{0,4},{2,6},{4,0},{6,2},{8,12},{10,14},{12,8},{14,10},{16,20},{18,... | collective-permute-start | bytes 6152 | tf_op jit(solution)/shard_map/ppermute | solution.py:226
  19.4 0.0 copy-done.3
  19.4 0.0 copy-done.4
  19.4 1.7 %collective-permute-done.1 = f32[2,2,128]{2,1,0:T(2,128)S(1)} collective-permute-done((f32[2,2,128]{2,1,0:T(2,128)S(1)}, f32[2,2,128]{2,1,0:T(2,128)S(1)}, u32[]{:S(2)}, u32[]{:S(2)}) %collective-permute-start.1) | collective-permute-done | bytes 2080 | tf_op jit(solution)/shard_map/ppermute | solution.py:226
  21.1 1.9 %collective-permute-start.2 = (f32[4,2,128]{2,1,0:T(2,128)S(1)}, f32[4,2,128]{2,1,0:T(2,128)S(1)}, u32[]{:S(2)}, u32[]{:S(2)}) collective-permute-start(f32[4,2,128]{2,1,0:T(2,128)S(1)} %maximum_select_fusion.2), channel_id=1, source_target_pairs={{0,8},{2,10},{4,12},{6,14},{8,0},{10,2},{12,4},{14,6},{16,24},{18,... | collective-permute-start | bytes 12296 | tf_op jit(solution)/shard_map/ppermute | solution.py:226
  22.9 0.7 fusion.3
  23.6 12.9 %collective-permute-done.2 = f32[4,2,128]{2,1,0:T(2,128)S(1)} collective-permute-done((f32[4,2,128]{2,1,0:T(2,128)S(1)}, f32[4,2,128]{2,1,0:T(2,128)S(1)}, u32[]{:S(2)}, u32[]{:S(2)}) %collective-permute-start.2) | collective-permute-done | bytes 4128 | tf_op jit(solution)/shard_map/ppermute | solution.py:226
  36.5 4.6 %collective-permute-start.3 = (f32[8,2,128]{2,1,0:T(2,128)S(1)}, f32[8,2,128]{2,1,0:T(2,128)S(1)}, u32[]{:S(2)}, u32[]{:S(2)}) collective-permute-start(f32[8,2,128]{2,1,0:T(2,128)S(1)} %maximum_select_fusion.1), channel_id=1, source_target_pairs={{0,16},{2,18},{4,20},{6,22},{8,24},{10,26},{12,28},{14,30},{16,0},... | collective-permute-start | bytes 24584 | tf_op jit(solution)/shard_map/ppermute | solution.py:226
  41.1 0.1 pad_add_fusion.counts_hbm
  41.2 0.1 copy.11
  41.3 0.1 reshape.19.lists_hbm
  41.4 6.8 %collective-permute-done.3 = f32[8,2,128]{2,1,0:T(2,128)S(1)} collective-permute-done((f32[8,2,128]{2,1,0:T(2,128)S(1)}, f32[8,2,128]{2,1,0:T(2,128)S(1)}, u32[]{:S(2)}, u32[]{:S(2)}) %collective-permute-start.3) | collective-permute-done | bytes 8224 | tf_op jit(solution)/shard_map/ppermute | solution.py:226
  48.2 0.0 all-to-all-done.gathered_ref
  48.2 2.3 %attend.1 = bf16[16,128,128]{2,1,0:T(8,128)(2,1)S(1)} custom-call(s32[64]{0:T(128)S(1)} %reshape.19.lists_hbm, s32[17]{0:T(128)S(1)} %pad_add_fusion.counts_hbm, f32[128,128]{1,0:T(8,128)S(1)} %pad.4.factors_ref, f32[2,128]{1,0:T(2,128)S(1)} %fusion.2.gains_ref, bf16[16,3,128,128]{3,2,1,0:T(8,128)(2,1)S(1)} %all-to-all-done.gathered_ref), custom_call_target="tpu_custom_call" | custom-call | tf_op jit(solution)/shard_map/attend/pallas_call | solution.py:197
  50.6 19.2 %all_to_all.10 = bf16[16,128,128]{2,1,0:T(8,128)(2,1)S(1)} all-to-all(bf16[16,128,128]{2,1,0:T(8,128)(2,1)S(1)} %attend.1), channel_id=1, replica_groups=mesh['seq'=16,'tp'=2] {'seq'}, dimensions={0} | all-to-all | bytes 1048576 | tf_op jit(solution)/shard_map/all_to_all | solution.py:276
  69.8 0.9 %copy_bitcast_fusion = bf16[128,2048]{1,0:T(8,128)(2,1)} fusion(bf16[16,128,128]{2,1,0:T(8,128)(2,1)S(1)} %all_to_all.10), kind=kLoop, calls=%fused_computation.2 | loop fusion | bytes 1048576 | tf_op jit(solution)/shard_map/reshape | solution.py:281
  (10 shorter events, 0.1 us)
Async XLA Ops:
  0.0 15.7 %copy-start = (s32[16,16,4]{1,2,0:T(4,128)S(1)}, s32[16,16,4]{1,2,0:T(4,128)}, u32[]{:S(2)}) copy-start(s32[16,16,4]{1,2,0:T(4,128)} %param.12) | copy-start | bytes 12292
  2.4 8.5 %copy-start.1 = (bf16[128,2048]{1,0:T(8,128)(2,1)S(1)}, bf16[128,2048]{1,0:T(8,128)(2,1)}, u32[]{:S(2)}) copy-start(bf16[128,2048]{1,0:T(8,128)(2,1)} %query_hbm.1) | copy-start | bytes 1572868
  2.4 8.7 %copy-start.2 = (bf16[128,2048]{1,0:T(8,128)(2,1)S(1)}, bf16[128,2048]{1,0:T(8,128)(2,1)}, u32[]{:S(2)}) copy-start(bf16[128,2048]{1,0:T(8,128)(2,1)} %key_hbm.1) | copy-start | bytes 1572868
  2.4 16.9 %copy-start.3 = (f32[2048]{0:T(1024)S(1)}, f32[2048]{0:T(1024)}, u32[]{:S(2)}) copy-start(f32[2048]{0:T(1024)} %param.11) | copy-start | bytes 24580
  2.4 16.9 %copy-start.4 = (f32[2048]{0:T(1024)S(1)}, f32[2048]{0:T(1024)}, u32[]{:S(2)}) copy-start(f32[2048]{0:T(1024)} %param.10) | copy-start | bytes 24580
  2.5 45.8 %all-to-all-start = ((bf16[16,3,128,128]{3,2,1,0:T(8,128)(2,1)}), bf16[16,3,128,128]{3,2,1,0:T(8,128)(2,1)S(1)}, u32[]{:S(2)}, u32[]{:S(2)}) async-start(bf16[16,3,128,128]{3,2,1,0:T(8,128)(2,1)} %pack_heads.1), calls=%async_computation | async-start | bytes 3145728 | tf_op jit(solution)/shard_map/all_to_all | solution.py:249
  13.8 3.6 %collective-permute-start = (f32[1,2,128]{2,1,0:T(2,128)S(1)}, f32[1,2,128]{2,1,0:T(2,128)S(1)}, u32[]{:S(2)}, u32[]{:S(2)}) collective-permute-start(f32[1,2,128]{2,1,0:T(2,128)S(1)} %rsqrt_bitcast_fusion), channel_id=1, source_target_pairs={{0,2},{2,0},{4,6},{6,4},{8,10},{10,8},{12,14},{14,12},{16,18},{18,... | collective-permute-start | bytes 3080 | tf_op jit(solution)/shard_map/ppermute | solution.py:226
  17.5 3.6 %collective-permute-start.1 = (f32[2,2,128]{2,1,0:T(2,128)S(1)}, f32[2,2,128]{2,1,0:T(2,128)S(1)}, u32[]{:S(2)}, u32[]{:S(2)}) collective-permute-start(f32[2,2,128]{2,1,0:T(2,128)S(1)} %maximum_select_fusion.3), channel_id=1, source_target_pairs={{0,4},{2,6},{4,0},{6,2},{8,12},{10,14},{12,8},{14,10},{16,20},{18,... | collective-permute-start | bytes 6152 | tf_op jit(solution)/shard_map/ppermute | solution.py:226
  21.1 15.5 %collective-permute-start.2 = (f32[4,2,128]{2,1,0:T(2,128)S(1)}, f32[4,2,128]{2,1,0:T(2,128)S(1)}, u32[]{:S(2)}, u32[]{:S(2)}) collective-permute-start(f32[4,2,128]{2,1,0:T(2,128)S(1)} %maximum_select_fusion.2), channel_id=1, source_target_pairs={{0,8},{2,10},{4,12},{6,14},{8,0},{10,2},{12,4},{14,6},{16,24},{18,... | collective-permute-start | bytes 12296 | tf_op jit(solution)/shard_map/ppermute | solution.py:226
  36.5 11.6 %collective-permute-start.3 = (f32[8,2,128]{2,1,0:T(2,128)S(1)}, f32[8,2,128]{2,1,0:T(2,128)S(1)}, u32[]{:S(2)}, u32[]{:S(2)}) collective-permute-start(f32[8,2,128]{2,1,0:T(2,128)S(1)} %maximum_select_fusion.1), channel_id=1, source_target_pairs={{0,16},{2,18},{4,20},{6,22},{8,24},{10,26},{12,28},{14,30},{16,0},... | collective-permute-start | bytes 24584 | tf_op jit(solution)/shard_map/ppermute | solution.py:226

commit v6 on v5

--- a/solution.py
+++ b/solution.py
@@ -215,21 +215,22 @@
     )(lists, counts, factors, gains, gathered)
 
 
-def gather_over(values, axis):
-    count = lax.axis_size(axis)
-    if count & (count - 1):
-        return lax.all_gather(values, axis)
-    me = lax.axis_index(axis)
-    held = values[None]
-    reach = 1
-    while reach < count:
-        other = lax.ppermute(held, axis, [(i, i ^ reach) for i in range(count)])
-        upper = (me & reach) != 0
-        held = jnp.where(
-            upper, jnp.concatenate([other, held], 0), jnp.concatenate([held, other], 0)
-        )
-        reach *= 2
-    return held
+def squares_of(query, key):
+    query, key = query.astype(jnp.float32), key.astype(jnp.float32)
+    return jnp.stack([jnp.sum(query * query, axis=1), jnp.sum(key * key, axis=1)])
+
+
+def swapped(held, reach, halves):
+    count, width = lax.axis_size("seq"), lax.axis_size("tp")
+    pairs = [(i * width + t, (i ^ reach) * width + t) for i in range(count) for t in halves]
+    return lax.ppermute(held, ("seq", "tp"), pairs)
+
+
+def doubled(held, reach, halves):
+    other = swapped(held, reach, halves)
+    upper = (lax.axis_index("seq") & reach) != 0
+    first, second = jnp.where(upper, other, held), jnp.where(upper, held, other)
+    return jnp.stack([first, second], axis=held.ndim - 2)
 
 
 def local(query_proj, key_proj, value_proj, query_gain, key_gain, live_tiles, live_count):
@@ -244,17 +245,36 @@
     my_member = my_index % group_size
 
     outgoing = pack(query_proj, key_proj, value_proj, heads_here)
+    halves = range(lax.axis_size("tp"))
+    first_half = lax.axis_index("tp") == 0
+    reaches = [1 << bit for bit in reversed(range((device_count - 1).bit_length()))]
+    far, near = reaches[: len(reaches) // 2], reaches[len(reaches) // 2 :]
+    spread = 1 << len(far)
+
+    def gather_far(query, key):
+        held = squares_of(query, key)
+        for reach in far:
+            held = doubled(held, reach, halves[:1])
+        return held.reshape(spread, 2, tokens_here)
+
+    def nothing(query, key):
+        return jnp.zeros((spread, 2, tokens_here), jnp.float32)
+
+    early = lax.cond(first_half, gather_far, nothing, query_proj, key_proj)
+    outgoing, early = lax.optimization_barrier((outgoing, early))
     if group_size > 1:
         outgoing = jnp.repeat(outgoing, group_size, axis=0)
     gathered = lax.all_to_all(outgoing, "seq", split_axis=0, concat_axis=0, tiled=True)
 
-    query_values = query_proj.astype(jnp.float32)
-    key_values = key_proj.astype(jnp.float32)
-    squares = jnp.stack(
-        [jnp.sum(query_values * query_values, axis=1), jnp.sum(key_values * key_values, axis=1)]
-    )
-    squares = lax.psum(squares, "tp")
-    factors = gather_over(lax.rsqrt(squares / full_width + epsilon), "seq")
+    place = jnp.arange(spread)[:, None, None] == my_index // (device_count // spread)
+    own = jnp.where(place, squares_of(query_proj, key_proj)[None], 0.0)
+    held = jnp.where(first_half, early, own)
+    for reach in near:
+        held = doubled(held, reach, halves)
+    for reach in reversed(far):
+        held = held + swapped(held, reach, halves[1:])
+    squares = lax.psum(held.reshape(device_count, 2, tokens_here), "tp")
+    factors = lax.rsqrt(squares / full_width + epsilon)
     tile_count = device_count * tokens_here // TILE
     factors = factors.transpose(1, 0, 2).reshape(2 * tile_count, TILE)
     gains = jnp.stack([query_gain, key_gain]).reshape(2, heads_here, head_width)

time: 70.9 us -> 68.3 us (0.963)
  waiting for transfers between devices: 23.1 us -> 15.4 us
  starting transfers between devices: 18.7 us -> 23.4 us
  other arithmetic: 0.5 us -> 2.22 us
  blocking collectives: 21.7 us -> 20.2 us
    ppermute x4 -> x6, waiting for transfers between devices: 23.1 us -> 11.4 us  [swapped(): return lax.ppermute(held, ('seq', 'tp'), pairs)]
    ppermute x4 -> x6, starting transfers between devices: 10.3 us -> 14.3 us  [swapped(): return lax.ppermute(held, ('seq', 'tp'), pairs)]
    all_to_all x1, waiting for transfers between devices: 0.01 us -> 3.96 us  [local(): lax.all_to_all(outgoing, 'seq', split_axis=0, concat_axis=0, tiled=True)]
    all_to_all x1, blocking collectives: 19.2 us -> 16.8 us  [local(): lax.all_to_all(results, 'seq', split_axis=0, concat_axis=0, tiled=True)]
    reduce_sum x2 -> x3, other arithmetic: 0.37 us -> 1.86 us  [the longest x2 1.67 us: squares_of(): jnp.sum(key * key, axis=1)]
    psum x1, blocking collectives: 2.47 us -> 3.36 us  [local(): squares = lax.psum(held.reshape(device_count, 2, tokens_here), 'tp')]
  transfers between devices with their start and end apart: 5 -> 7, of which waited for: 4 -> 5; matrix products, arithmetic and copies ran while one was open for 2% -> 2% of each run, Pallas kernels for 0% -> 0%
where the time goes in v6:
time: 68.3 us; the launch traced here: 67.9 us
  starting transfers between devices  23.4 us (34%)
  blocking collectives  20.2 us (30%)
  waiting for transfers between devices  15.4 us (23%)
  Pallas kernels  4.68 us (7%)
  other arithmetic  2.22 us (3%)
  local copies, waits for them, and re-layouts  1.79 us (3%)
    all_to_all x1, blocking collectives, local(): lax.all_to_all(results, 'seq', split_axis=0, concat_axis=0, tiled=True)  16.8 us
    ppermute x6, starting transfers between devices, swapped(): return lax.ppermute(held, ('seq', 'tp'), pairs)  14.3 us
    ppermute x6, waiting for transfers between devices, swapped(): return lax.ppermute(held, ('seq', 'tp'), pairs)  11.4 us
    all_to_all x1, starting transfers between devices, local(): lax.all_to_all(outgoing, 'seq', split_axis=0, concat_axis=0, tiled=True)  9.04 us
    all_to_all x1, waiting for transfers between devices, local(): lax.all_to_all(outgoing, 'seq', split_axis=0, concat_axis=0, tiled=True)  3.96 us
    psum x1, blocking collectives, local(): squares = lax.psum(held.reshape(device_count, 2, tokens_here), 'tp')  3.36 us
    pallas_call x1, Pallas kernels, pack(): pl.pallas_call(pack_kernel, out_shape=jax.ShapeDtypeStruct(shape, query.d...  2.35 us
    pallas_call x1, Pallas kernels, attend(): pl.pallas_call(functools.partial(attend_kernel, most_live), out_shape=jax...  2.33 us
  transfers between devices with their start and end apart: 7, of which 5 were waited for; matrix products, arithmetic and copies ran while one was open for 2% of the time, Pallas kernels for 0%

profile of v6, /device:TPU:0, one launch (start us, length us, event | category | flops | bytes accessed | tf_op | source)
XLA Modules:
  0.0 67.9 jit_solution(10043033708548639358)
XLA Ops:
  0.0 2.4 %pack_heads.1 = bf16[16,3,128,128]{3,2,1,0:T(8,128)(2,1)} custom-call(bf16[128,2048]{1,0:T(8,128)(2,1)} %query_hbm.1, bf16[128,2048]{1,0:T(8,128)(2,1)} %key_hbm.1, bf16[128,2048]{1,0:T(8,128)(2,1)} %value_hbm.1), custom_call_target="tpu_custom_call" | custom-call | tf_op jit(solution)/shard_map/pack_heads/pallas_call | solution.py:52
  2.4 15.0 %conditional.1 = (f32[4,2,128]{2,1,0:T(2,128)S(1)}) conditional(s32[]{:T(128)} %convert_element_type.17, () %tuple.12, (bf16[128,2048]{1,0:T(8,128)(2,1)}, bf16[128,2048]{1,0:T(8,128)(2,1)}) %tuple.13), branch_computations={%region_0.1_spmd, %region_1.4_spmd} | conditional | flops 1576711 | bytes 1096868 | solution.py:263
  2.4 1.5 %multiply_reduce_fusion = (f32[128]{0:T(128)S(1)}, f32[128]{0:T(128)S(1)}) fusion(bf16[128,2048]{1,0:T(8,128)(2,1)} %get-tuple-element.13, bf16[128,2048]{1,0:T(8,128)(2,1)} %get-tuple-element.12), kind=kLoop, calls=%fused_computation | loop fusion | flops 1572608 | bytes 1049600 | tf_op jit(solution)/shard_map/cond/branch_1_fun/reduce_sum | solution.py:220
  3.9 5.9 %collective-permute-start = (f32[2,128]{1,0:T(2,128)S(1)}, f32[2,128]{1,0:T(2,128)S(1)}, u32[]{:S(2)}, u32[]{:S(2)}) collective-permute-start(f32[2,128]{1,0:T(2,128)S(1)} %pad_maximum_fusion.2), channel_id=1, source_target_pairs={{0,16},{2,18},{4,20},{6,22},{8,24},{10,26},{12,28},{14,30},{16,0},... | collective-permute-start | bytes 3080 | tf_op jit(solution)/shard_map/cond/branch_1_fun/ppermute | solution.py:226
  9.8 1.5 %collective-permute-done = f32[2,128]{1,0:T(2,128)S(1)} collective-permute-done((f32[2,128]{1,0:T(2,128)S(1)}, f32[2,128]{1,0:T(2,128)S(1)}, u32[]{:S(2)}, u32[]{:S(2)}) %collective-permute-start) | collective-permute-done | bytes 1056 | tf_op jit(solution)/shard_map/cond/branch_1_fun/ppermute | solution.py:226
  11.4 3.8 %collective-permute-start.1 = (f32[2,2,128]{2,1,0:T(2,128)S(1)}, f32[2,2,128]{2,1,0:T(2,128)S(1)}, u32[]{:S(2)}, u32[]{:S(2)}) collective-permute-start(f32[2,2,128]{2,1,0:T(2,128)S(1)} %pad_maximum_fusion.1), channel_id=1, source_target_pairs={{0,8},{2,10},{4,12},{6,14},{8,0},{10,2},{12,4},{14,6},{16,24},{18,... | collective-permute-start | bytes 6152 | tf_op jit(solution)/shard_map/cond/branch_1_fun/ppermute | solution.py:226
  15.2 2.2 %collective-permute-done.1 = f32[2,2,128]{2,1,0:T(2,128)S(1)} collective-permute-done((f32[2,2,128]{2,1,0:T(2,128)S(1)}, f32[2,2,128]{2,1,0:T(2,128)S(1)}, u32[]{:S(2)}, u32[]{:S(2)}) %collective-permute-start.1) | collective-permute-done | bytes 2080 | tf_op jit(solution)/shard_map/cond/branch_1_fun/ppermute | solution.py:226
  17.4 0.0 copy-start.1
  17.4 0.0 copy-start.2
  17.4 0.0 copy-start.3
  17.4 0.0 copy-start.4
  17.5 9.0 %all-to-all-start = ((bf16[16,3,128,128]{3,2,1,0:T(8,128)(2,1)}), bf16[16,3,128,128]{3,2,1,0:T(8,128)(2,1)S(1)}, u32[]{:S(2)}, u32[]{:S(2)}) async-start(bf16[16,3,128,128]{3,2,1,0:T(8,128)(2,1)} %pack_heads.1), calls=%async_computation | async-start | bytes 3145728 | tf_op jit(solution)/shard_map/all_to_all | solution.py:267
  26.5 0.2 multiply_reduce_fusion.3
  26.7 0.2 multiply_reduce_fusion.2
  26.9 0.1 select_select_fusion
  27.0 1.9 %collective-permute-start.2 = (f32[4,2,128]{2,1,0:T(2,128)S(1)}, f32[4,2,128]{2,1,0:T(2,128)S(1)}, u32[]{:S(2)}, u32[]{:S(2)}) collective-permute-start(f32[4,2,128]{2,1,0:T(2,128)S(1)} %select_select_fusion), channel_id=1, source_target_pairs={{0,4},{1,5},{2,6},{3,7},{4,0},{5,1},{6,2},{7,3},{8,12},{9,13},{10,... | collective-permute-start | bytes 12296 | tf_op jit(solution)/shard_map/ppermute | solution.py:226
  28.9 5.4 %collective-permute-done.2 = f32[4,2,128]{2,1,0:T(2,128)S(1)} collective-permute-done((f32[4,2,128]{2,1,0:T(2,128)S(1)}, f32[4,2,128]{2,1,0:T(2,128)S(1)}, u32[]{:S(2)}, u32[]{:S(2)}) %collective-permute-start.2) | collective-permute-done | bytes 4128 | tf_op jit(solution)/shard_map/ppermute | solution.py:226
  34.3 0.1 select_bitcast_fusion.7
  34.4 1.4 %collective-permute-start.3 = (f32[4,2,2,128]{3,2,0,1:T(2,128)S(1)}, f32[4,2,2,128]{3,2,0,1:T(2,128)S(1)}, u32[]{:S(2)}, u32[]{:S(2)}) collective-permute-start(f32[4,2,2,128]{3,2,0,1:T(2,128)S(1)} %pad_maximum_fusion.4), channel_id=1, source_target_pairs={{0,2},{1,3},{2,0},{3,1},{4,6},{5,7},{6,4},{7,5},{8,10},{9,11},{10,... | collective-permute-start | bytes 24584 | tf_op jit(solution)/shard_map/ppermute | solution.py:226
  35.8 2.3 %collective-permute-done.3 = f32[4,2,2,128]{3,2,0,1:T(2,128)S(1)} collective-permute-done((f32[4,2,2,128]{3,2,0,1:T(2,128)S(1)}, f32[4,2,2,128]{3,2,0,1:T(2,128)S(1)}, u32[]{:S(2)}, u32[]{:S(2)}) %collective-permute-start.3) | collective-permute-done | bytes 8224 | tf_op jit(solution)/shard_map/ppermute | solution.py:226
  38.1 0.7 collective-permute-start.4
  38.8 0.7 %fusion.2 = s32[16]{0:T(128)S(1)} fusion(s32[16,16]{1,0:T(8,128)} %param.15, s32[]{:T(128)S(6)} %select_n.78), kind=kLoop, calls=%fused_computation.27 | loop fusion | bytes 132 | tf_op jit(solution)/shard_map/jit(dynamic_index_in_dim)/squeeze | solution.py:286
  39.5 0.0 collective-permute-done.4
  39.5 0.7 collective-permute-start.5
  40.2 0.1 pad_add_fusion.counts_hbm
  40.3 0.1 copy.11
  40.4 0.1 reshape.31.lists_hbm
  40.5 3.4 %psum.7 = f32[16,2,128]{2,0,1:T(8,128)S(1)} all-reduce(f32[16,2,128]{2,0,1:T(8,128)S(1)} %bitcast.39), channel_id=1, replica_groups=mesh['seq'=16,'tp'=2] {'tp'}, use_global_device_ids=true, to_apply=%region_6.7 | all-reduce | flops 4096 | bytes 32768 | tf_op jit(solution)/shard_map/psum | solution.py:276
  43.9 4.0 %all-to-all-done.gathered_ref = bf16[16,3,128,128]{3,2,1,0:T(8,128)(2,1)S(1)} async-done(((bf16[16,3,128,128]{3,2,1,0:T(8,128)(2,1)}), bf16[16,3,128,128]{3,2,1,0:T(8,128)(2,1)S(1)}, u32[]{:S(2)}, u32[]{:S(2)}) %all-to-all-start) | async-done | bytes 1572896 | tf_op jit(solution)/shard_map/all_to_all | solution.py:267
  47.8 2.3 %attend.1 = bf16[16,128,128]{2,1,0:T(8,128)(2,1)S(1)} custom-call(s32[64]{0:T(128)S(1)} %reshape.31.lists_hbm, s32[17]{0:T(128)S(1)} %pad_add_fusion.counts_hbm, f32[128,128]{1,0:T(8,128)S(1)} %pad.4.factors_ref, f32[2,128]{1,0:T(2,128)S(1)} %fusion.1.gains_ref, bf16[16,3,128,128]{3,2,1,0:T(8,128)(2,1)S(1)} %all-to-all-done.gathered_ref), custom_call_target="tpu_custom_call" | custom-call | tf_op jit(solution)/shard_map/attend/pallas_call | solution.py:197
  50.2 16.8 %all_to_all.10 = bf16[16,128,128]{2,1,0:T(8,128)(2,1)S(1)} all-to-all(bf16[16,128,128]{2,1,0:T(8,128)(2,1)S(1)} %attend.1), channel_id=1, replica_groups=mesh['seq'=16,'tp'=2] {'seq'}, dimensions={0} | all-to-all | bytes 1048576 | tf_op jit(solution)/shard_map/all_to_all | solution.py:296
  67.0 0.9 %copy_bitcast_fusion = bf16[128,2048]{1,0:T(8,128)(2,1)} fusion(bf16[16,128,128]{2,1,0:T(8,128)(2,1)S(1)} %all_to_all.10), kind=kLoop, calls=%fused_computation.11 | loop fusion | bytes 1048576 | tf_op jit(solution)/shard_map/reshape | solution.py:301
  (25 shorter events, 0.2 us)
Async XLA Ops:
  0.0 28.9 %copy-start = (s32[16,16,4]{1,2,0:T(4,128)S(1)}, s32[16,16,4]{1,2,0:T(4,128)}, u32[]{:S(2)}) copy-start(s32[16,16,4]{1,2,0:T(4,128)} %param.14) | copy-start | bytes 12292
  3.9 7.5 %collective-permute-start = (f32[2,128]{1,0:T(2,128)S(1)}, f32[2,128]{1,0:T(2,128)S(1)}, u32[]{:S(2)}, u32[]{:S(2)}) collective-permute-start(f32[2,128]{1,0:T(2,128)S(1)} %pad_maximum_fusion.2), channel_id=1, source_target_pairs={{0,16},{2,18},{4,20},{6,22},{8,24},{10,26},{12,28},{14,30},{16,0},... | collective-permute-start | bytes 3080 | tf_op jit(solution)/shard_map/cond/branch_1_fun/ppermute | solution.py:226
  11.4 6.0 %collective-permute-start.1 = (f32[2,2,128]{2,1,0:T(2,128)S(1)}, f32[2,2,128]{2,1,0:T(2,128)S(1)}, u32[]{:S(2)}, u32[]{:S(2)}) collective-permute-start(f32[2,2,128]{2,1,0:T(2,128)S(1)} %pad_maximum_fusion.1), channel_id=1, source_target_pairs={{0,8},{2,10},{4,12},{6,14},{8,0},{10,2},{12,4},{14,6},{16,24},{18,... | collective-permute-start | bytes 6152 | tf_op jit(solution)/shard_map/cond/branch_1_fun/ppermute | solution.py:226
  17.4 9.1 %copy-start.1 = (bf16[128,2048]{1,0:T(8,128)(2,1)S(1)}, bf16[128,2048]{1,0:T(8,128)(2,1)}, u32[]{:S(2)}) copy-start(bf16[128,2048]{1,0:T(8,128)(2,1)} %query_hbm.1) | copy-start | bytes 1572868
  17.4 9.3 %copy-start.2 = (bf16[128,2048]{1,0:T(8,128)(2,1)S(1)}, bf16[128,2048]{1,0:T(8,128)(2,1)}, u32[]{:S(2)}) copy-start(bf16[128,2048]{1,0:T(8,128)(2,1)} %key_hbm.1) | copy-start | bytes 1572868
  17.4 18.3 %copy-start.3 = (f32[2048]{0:T(1024)S(1)}, f32[2048]{0:T(1024)}, u32[]{:S(2)}) copy-start(f32[2048]{0:T(1024)} %param.13) | copy-start | bytes 24580
  17.4 18.3 %copy-start.4 = (f32[2048]{0:T(1024)S(1)}, f32[2048]{0:T(1024)}, u32[]{:S(2)}) copy-start(f32[2048]{0:T(1024)} %param.12) | copy-start | bytes 24580
  17.5 30.4 %all-to-all-start = ((bf16[16,3,128,128]{3,2,1,0:T(8,128)(2,1)}), bf16[16,3,128,128]{3,2,1,0:T(8,128)(2,1)S(1)}, u32[]{:S(2)}, u32[]{:S(2)}) async-start(bf16[16,3,128,128]{3,2,1,0:T(8,128)(2,1)} %pack_heads.1), calls=%async_computation | async-start | bytes 3145728 | tf_op jit(solution)/shard_map/all_to_all | solution.py:267
  27.0 7.3 %collective-permute-start.2 = (f32[4,2,128]{2,1,0:T(2,128)S(1)}, f32[4,2,128]{2,1,0:T(2,128)S(1)}, u32[]{:S(2)}, u32[]{:S(2)}) collective-permute-start(f32[4,2,128]{2,1,0:T(2,128)S(1)} %select_select_fusion), channel_id=1, source_target_pairs={{0,4},{1,5},{2,6},{3,7},{4,0},{5,1},{6,2},{7,3},{8,12},{9,13},{10,... | collective-permute-start | bytes 12296 | tf_op jit(solution)/shard_map/ppermute | solution.py:226
  34.4 3.7 %collective-permute-start.3 = (f32[4,2,2,128]{3,2,0,1:T(2,128)S(1)}, f32[4,2,2,128]{3,2,0,1:T(2,128)S(1)}, u32[]{:S(2)}, u32[]{:S(2)}) collective-permute-start(f32[4,2,2,128]{3,2,0,1:T(2,128)S(1)} %pad_maximum_fusion.4), channel_id=1, source_target_pairs={{0,2},{1,3},{2,0},{3,1},{4,6},{5,7},{6,4},{7,5},{8,10},{9,11},{10,... | collective-permute-start | bytes 24584 | tf_op jit(solution)/shard_map/ppermute | solution.py:226
  38.1 1.4 %collective-permute-start.4 = (f32[4,2,2,2,128]{4,3,0,1,2:T(2,128)S(1)}, f32[4,2,2,2,128]{4,3,0,1,2:T(2,128)S(1)}, u32[]{:S(2)}, u32[]{:S(2)}) collective-permute-start(f32[4,2,2,2,128]{4,3,0,1,2:T(2,128)S(1)} %pad_maximum_fusion.3), channel_id=1, source_target_pairs={{1,9},{3,11},{5,13},{7,15},{9,1},{11,3},{13,5},{15,7},{17,25},{19,... | collective-permute-start | bytes 49160 | tf_op jit(solution)/shard_map/ppermute | solution.py:226
  39.5 0.9 %collective-permute-start.5 = (f32[4,2,2,2,128]{4,3,0,1,2:T(2,128)S(1)}, f32[4,2,2,2,128]{4,3,0,1,2:T(2,128)S(1)}, u32[]{:S(2)}, u32[]{:S(2)}) collective-permute-start(f32[4,2,2,2,128]{4,3,0,1,2:T(2,128)S(1)} %fusion.3), channel_id=1, source_target_pairs={{1,17},{3,19},{5,21},{7,23},{9,25},{11,27},{13,29},{15,31},{17,1},... | collective-permute-start | bytes 49160 | tf_op jit(solution)/shard_map/ppermute | solution.py:226

commit v7 on v6

--- a/solution.py
+++ b/solution.py
@@ -226,8 +226,8 @@
     return lax.ppermute(held, ("seq", "tp"), pairs)
 
 
-def doubled(held, reach, halves):
-    other = swapped(held, reach, halves)
+def doubled(held, reach, halves, across=None):
+    other = swapped(held, across or reach, halves)
     upper = (lax.axis_index("seq") & reach) != 0
     first, second = jnp.where(upper, other, held), jnp.where(upper, held, other)
     return jnp.stack([first, second], axis=held.ndim - 2)
@@ -254,7 +254,7 @@
     def gather_far(query, key):
         held = squares_of(query, key)
         for reach in far:
-            held = doubled(held, reach, halves[:1])
+            held = doubled(held, reach, halves[:1], reach + sum(far[: far.index(reach)]))
         return held.reshape(spread, 2, tokens_here)
 
     def nothing(query, key):
@@ -266,14 +266,26 @@
         outgoing = jnp.repeat(outgoing, group_size, axis=0)
     gathered = lax.all_to_all(outgoing, "seq", split_axis=0, concat_axis=0, tiled=True)
 
-    place = jnp.arange(spread)[:, None, None] == my_index // (device_count // spread)
-    own = jnp.where(place, squares_of(query_proj, key_proj)[None], 0.0)
-    held = jnp.where(first_half, early, own)
-    for reach in near:
-        held = doubled(held, reach, halves)
-    for reach in reversed(far):
-        held = held + swapped(held, reach, halves[1:])
-    squares = lax.psum(held.reshape(device_count, 2, tokens_here), "tp")
+    def rest_of_first(early, query, key):
+        for reach in near:
+            early = doubled(early, reach, halves[:1])
+        return early.reshape(device_count, 2, tokens_here)
+
+    def all_of_second(early, query, key):
+        held = squares_of(query, key)
+        for reach in near:
+            held = doubled(held, reach, halves[1:])
+        held = held.reshape(-1, 2, tokens_here)
+        for reach in reversed(far):
+            other = swapped(held, reach, halves[1:])
+            upper = (my_index & reach) != 0
+            held = jnp.concatenate(
+                [jnp.where(upper, other, held), jnp.where(upper, held, other)], axis=0
+            )
+        return held
+
+    held = lax.cond(first_half, rest_of_first, all_of_second, early, query_proj, key_proj)
+    squares = lax.psum(held, "tp")
     factors = lax.rsqrt(squares / full_width + epsilon)
     tile_count = device_count * tokens_here // TILE
     factors = factors.transpose(1, 0, 2).reshape(2 * tile_count, TILE)

time: 68.3 us -> 68 us (level)
  starting transfers between devices: 23.4 us -> 26.1 us
  waiting for transfers between devices: 15.4 us -> 13 us
    ppermute x6 -> x4, starting transfers between devices: 14.3 us -> 18.9 us  [swapped(): return lax.ppermute(held, ('seq', 'tp'), pairs)]
    all_to_all x1, starting transfers between devices: 9.04 us -> 7.2 us  [local(): lax.all_to_all(outgoing, 'seq', split_axis=0, concat_axis=0, tiled=True)]
    all_to_all x1, waiting for transfers between devices: 3.96 us -> 2.75 us  [local(): lax.all_to_all(outgoing, 'seq', split_axis=0, concat_axis=0, tiled=True)]
    ppermute x6 -> x4, waiting for transfers between devices: 11.4 us -> 10.3 us  [swapped(): return lax.ppermute(held, ('seq', 'tp'), pairs)]
    reduce_sum x2 -> x1, other arithmetic: 1.67 us -> 1.49 us  [squares_of(): jnp.sum(key * key, axis=1)]
  transfers between devices with their start and end apart: 7 -> 5, of which waited for: 5 -> 5; matrix products, arithmetic and copies ran while one was open for 2% -> 2% of each run, Pallas kernels for 0% -> 0%
where the time goes in v7:
time: 68 us; the launch traced here: 67.6 us
  starting transfers between devices  26.1 us (38%)
  blocking collectives  20.1 us (30%)
  waiting for transfers between devices  13 us (19%)
  Pallas kernels  4.69 us (7%)
  local copies, waits for them, and re-layouts  1.8 us (3%)
  other arithmetic  1.66 us (2%)
    ppermute x4, starting transfers between devices, swapped(): return lax.ppermute(held, ('seq', 'tp'), pairs)  18.9 us
    all_to_all x1, blocking collectives, local(): lax.all_to_all(results, 'seq', split_axis=0, concat_axis=0, tiled=True)  16.7 us
    ppermute x4, waiting for transfers between devices, swapped(): return lax.ppermute(held, ('seq', 'tp'), pairs)  10.3 us
    all_to_all x1, starting transfers between devices, local(): lax.all_to_all(outgoing, 'seq', split_axis=0, concat_axis=0, tiled=True)  7.2 us
    psum x1, blocking collectives, local(): squares = lax.psum(held, 'tp')  3.36 us
    all_to_all x1, waiting for transfers between devices, local(): lax.all_to_all(outgoing, 'seq', split_axis=0, concat_axis=0, tiled=True)  2.75 us
    pallas_call x1, Pallas kernels, pack(): pl.pallas_call(pack_kernel, out_shape=jax.ShapeDtypeStruct(shape, query.d...  2.37 us
    pallas_call x1, Pallas kernels, attend(): pl.pallas_call(functools.partial(attend_kernel, most_live), out_shape=jax...  2.32 us
  transfers between devices with their start and end apart: 5, of which 5 were waited for; matrix products, arithmetic and copies ran while one was open for 2% of the time, Pallas kernels for 0%

profile of v7, /device:TPU:0, one launch (start us, length us, event | category | flops | bytes accessed | tf_op | source)
XLA Modules:
  0.0 67.6 jit_solution(2755769100060125108)
XLA Ops:
  0.0 0.0 copy-start
  0.0 2.4 %pack_heads.1 = bf16[16,3,128,128]{3,2,1,0:T(8,128)(2,1)} custom-call(bf16[128,2048]{1,0:T(8,128)(2,1)} %query_hbm.1, bf16[128,2048]{1,0:T(8,128)(2,1)} %key_hbm.1, bf16[128,2048]{1,0:T(8,128)(2,1)} %value_hbm.1), custom_call_target="tpu_custom_call" | custom-call | tf_op jit(solution)/shard_map/pack_heads/pallas_call | solution.py:52
  2.4 16.6 %conditional.2 = (f32[4,2,128]{2,1,0:T(2,128)S(1)}) conditional(s32[]{:T(128)} %convert_element_type.18, () %tuple.19, (bf16[128,2048]{1,0:T(8,128)(2,1)}, bf16[128,2048]{1,0:T(8,128)(2,1)}) %tuple.20), branch_computations={%region_0.1_spmd, %region_1.4_spmd} | conditional | flops 1576711 | bytes 1096868 | solution.py:263
  2.4 1.5 %multiply_reduce_fusion = (f32[128]{0:T(128)S(1)}, f32[128]{0:T(128)S(1)}) fusion(bf16[128,2048]{1,0:T(8,128)(2,1)} %get-tuple-element.23, bf16[128,2048]{1,0:T(8,128)(2,1)} %get-tuple-element.22), kind=kLoop, calls=%fused_computation | loop fusion | flops 1572608 | bytes 1049600 | tf_op jit(solution)/shard_map/cond/branch_1_fun/reduce_sum | solution.py:220
  3.9 5.9 %collective-permute-start = (f32[2,128]{1,0:T(2,128)S(1)}, f32[2,128]{1,0:T(2,128)S(1)}, u32[]{:S(2)}, u32[]{:S(2)}) collective-permute-start(f32[2,128]{1,0:T(2,128)S(1)} %pad_maximum_fusion.2), channel_id=1, source_target_pairs={{0,16},{2,18},{4,20},{6,22},{8,24},{10,26},{12,28},{14,30},{16,0},... | collective-permute-start | bytes 3080 | tf_op jit(solution)/shard_map/cond/branch_1_fun/ppermute | solution.py:226
  9.9 1.5 %collective-permute-done = f32[2,128]{1,0:T(2,128)S(1)} collective-permute-done((f32[2,128]{1,0:T(2,128)S(1)}, f32[2,128]{1,0:T(2,128)S(1)}, u32[]{:S(2)}, u32[]{:S(2)}) %collective-permute-start) | collective-permute-done | bytes 1056 | tf_op jit(solution)/shard_map/cond/branch_1_fun/ppermute | solution.py:226
  11.4 5.8 %collective-permute-start.1 = (f32[2,2,128]{2,1,0:T(2,128)S(1)}, f32[2,2,128]{2,1,0:T(2,128)S(1)}, u32[]{:S(2)}, u32[]{:S(2)}) collective-permute-start(f32[2,2,128]{2,1,0:T(2,128)S(1)} %pad_maximum_fusion.1), channel_id=1, source_target_pairs={{0,24},{2,26},{4,28},{6,30},{8,16},{10,18},{12,20},{14,22},{16,8},... | collective-permute-start | bytes 6152 | tf_op jit(solution)/shard_map/cond/branch_1_fun/ppermute | solution.py:226
  17.3 1.7 %collective-permute-done.1 = f32[2,2,128]{2,1,0:T(2,128)S(1)} collective-permute-done((f32[2,2,128]{2,1,0:T(2,128)S(1)}, f32[2,2,128]{2,1,0:T(2,128)S(1)}, u32[]{:S(2)}, u32[]{:S(2)}) %collective-permute-start.1) | collective-permute-done | bytes 2080 | tf_op jit(solution)/shard_map/cond/branch_1_fun/ppermute | solution.py:226
  19.0 0.0 copy-start.1
  19.0 0.0 copy-start.2
  19.0 7.2 %all-to-all-start = ((bf16[16,3,128,128]{3,2,1,0:T(8,128)(2,1)}), bf16[16,3,128,128]{3,2,1,0:T(8,128)(2,1)S(1)}, u32[]{:S(2)}, u32[]{:S(2)}) async-start(bf16[16,3,128,128]{3,2,1,0:T(8,128)(2,1)} %pack_heads.1), calls=%async_computation | async-start | bytes 3145728 | tf_op jit(solution)/shard_map/all_to_all | solution.py:267
  26.2 0.0 copy-start.3
  26.2 0.0 copy-start.4
  26.2 0.0 copy-done
  26.3 0.1 copy.15
  26.3 0.0 copy-done.1
  26.3 0.0 copy-done.2
  26.3 0.1 reshape.28.lists_hbm
  26.4 14.2 %conditional.3 = (f32[16,2,128]{2,1,0:T(2,128)S(1)}) conditional(s32[]{:T(128)} %convert_element_type.18, (s32[]{:T(128)}, bf16[128,2048]{1,0:T(8,128)(2,1)S(1)}, bf16[128,2048]{1,0:T(8,128)(2,1)S(1)}) %tuple.37, f32[4,2,128]{2,1,0:T(2,128)S(1)} %get-tuple-element.51), branch_computations={%region_4.7_spmd, %region_7.8_spmd} | conditional | flops 1591051 | bytes 1244448 | solution.py:287
  26.4 3.8 %collective-permute-start.6 = (f32[4,2,128]{2,1,0:T(2,128)S(1)}, f32[4,2,128]{2,1,0:T(2,128)S(1)}, u32[]{:S(2)}, u32[]{:S(2)}) collective-permute-start(f32[4,2,128]{2,1,0:T(2,128)S(1)} %param.3), channel_id=1, source_target_pairs={{0,4},{2,6},{4,0},{6,2},{8,12},{10,14},{12,8},{14,10},{16,20},{18,... | collective-permute-start | bytes 12296 | tf_op jit(solution)/shard_map/cond/branch_1_fun/ppermute | solution.py:226
  30.3 4.0 %collective-permute-done.6 = f32[4,2,128]{2,1,0:T(2,128)S(1)} collective-permute-done((f32[4,2,128]{2,1,0:T(2,128)S(1)}, f32[4,2,128]{2,1,0:T(2,128)S(1)}, u32[]{:S(2)}, u32[]{:S(2)}) %collective-permute-start.6) | collective-permute-done | bytes 4128 | tf_op jit(solution)/shard_map/cond/branch_1_fun/ppermute | solution.py:226
  34.3 3.3 %collective-permute-start.7 = (f32[4,2,2,128]{3,2,0,1:T(2,128)S(1)}, f32[4,2,2,128]{3,2,0,1:T(2,128)S(1)}, u32[]{:S(2)}, u32[]{:S(2)}) collective-permute-start(f32[4,2,2,128]{3,2,0,1:T(2,128)S(1)} %pad_maximum_fusion.9), channel_id=1, source_target_pairs={{0,2},{2,0},{4,6},{6,4},{8,10},{10,8},{12,14},{14,12},{16,18},{18,... | collective-permute-start | bytes 24584 | tf_op jit(solution)/shard_map/cond/branch_1_fun/ppermute | solution.py:226
  37.6 3.1 %collective-permute-done.7 = f32[4,2,2,128]{3,2,0,1:T(2,128)S(1)} collective-permute-done((f32[4,2,2,128]{3,2,0,1:T(2,128)S(1)}, f32[4,2,2,128]{3,2,0,1:T(2,128)S(1)}, u32[]{:S(2)}, u32[]{:S(2)}) %collective-permute-start.7) | collective-permute-done | bytes 8224 | tf_op jit(solution)/shard_map/cond/branch_1_fun/ppermute | solution.py:226
  40.7 3.4 %psum.7 = f32[16,2,128]{2,1,0:T(2,128)S(1)} all-reduce(f32[16,2,128]{2,1,0:T(2,128)S(1)} %get-tuple-element.52), channel_id=1, replica_groups=mesh['seq'=16,'tp'=2] {'tp'}, use_global_device_ids=true, to_apply=%region_8.9 | all-reduce | flops 4096 | bytes 32768 | tf_op jit(solution)/shard_map/psum | solution.py:288
  44.1 0.7 %fusion.2 = s32[16]{0:T(128)S(1)} fusion(s32[16,16]{1,0:T(8,128)} %param.17, s32[]{:T(128)S(6)} %select_n.107), kind=kLoop, calls=%fused_computation.38 | loop fusion | bytes 132 | tf_op jit(solution)/shard_map/jit(dynamic_index_in_dim)/squeeze | solution.py:298
  44.8 0.1 pad_add_fusion.counts_hbm
  44.9 0.0 copy-done.3
  44.9 0.0 copy-done.4
  44.9 2.8 %all-to-all-done.gathered_ref = bf16[16,3,128,128]{3,2,1,0:T(8,128)(2,1)S(1)} async-done(((bf16[16,3,128,128]{3,2,1,0:T(8,128)(2,1)}), bf16[16,3,128,128]{3,2,1,0:T(8,128)(2,1)S(1)}, u32[]{:S(2)}, u32[]{:S(2)}) %all-to-all-start) | async-done | bytes 1572896 | tf_op jit(solution)/shard_map/all_to_all | solution.py:267
  47.6 2.3 %attend.1 = bf16[16,128,128]{2,1,0:T(8,128)(2,1)S(1)} custom-call(s32[64]{0:T(128)S(1)} %reshape.28.lists_hbm, s32[17]{0:T(128)S(1)} %pad_add_fusion.counts_hbm, f32[128,128]{1,0:T(8,128)S(1)} %pad.4.factors_ref, f32[2,128]{1,0:T(2,128)S(1)} %fusion.1.gains_ref, bf16[16,3,128,128]{3,2,1,0:T(8,128)(2,1)S(1)} %all-to-all-done.gathered_ref), custom_call_target="tpu_custom_call" | custom-call | tf_op jit(solution)/shard_map/attend/pallas_call | solution.py:197
  50.0 16.7 %all_to_all.10 = bf16[16,128,128]{2,1,0:T(8,128)(2,1)S(1)} all-to-all(bf16[16,128,128]{2,1,0:T(8,128)(2,1)S(1)} %attend.1), channel_id=1, replica_groups=mesh['seq'=16,'tp'=2] {'seq'}, dimensions={0} | all-to-all | bytes 1048576 | tf_op jit(solution)/shard_map/all_to_all | solution.py:308
  66.7 0.9 %copy_bitcast_fusion = bf16[128,2048]{1,0:T(8,128)(2,1)} fusion(bf16[16,128,128]{2,1,0:T(8,128)(2,1)S(1)} %all_to_all.10), kind=kLoop, calls=%fused_computation.30 | loop fusion | bytes 1048576 | tf_op jit(solution)/shard_map/reshape | solution.py:313
  (16 shorter events, 0.1 us)
Async XLA Ops:
  0.0 26.2 %copy-start = (s32[16,16,4]{1,2,0:T(4,128)S(1)}, s32[16,16,4]{1,2,0:T(4,128)}, u32[]{:S(2)}) copy-start(s32[16,16,4]{1,2,0:T(4,128)} %param.16) | copy-start | bytes 12292
  3.9 7.5 %collective-permute-start = (f32[2,128]{1,0:T(2,128)S(1)}, f32[2,128]{1,0:T(2,128)S(1)}, u32[]{:S(2)}, u32[]{:S(2)}) collective-permute-start(f32[2,128]{1,0:T(2,128)S(1)} %pad_maximum_fusion.2), channel_id=1, source_target_pairs={{0,16},{2,18},{4,20},{6,22},{8,24},{10,26},{12,28},{14,30},{16,0},... | collective-permute-start | bytes 3080 | tf_op jit(solution)/shard_map/cond/branch_1_fun/ppermute | solution.py:226
  11.4 7.5 %collective-permute-start.1 = (f32[2,2,128]{2,1,0:T(2,128)S(1)}, f32[2,2,128]{2,1,0:T(2,128)S(1)}, u32[]{:S(2)}, u32[]{:S(2)}) collective-permute-start(f32[2,2,128]{2,1,0:T(2,128)S(1)} %pad_maximum_fusion.1), channel_id=1, source_target_pairs={{0,24},{2,26},{4,28},{6,30},{8,16},{10,18},{12,20},{14,22},{16,8},... | collective-permute-start | bytes 6152 | tf_op jit(solution)/shard_map/cond/branch_1_fun/ppermute | solution.py:226
  19.0 7.4 %copy-start.1 = (bf16[128,2048]{1,0:T(8,128)(2,1)S(1)}, bf16[128,2048]{1,0:T(8,128)(2,1)}, u32[]{:S(2)}) copy-start(bf16[128,2048]{1,0:T(8,128)(2,1)} %query_hbm.1) | copy-start | bytes 1572868
  19.0 7.4 %copy-start.2 = (bf16[128,2048]{1,0:T(8,128)(2,1)S(1)}, bf16[128,2048]{1,0:T(8,128)(2,1)}, u32[]{:S(2)}) copy-start(bf16[128,2048]{1,0:T(8,128)(2,1)} %key_hbm.1) | copy-start | bytes 1572868
  19.0 28.6 %all-to-all-start = ((bf16[16,3,128,128]{3,2,1,0:T(8,128)(2,1)}), bf16[16,3,128,128]{3,2,1,0:T(8,128)(2,1)S(1)}, u32[]{:S(2)}, u32[]{:S(2)}) async-start(bf16[16,3,128,128]{3,2,1,0:T(8,128)(2,1)} %pack_heads.1), calls=%async_computation | async-start | bytes 3145728 | tf_op jit(solution)/shard_map/all_to_all | solution.py:267
  26.2 18.7 %copy-start.3 = (f32[2048]{0:T(1024)S(1)}, f32[2048]{0:T(1024)}, u32[]{:S(2)}) copy-start(f32[2048]{0:T(1024)} %param.15) | copy-start | bytes 24580
  26.2 18.7 %copy-start.4 = (f32[2048]{0:T(1024)S(1)}, f32[2048]{0:T(1024)}, u32[]{:S(2)}) copy-start(f32[2048]{0:T(1024)} %param.14) | copy-start | bytes 24580
  26.4 7.8 %collective-permute-start.6 = (f32[4,2,128]{2,1,0:T(2,128)S(1)}, f32[4,2,128]{2,1,0:T(2,128)S(1)}, u32[]{:S(2)}, u32[]{:S(2)}) collective-permute-start(f32[4,2,128]{2,1,0:T(2,128)S(1)} %param.3), channel_id=1, source_target_pairs={{0,4},{2,6},{4,0},{6,2},{8,12},{10,14},{12,8},{14,10},{16,20},{18,... | collective-permute-start | bytes 12296 | tf_op jit(solution)/shard_map/cond/branch_1_fun/ppermute | solution.py:226
  34.3 6.3 %collective-permute-start.7 = (f32[4,2,2,128]{3,2,0,1:T(2,128)S(1)}, f32[4,2,2,128]{3,2,0,1:T(2,128)S(1)}, u32[]{:S(2)}, u32[]{:S(2)}) collective-permute-start(f32[4,2,2,128]{3,2,0,1:T(2,128)S(1)} %pad_maximum_fusion.9), channel_id=1, source_target_pairs={{0,2},{2,0},{4,6},{6,4},{8,10},{10,8},{12,14},{14,12},{16,18},{18,... | collective-permute-start | bytes 24584 | tf_op jit(solution)/shard_map/cond/branch_1_fun/ppermute | solution.py:226

commit v8 on v7

--- a/solution.py
+++ b/solution.py
@@ -285,7 +285,7 @@
         return held
 
     held = lax.cond(first_half, rest_of_first, all_of_second, early, query_proj, key_proj)
-    squares = lax.psum(held, "tp")
+    squares = held + lax.ppermute(held, "tp", [(0, 1), (1, 0)])
     factors = lax.rsqrt(squares / full_width + epsilon)
     tile_count = device_count * tokens_here // TILE
     factors = factors.transpose(1, 0, 2).reshape(2 * tile_count, TILE)

time: 68 us -> 67.8 us (level)
  blocking collectives: 20.1 us -> 16.6 us
  waiting for transfers between devices: 13 us -> 16.3 us
    psum x1 -> x0, blocking collectives: 3.36 us -> none  [local(): squares = lax.psum(held, 'tp')]
    all_to_all x1, waiting for transfers between devices: 2.75 us -> 5.65 us  [local(): lax.all_to_all(outgoing, 'seq', split_axis=0, concat_axis=0, tiled=True)]
  transfers between devices with their start and end apart: 5 -> 6, of which waited for: 5 -> 6; matrix products, arithmetic and copies ran while one was open for 2% -> 2% of each run, Pallas kernels for 0% -> 0%
where the time goes in v8:
time: 67.8 us; the launch traced here: 67.4 us
  starting transfers between devices  26.1 us (38%)
  blocking collectives  16.6 us (24%)
  waiting for transfers between devices  16.3 us (24%)
  Pallas kernels  4.67 us (7%)
  local copies, waits for them, and re-layouts  1.8 us (3%)
  other arithmetic  1.66 us (2%)
    ppermute x4, starting transfers between devices, swapped(): return lax.ppermute(held, ('seq', 'tp'), pairs)  18.9 us
    all_to_all x1, blocking collectives, local(): lax.all_to_all(results, 'seq', split_axis=0, concat_axis=0, tiled=True)  16.6 us
    ppermute x4, waiting for transfers between devices, swapped(): return lax.ppermute(held, ('seq', 'tp'), pairs)  10.5 us
    all_to_all x1, starting transfers between devices, local(): lax.all_to_all(outgoing, 'seq', split_axis=0, concat_axis=0, tiled=True)  7.19 us
    all_to_all x1, waiting for transfers between devices, local(): lax.all_to_all(outgoing, 'seq', split_axis=0, concat_axis=0, tiled=True)  5.65 us
    pallas_call x1, Pallas kernels, pack(): pl.pallas_call(pack_kernel, out_shape=jax.ShapeDtypeStruct(shape, query.d...  2.34 us
    pallas_call x1, Pallas kernels, attend(): pl.pallas_call(functools.partial(attend_kernel, most_live), out_shape=jax...  2.32 us
    reduce_sum x1, other arithmetic, squares_of(): jnp.sum(key * key, axis=1)  1.49 us
  transfers between devices with their start and end apart: 6, of which 6 were waited for; matrix products, arithmetic and copies ran while one was open for 2% of the time, Pallas kernels for 0%

profile of v8, /device:TPU:0, one launch (start us, length us, event | category | flops | bytes accessed | tf_op | source)
XLA Modules:
  0.0 67.4 jit_solution(16096660018744959541)
XLA Ops:
  0.0 0.0 copy-start
  0.0 2.3 %pack_heads.1 = bf16[16,3,128,128]{3,2,1,0:T(8,128)(2,1)} custom-call(bf16[128,2048]{1,0:T(8,128)(2,1)} %query_hbm.1, bf16[128,2048]{1,0:T(8,128)(2,1)} %key_hbm.1, bf16[128,2048]{1,0:T(8,128)(2,1)} %value_hbm.1), custom_call_target="tpu_custom_call" | custom-call | tf_op jit(solution)/shard_map/pack_heads/pallas_call | solution.py:52
  2.4 16.6 %conditional.2 = (f32[4,2,128]{2,1,0:T(2,128)S(1)}) conditional(s32[]{:T(128)} %convert_element_type.18, () %tuple.19, (bf16[128,2048]{1,0:T(8,128)(2,1)}, bf16[128,2048]{1,0:T(8,128)(2,1)}) %tuple.20), branch_computations={%region_0.1_spmd, %region_1.4_spmd} | conditional | flops 1576711 | bytes 1096868 | solution.py:263
  2.4 1.5 %multiply_reduce_fusion = (f32[128]{0:T(128)S(1)}, f32[128]{0:T(128)S(1)}) fusion(bf16[128,2048]{1,0:T(8,128)(2,1)} %get-tuple-element.23, bf16[128,2048]{1,0:T(8,128)(2,1)} %get-tuple-element.22), kind=kLoop, calls=%fused_computation | loop fusion | flops 1572608 | bytes 1049600 | tf_op jit(solution)/shard_map/cond/branch_1_fun/reduce_sum | solution.py:220
  3.9 5.9 %collective-permute-start = (f32[2,128]{1,0:T(2,128)S(1)}, f32[2,128]{1,0:T(2,128)S(1)}, u32[]{:S(2)}, u32[]{:S(2)}) collective-permute-start(f32[2,128]{1,0:T(2,128)S(1)} %pad_maximum_fusion.2), channel_id=1, source_target_pairs={{0,16},{2,18},{4,20},{6,22},{8,24},{10,26},{12,28},{14,30},{16,0},... | collective-permute-start | bytes 3080 | tf_op jit(solution)/shard_map/cond/branch_1_fun/ppermute | solution.py:226
  9.8 1.5 %collective-permute-done = f32[2,128]{1,0:T(2,128)S(1)} collective-permute-done((f32[2,128]{1,0:T(2,128)S(1)}, f32[2,128]{1,0:T(2,128)S(1)}, u32[]{:S(2)}, u32[]{:S(2)}) %collective-permute-start) | collective-permute-done | bytes 1056 | tf_op jit(solution)/shard_map/cond/branch_1_fun/ppermute | solution.py:226
  11.4 5.8 %collective-permute-start.1 = (f32[2,2,128]{2,1,0:T(2,128)S(1)}, f32[2,2,128]{2,1,0:T(2,128)S(1)}, u32[]{:S(2)}, u32[]{:S(2)}) collective-permute-start(f32[2,2,128]{2,1,0:T(2,128)S(1)} %pad_maximum_fusion.1), channel_id=1, source_target_pairs={{0,24},{2,26},{4,28},{6,30},{8,16},{10,18},{12,20},{14,22},{16,8},... | collective-permute-start | bytes 6152 | tf_op jit(solution)/shard_map/cond/branch_1_fun/ppermute | solution.py:226
  17.2 1.7 %collective-permute-done.1 = f32[2,2,128]{2,1,0:T(2,128)S(1)} collective-permute-done((f32[2,2,128]{2,1,0:T(2,128)S(1)}, f32[2,2,128]{2,1,0:T(2,128)S(1)}, u32[]{:S(2)}, u32[]{:S(2)}) %collective-permute-start.1) | collective-permute-done | bytes 2080 | tf_op jit(solution)/shard_map/cond/branch_1_fun/ppermute | solution.py:226
  18.9 0.0 copy-start.1
  19.0 0.0 copy-start.2
  19.0 0.0 copy-start.3
  19.0 0.0 copy-start.4
  19.0 7.2 %all-to-all-start = ((bf16[16,3,128,128]{3,2,1,0:T(8,128)(2,1)}), bf16[16,3,128,128]{3,2,1,0:T(8,128)(2,1)S(1)}, u32[]{:S(2)}, u32[]{:S(2)}) async-start(bf16[16,3,128,128]{3,2,1,0:T(8,128)(2,1)} %pack_heads.1), calls=%async_computation | async-start | bytes 3145728 | tf_op jit(solution)/shard_map/all_to_all | solution.py:267
  26.2 0.0 copy-done.1
  26.2 0.0 copy-done.2
  26.2 14.5 %conditional.3 = (f32[16,2,128]{2,1,0:T(2,128)S(1)}) conditional(s32[]{:T(128)} %convert_element_type.18, (s32[]{:T(128)}, bf16[128,2048]{1,0:T(8,128)(2,1)S(1)}, bf16[128,2048]{1,0:T(8,128)(2,1)S(1)}) %tuple.37, f32[4,2,128]{2,1,0:T(2,128)S(1)} %get-tuple-element.51), branch_computations={%region_4.7_spmd, %region_7.8_spmd} | conditional | flops 1591051 | bytes 1244448 | solution.py:287
  26.2 3.8 %collective-permute-start.6 = (f32[4,2,128]{2,1,0:T(2,128)S(1)}, f32[4,2,128]{2,1,0:T(2,128)S(1)}, u32[]{:S(2)}, u32[]{:S(2)}) collective-permute-start(f32[4,2,128]{2,1,0:T(2,128)S(1)} %param.3), channel_id=1, source_target_pairs={{0,4},{2,6},{4,0},{6,2},{8,12},{10,14},{12,8},{14,10},{16,20},{18,... | collective-permute-start | bytes 12296 | tf_op jit(solution)/shard_map/cond/branch_1_fun/ppermute | solution.py:226
  30.1 4.2 %collective-permute-done.6 = f32[4,2,128]{2,1,0:T(2,128)S(1)} collective-permute-done((f32[4,2,128]{2,1,0:T(2,128)S(1)}, f32[4,2,128]{2,1,0:T(2,128)S(1)}, u32[]{:S(2)}, u32[]{:S(2)}) %collective-permute-start.6) | collective-permute-done | bytes 4128 | tf_op jit(solution)/shard_map/cond/branch_1_fun/ppermute | solution.py:226
  34.3 3.3 %collective-permute-start.7 = (f32[4,2,2,128]{3,2,0,1:T(2,128)S(1)}, f32[4,2,2,128]{3,2,0,1:T(2,128)S(1)}, u32[]{:S(2)}, u32[]{:S(2)}) collective-permute-start(f32[4,2,2,128]{3,2,0,1:T(2,128)S(1)} %pad_maximum_fusion.9), channel_id=1, source_target_pairs={{0,2},{2,0},{4,6},{6,4},{8,10},{10,8},{12,14},{14,12},{16,18},{18,... | collective-permute-start | bytes 24584 | tf_op jit(solution)/shard_map/cond/branch_1_fun/ppermute | solution.py:226
  37.6 3.1 %collective-permute-done.7 = f32[4,2,2,128]{3,2,0,1:T(2,128)S(1)} collective-permute-done((f32[4,2,2,128]{3,2,0,1:T(2,128)S(1)}, f32[4,2,2,128]{3,2,0,1:T(2,128)S(1)}, u32[]{:S(2)}, u32[]{:S(2)}) %collective-permute-start.7) | collective-permute-done | bytes 8224 | tf_op jit(solution)/shard_map/cond/branch_1_fun/ppermute | solution.py:226
  40.7 0.1 collective-permute-start.8
  40.8 0.7 %fusion.2 = s32[16]{0:T(128)S(1)} fusion(s32[16,16]{1,0:T(8,128)} %param.17, s32[]{:T(128)S(6)} %select_n.107), kind=kLoop, calls=%fused_computation.38 | loop fusion | bytes 132 | tf_op jit(solution)/shard_map/jit(dynamic_index_in_dim)/squeeze | solution.py:298
  41.5 0.0 copy-done.3
  41.5 0.0 copy-done.4
  41.5 0.1 pad_add_fusion.counts_hbm
  41.6 0.1 copy.15
  41.7 0.1 reshape.28.lists_hbm
  41.8 0.2 collective-permute-done.8
  42.0 5.7 %all-to-all-done.gathered_ref = bf16[16,3,128,128]{3,2,1,0:T(8,128)(2,1)S(1)} async-done(((bf16[16,3,128,128]{3,2,1,0:T(8,128)(2,1)}), bf16[16,3,128,128]{3,2,1,0:T(8,128)(2,1)S(1)}, u32[]{:S(2)}, u32[]{:S(2)}) %all-to-all-start) | async-done | bytes 1572896 | tf_op jit(solution)/shard_map/all_to_all | solution.py:267
  47.6 2.3 %attend.1 = bf16[16,128,128]{2,1,0:T(8,128)(2,1)S(1)} custom-call(s32[64]{0:T(128)S(1)} %reshape.28.lists_hbm, s32[17]{0:T(128)S(1)} %pad_add_fusion.counts_hbm, f32[128,128]{1,0:T(8,128)S(1)} %pad.4.factors_ref, f32[2,128]{1,0:T(2,128)S(1)} %fusion.1.gains_ref, bf16[16,3,128,128]{3,2,1,0:T(8,128)(2,1)S(1)} %all-to-all-done.gathered_ref), custom_call_target="tpu_custom_call" | custom-call | tf_op jit(solution)/shard_map/attend/pallas_call | solution.py:197
  50.0 16.6 %all_to_all.10 = bf16[16,128,128]{2,1,0:T(8,128)(2,1)S(1)} all-to-all(bf16[16,128,128]{2,1,0:T(8,128)(2,1)S(1)} %attend.1), channel_id=1, replica_groups=mesh['seq'=16,'tp'=2] {'seq'}, dimensions={0} | all-to-all | bytes 1048576 | tf_op jit(solution)/shard_map/all_to_all | solution.py:308
  66.6 0.9 %copy_bitcast_fusion = bf16[128,2048]{1,0:T(8,128)(2,1)} fusion(bf16[16,128,128]{2,1,0:T(8,128)(2,1)S(1)} %all_to_all.10), kind=kLoop, calls=%fused_computation.30 | loop fusion | bytes 1048576 | tf_op jit(solution)/shard_map/reshape | solution.py:313
  (17 shorter events, 0.1 us)
Async XLA Ops:
  0.0 41.5 %copy-start = (s32[16,16,4]{1,2,0:T(4,128)S(1)}, s32[16,16,4]{1,2,0:T(4,128)}, u32[]{:S(2)}) copy-start(s32[16,16,4]{1,2,0:T(4,128)} %param.16) | copy-start | bytes 12292
  3.9 7.5 %collective-permute-start = (f32[2,128]{1,0:T(2,128)S(1)}, f32[2,128]{1,0:T(2,128)S(1)}, u32[]{:S(2)}, u32[]{:S(2)}) collective-permute-start(f32[2,128]{1,0:T(2,128)S(1)} %pad_maximum_fusion.2), channel_id=1, source_target_pairs={{0,16},{2,18},{4,20},{6,22},{8,24},{10,26},{12,28},{14,30},{16,0},... | collective-permute-start | bytes 3080 | tf_op jit(solution)/shard_map/cond/branch_1_fun/ppermute | solution.py:226
  11.4 7.5 %collective-permute-start.1 = (f32[2,2,128]{2,1,0:T(2,128)S(1)}, f32[2,2,128]{2,1,0:T(2,128)S(1)}, u32[]{:S(2)}, u32[]{:S(2)}) collective-permute-start(f32[2,2,128]{2,1,0:T(2,128)S(1)} %pad_maximum_fusion.1), channel_id=1, source_target_pairs={{0,24},{2,26},{4,28},{6,30},{8,16},{10,18},{12,20},{14,22},{16,8},... | collective-permute-start | bytes 6152 | tf_op jit(solution)/shard_map/cond/branch_1_fun/ppermute | solution.py:226
  18.9 7.3 %copy-start.1 = (bf16[128,2048]{1,0:T(8,128)(2,1)S(1)}, bf16[128,2048]{1,0:T(8,128)(2,1)}, u32[]{:S(2)}) copy-start(bf16[128,2048]{1,0:T(8,128)(2,1)} %query_hbm.1) | copy-start | bytes 1572868
  19.0 7.3 %copy-start.2 = (bf16[128,2048]{1,0:T(8,128)(2,1)S(1)}, bf16[128,2048]{1,0:T(8,128)(2,1)}, u32[]{:S(2)}) copy-start(bf16[128,2048]{1,0:T(8,128)(2,1)} %key_hbm.1) | copy-start | bytes 1572868
  19.0 22.5 %copy-start.3 = (f32[2048]{0:T(1024)S(1)}, f32[2048]{0:T(1024)}, u32[]{:S(2)}) copy-start(f32[2048]{0:T(1024)} %param.15) | copy-start | bytes 24580
  19.0 22.5 %copy-start.4 = (f32[2048]{0:T(1024)S(1)}, f32[2048]{0:T(1024)}, u32[]{:S(2)}) copy-start(f32[2048]{0:T(1024)} %param.14) | copy-start | bytes 24580
  19.0 28.6 %all-to-all-start = ((bf16[16,3,128,128]{3,2,1,0:T(8,128)(2,1)}), bf16[16,3,128,128]{3,2,1,0:T(8,128)(2,1)S(1)}, u32[]{:S(2)}, u32[]{:S(2)}) async-start(bf16[16,3,128,128]{3,2,1,0:T(8,128)(2,1)} %pack_heads.1), calls=%async_computation | async-start | bytes 3145728 | tf_op jit(solution)/shard_map/all_to_all | solution.py:267
  26.2 8.0 %collective-permute-start.6 = (f32[4,2,128]{2,1,0:T(2,128)S(1)}, f32[4,2,128]{2,1,0:T(2,128)S(1)}, u32[]{:S(2)}, u32[]{:S(2)}) collective-permute-start(f32[4,2,128]{2,1,0:T(2,128)S(1)} %param.3), channel_id=1, source_target_pairs={{0,4},{2,6},{4,0},{6,2},{8,12},{10,14},{12,8},{14,10},{16,20},{18,... | collective-permute-start | bytes 12296 | tf_op jit(solution)/shard_map/cond/branch_1_fun/ppermute | solution.py:226
  34.3 6.3 %collective-permute-start.7 = (f32[4,2,2,128]{3,2,0,1:T(2,128)S(1)}, f32[4,2,2,128]{3,2,0,1:T(2,128)S(1)}, u32[]{:S(2)}, u32[]{:S(2)}) collective-permute-start(f32[4,2,2,128]{3,2,0,1:T(2,128)S(1)} %pad_maximum_fusion.9), channel_id=1, source_target_pairs={{0,2},{2,0},{4,6},{6,4},{8,10},{10,8},{12,14},{14,12},{16,18},{18,... | collective-permute-start | bytes 24584 | tf_op jit(solution)/shard_map/cond/branch_1_fun/ppermute | solution.py:226
  40.7 1.2 %collective-permute-start.8 = (f32[16,2,128]{2,1,0:T(2,128)S(1)}, f32[16,2,128]{2,1,0:T(2,128)S(1)}, u32[]{:S(2)}, u32[]{:S(2)}) collective-permute-start(f32[16,2,128]{2,1,0:T(2,128)S(1)} %get-tuple-element.52), channel_id=1, source_target_pairs={{0,1},{1,0},{2,3},{3,2},{4,5},{5,4},{6,7},{7,6},{8,9},{9,8},{10,11... | collective-permute-start | bytes 49160 | tf_op jit(solution)/shard_map/ppermute | solution.py:288

commit v9 on v8

--- a/solution.py
+++ b/solution.py
@@ -145,8 +145,10 @@
             (((1,), (1,)), ((), ())),
             preferred_element_type=jnp.float32,
         )
-        slot = lax.broadcasted_iota(jnp.int32, (1, most_live * TILE), 1) // TILE
-        score = jnp.where(slot < counts[step], score, -jnp.inf)
+        slots = [score[:, slot * TILE : (slot + 1) * TILE] for slot in range(most_live)]
+        for slot in range(1, most_live):
+            slots[slot] = jnp.where(slot < counts[step], slots[slot], -jnp.inf)
+        score = jnp.concatenate(slots, axis=1)
         scores[place] = score
         largest = jnp.max(score, axis=1, keepdims=True)
         rows_kept[place] = jnp.broadcast_to(largest, (TILE, LANES))

time: 67.8 us -> 67.8 us (level)
  no operation moved by 1% of the time
where the time goes in v9:
time: 67.8 us; the launch traced here: 67.4 us
  starting transfers between devices  26.1 us (38%)
  blocking collectives  16.6 us (24%)
  waiting for transfers between devices  16.3 us (24%)
  Pallas kernels  4.64 us (7%)
  local copies, waits for them, and re-layouts  1.8 us (3%)
  other arithmetic  1.66 us (2%)
    ppermute x4, starting transfers between devices, swapped(): return lax.ppermute(held, ('seq', 'tp'), pairs)  18.9 us
    all_to_all x1, blocking collectives, local(): lax.all_to_all(results, 'seq', split_axis=0, concat_axis=0, tiled=True)  16.6 us
    ppermute x4, waiting for transfers between devices, swapped(): return lax.ppermute(held, ('seq', 'tp'), pairs)  10.5 us
    all_to_all x1, starting transfers between devices, local(): lax.all_to_all(outgoing, 'seq', split_axis=0, concat_axis=0, tiled=True)  7.19 us
    all_to_all x1, waiting for transfers between devices, local(): lax.all_to_all(outgoing, 'seq', split_axis=0, concat_axis=0, tiled=True)  5.65 us
    pallas_call x1, Pallas kernels, pack(): pl.pallas_call(pack_kernel, out_shape=jax.ShapeDtypeStruct(shape, query.d...  2.34 us
    pallas_call x1, Pallas kernels, attend(): pl.pallas_call(functools.partial(attend_kernel, most_live), out_shape=jax...  2.29 us
    reduce_sum x1, other arithmetic, squares_of(): jnp.sum(key * key, axis=1)  1.49 us
  transfers between devices with their start and end apart: 6, of which 6 were waited for; matrix products, arithmetic and copies ran while one was open for 2% of the time, Pallas kernels for 0%

profile of v9, /device:TPU:0, one launch (start us, length us, event | category | flops | bytes accessed | tf_op | source)
XLA Modules:
  0.0 67.4 jit_solution(14939947466943327552)
XLA Ops:
  0.0 0.0 copy-start
  0.0 2.3 %pack_heads.1 = bf16[16,3,128,128]{3,2,1,0:T(8,128)(2,1)} custom-call(bf16[128,2048]{1,0:T(8,128)(2,1)} %query_hbm.1, bf16[128,2048]{1,0:T(8,128)(2,1)} %key_hbm.1, bf16[128,2048]{1,0:T(8,128)(2,1)} %value_hbm.1), custom_call_target="tpu_custom_call" | custom-call | tf_op jit(solution)/shard_map/pack_heads/pallas_call | solution.py:52
  2.4 16.6 %conditional.2 = (f32[4,2,128]{2,1,0:T(2,128)S(1)}) conditional(s32[]{:T(128)} %convert_element_type.18, () %tuple.19, (bf16[128,2048]{1,0:T(8,128)(2,1)}, bf16[128,2048]{1,0:T(8,128)(2,1)}) %tuple.20), branch_computations={%region_0.1_spmd, %region_1.4_spmd} | conditional | flops 1576711 | bytes 1096868 | solution.py:265
  2.4 1.5 %multiply_reduce_fusion = (f32[128]{0:T(128)S(1)}, f32[128]{0:T(128)S(1)}) fusion(bf16[128,2048]{1,0:T(8,128)(2,1)} %get-tuple-element.23, bf16[128,2048]{1,0:T(8,128)(2,1)} %get-tuple-element.22), kind=kLoop, calls=%fused_computation | loop fusion | flops 1572608 | bytes 1049600 | tf_op jit(solution)/shard_map/cond/branch_1_fun/reduce_sum | solution.py:222
  3.9 5.9 %collective-permute-start = (f32[2,128]{1,0:T(2,128)S(1)}, f32[2,128]{1,0:T(2,128)S(1)}, u32[]{:S(2)}, u32[]{:S(2)}) collective-permute-start(f32[2,128]{1,0:T(2,128)S(1)} %pad_maximum_fusion.2), channel_id=1, source_target_pairs={{0,16},{2,18},{4,20},{6,22},{8,24},{10,26},{12,28},{14,30},{16,0},... | collective-permute-start | bytes 3080 | tf_op jit(solution)/shard_map/cond/branch_1_fun/ppermute | solution.py:228
  9.8 1.5 %collective-permute-done = f32[2,128]{1,0:T(2,128)S(1)} collective-permute-done((f32[2,128]{1,0:T(2,128)S(1)}, f32[2,128]{1,0:T(2,128)S(1)}, u32[]{:S(2)}, u32[]{:S(2)}) %collective-permute-start) | collective-permute-done | bytes 1056 | tf_op jit(solution)/shard_map/cond/branch_1_fun/ppermute | solution.py:228
  11.4 5.8 %collective-permute-start.1 = (f32[2,2,128]{2,1,0:T(2,128)S(1)}, f32[2,2,128]{2,1,0:T(2,128)S(1)}, u32[]{:S(2)}, u32[]{:S(2)}) collective-permute-start(f32[2,2,128]{2,1,0:T(2,128)S(1)} %pad_maximum_fusion.1), channel_id=1, source_target_pairs={{0,24},{2,26},{4,28},{6,30},{8,16},{10,18},{12,20},{14,22},{16,8},... | collective-permute-start | bytes 6152 | tf_op jit(solution)/shard_map/cond/branch_1_fun/ppermute | solution.py:228
  17.2 1.7 %collective-permute-done.1 = f32[2,2,128]{2,1,0:T(2,128)S(1)} collective-permute-done((f32[2,2,128]{2,1,0:T(2,128)S(1)}, f32[2,2,128]{2,1,0:T(2,128)S(1)}, u32[]{:S(2)}, u32[]{:S(2)}) %collective-permute-start.1) | collective-permute-done | bytes 2080 | tf_op jit(solution)/shard_map/cond/branch_1_fun/ppermute | solution.py:228
  18.9 0.0 copy-start.1
  19.0 0.0 copy-start.2
  19.0 0.0 copy-start.3
  19.0 0.0 copy-start.4
  19.0 7.2 %all-to-all-start = ((bf16[16,3,128,128]{3,2,1,0:T(8,128)(2,1)}), bf16[16,3,128,128]{3,2,1,0:T(8,128)(2,1)S(1)}, u32[]{:S(2)}, u32[]{:S(2)}) async-start(bf16[16,3,128,128]{3,2,1,0:T(8,128)(2,1)} %pack_heads.1), calls=%async_computation | async-start | bytes 3145728 | tf_op jit(solution)/shard_map/all_to_all | solution.py:269
  26.2 0.0 copy-done.1
  26.2 0.0 copy-done.2
  26.2 14.5 %conditional.3 = (f32[16,2,128]{2,1,0:T(2,128)S(1)}) conditional(s32[]{:T(128)} %convert_element_type.18, (s32[]{:T(128)}, bf16[128,2048]{1,0:T(8,128)(2,1)S(1)}, bf16[128,2048]{1,0:T(8,128)(2,1)S(1)}) %tuple.37, f32[4,2,128]{2,1,0:T(2,128)S(1)} %get-tuple-element.51), branch_computations={%region_4.7_spmd, %region_7.8_spmd} | conditional | flops 1591051 | bytes 1244448 | solution.py:289
  26.2 3.8 %collective-permute-start.6 = (f32[4,2,128]{2,1,0:T(2,128)S(1)}, f32[4,2,128]{2,1,0:T(2,128)S(1)}, u32[]{:S(2)}, u32[]{:S(2)}) collective-permute-start(f32[4,2,128]{2,1,0:T(2,128)S(1)} %param.3), channel_id=1, source_target_pairs={{0,4},{2,6},{4,0},{6,2},{8,12},{10,14},{12,8},{14,10},{16,20},{18,... | collective-permute-start | bytes 12296 | tf_op jit(solution)/shard_map/cond/branch_1_fun/ppermute | solution.py:228
  30.1 4.2 %collective-permute-done.6 = f32[4,2,128]{2,1,0:T(2,128)S(1)} collective-permute-done((f32[4,2,128]{2,1,0:T(2,128)S(1)}, f32[4,2,128]{2,1,0:T(2,128)S(1)}, u32[]{:S(2)}, u32[]{:S(2)}) %collective-permute-start.6) | collective-permute-done | bytes 4128 | tf_op jit(solution)/shard_map/cond/branch_1_fun/ppermute | solution.py:228
  34.3 3.3 %collective-permute-start.7 = (f32[4,2,2,128]{3,2,0,1:T(2,128)S(1)}, f32[4,2,2,128]{3,2,0,1:T(2,128)S(1)}, u32[]{:S(2)}, u32[]{:S(2)}) collective-permute-start(f32[4,2,2,128]{3,2,0,1:T(2,128)S(1)} %pad_maximum_fusion.9), channel_id=1, source_target_pairs={{0,2},{2,0},{4,6},{6,4},{8,10},{10,8},{12,14},{14,12},{16,18},{18,... | collective-permute-start | bytes 24584 | tf_op jit(solution)/shard_map/cond/branch_1_fun/ppermute | solution.py:228
  37.6 3.1 %collective-permute-done.7 = f32[4,2,2,128]{3,2,0,1:T(2,128)S(1)} collective-permute-done((f32[4,2,2,128]{3,2,0,1:T(2,128)S(1)}, f32[4,2,2,128]{3,2,0,1:T(2,128)S(1)}, u32[]{:S(2)}, u32[]{:S(2)}) %collective-permute-start.7) | collective-permute-done | bytes 8224 | tf_op jit(solution)/shard_map/cond/branch_1_fun/ppermute | solution.py:228
  40.7 0.1 collective-permute-start.8
  40.8 0.7 %fusion.2 = s32[16]{0:T(128)S(1)} fusion(s32[16,16]{1,0:T(8,128)} %param.17, s32[]{:T(128)S(6)} %select_n.107), kind=kLoop, calls=%fused_computation.38 | loop fusion | bytes 132 | tf_op jit(solution)/shard_map/jit(dynamic_index_in_dim)/squeeze | solution.py:300
  41.5 0.0 copy-done.3
  41.5 0.0 copy-done.4
  41.5 0.1 pad_add_fusion.counts_hbm
  41.6 0.1 copy.15
  41.7 0.1 reshape.28.lists_hbm
  41.8 0.2 collective-permute-done.8
  42.0 5.7 %all-to-all-done.gathered_ref = bf16[16,3,128,128]{3,2,1,0:T(8,128)(2,1)S(1)} async-done(((bf16[16,3,128,128]{3,2,1,0:T(8,128)(2,1)}), bf16[16,3,128,128]{3,2,1,0:T(8,128)(2,1)S(1)}, u32[]{:S(2)}, u32[]{:S(2)}) %all-to-all-start) | async-done | bytes 1572896 | tf_op jit(solution)/shard_map/all_to_all | solution.py:269
  47.6 2.3 %attend.1 = bf16[16,128,128]{2,1,0:T(8,128)(2,1)S(1)} custom-call(s32[64]{0:T(128)S(1)} %reshape.28.lists_hbm, s32[17]{0:T(128)S(1)} %pad_add_fusion.counts_hbm, f32[128,128]{1,0:T(8,128)S(1)} %pad.4.factors_ref, f32[2,128]{1,0:T(2,128)S(1)} %fusion.1.gains_ref, bf16[16,3,128,128]{3,2,1,0:T(8,128)(2,1)S(1)} %all-to-all-done.gathered_ref), custom_call_target="tpu_custom_call" | custom-call | tf_op jit(solution)/shard_map/attend/pallas_call | solution.py:199
  49.9 16.6 %all_to_all.10 = bf16[16,128,128]{2,1,0:T(8,128)(2,1)S(1)} all-to-all(bf16[16,128,128]{2,1,0:T(8,128)(2,1)S(1)} %attend.1), channel_id=1, replica_groups=mesh['seq'=16,'tp'=2] {'seq'}, dimensions={0} | all-to-all | bytes 1048576 | tf_op jit(solution)/shard_map/all_to_all | solution.py:310
  66.5 0.9 %copy_bitcast_fusion = bf16[128,2048]{1,0:T(8,128)(2,1)} fusion(bf16[16,128,128]{2,1,0:T(8,128)(2,1)S(1)} %all_to_all.10), kind=kLoop, calls=%fused_computation.30 | loop fusion | bytes 1048576 | tf_op jit(solution)/shard_map/reshape | solution.py:315
  (17 shorter events, 0.1 us)
Async XLA Ops:
  0.0 41.5 %copy-start = (s32[16,16,4]{1,2,0:T(4,128)S(1)}, s32[16,16,4]{1,2,0:T(4,128)}, u32[]{:S(2)}) copy-start(s32[16,16,4]{1,2,0:T(4,128)} %param.16) | copy-start | bytes 12292
  3.9 7.5 %collective-permute-start = (f32[2,128]{1,0:T(2,128)S(1)}, f32[2,128]{1,0:T(2,128)S(1)}, u32[]{:S(2)}, u32[]{:S(2)}) collective-permute-start(f32[2,128]{1,0:T(2,128)S(1)} %pad_maximum_fusion.2), channel_id=1, source_target_pairs={{0,16},{2,18},{4,20},{6,22},{8,24},{10,26},{12,28},{14,30},{16,0},... | collective-permute-start | bytes 3080 | tf_op jit(solution)/shard_map/cond/branch_1_fun/ppermute | solution.py:228
  11.4 7.5 %collective-permute-start.1 = (f32[2,2,128]{2,1,0:T(2,128)S(1)}, f32[2,2,128]{2,1,0:T(2,128)S(1)}, u32[]{:S(2)}, u32[]{:S(2)}) collective-permute-start(f32[2,2,128]{2,1,0:T(2,128)S(1)} %pad_maximum_fusion.1), channel_id=1, source_target_pairs={{0,24},{2,26},{4,28},{6,30},{8,16},{10,18},{12,20},{14,22},{16,8},... | collective-permute-start | bytes 6152 | tf_op jit(solution)/shard_map/cond/branch_1_fun/ppermute | solution.py:228
  18.9 7.3 %copy-start.1 = (bf16[128,2048]{1,0:T(8,128)(2,1)S(1)}, bf16[128,2048]{1,0:T(8,128)(2,1)}, u32[]{:S(2)}) copy-start(bf16[128,2048]{1,0:T(8,128)(2,1)} %query_hbm.1) | copy-start | bytes 1572868
  19.0 7.3 %copy-start.2 = (bf16[128,2048]{1,0:T(8,128)(2,1)S(1)}, bf16[128,2048]{1,0:T(8,128)(2,1)}, u32[]{:S(2)}) copy-start(bf16[128,2048]{1,0:T(8,128)(2,1)} %key_hbm.1) | copy-start | bytes 1572868
  19.0 22.5 %copy-start.3 = (f32[2048]{0:T(1024)S(1)}, f32[2048]{0:T(1024)}, u32[]{:S(2)}) copy-start(f32[2048]{0:T(1024)} %param.15) | copy-start | bytes 24580
  19.0 22.5 %copy-start.4 = (f32[2048]{0:T(1024)S(1)}, f32[2048]{0:T(1024)}, u32[]{:S(2)}) copy-start(f32[2048]{0:T(1024)} %param.14) | copy-start | bytes 24580
  19.0 28.6 %all-to-all-start = ((bf16[16,3,128,128]{3,2,1,0:T(8,128)(2,1)}), bf16[16,3,128,128]{3,2,1,0:T(8,128)(2,1)S(1)}, u32[]{:S(2)}, u32[]{:S(2)}) async-start(bf16[16,3,128,128]{3,2,1,0:T(8,128)(2,1)} %pack_heads.1), calls=%async_computation | async-start | bytes 3145728 | tf_op jit(solution)/shard_map/all_to_all | solution.py:269
  26.2 8.0 %collective-permute-start.6 = (f32[4,2,128]{2,1,0:T(2,128)S(1)}, f32[4,2,128]{2,1,0:T(2,128)S(1)}, u32[]{:S(2)}, u32[]{:S(2)}) collective-permute-start(f32[4,2,128]{2,1,0:T(2,128)S(1)} %param.3), channel_id=1, source_target_pairs={{0,4},{2,6},{4,0},{6,2},{8,12},{10,14},{12,8},{14,10},{16,20},{18,... | collective-permute-start | bytes 12296 | tf_op jit(solution)/shard_map/cond/branch_1_fun/ppermute | solution.py:228
  34.3 6.3 %collective-permute-start.7 = (f32[4,2,2,128]{3,2,0,1:T(2,128)S(1)}, f32[4,2,2,128]{3,2,0,1:T(2,128)S(1)}, u32[]{:S(2)}, u32[]{:S(2)}) collective-permute-start(f32[4,2,2,128]{3,2,0,1:T(2,128)S(1)} %pad_maximum_fusion.9), channel_id=1, source_target_pairs={{0,2},{2,0},{4,6},{6,4},{8,10},{10,8},{12,14},{14,12},{16,18},{18,... | collective-permute-start | bytes 24584 | tf_op jit(solution)/shard_map/cond/branch_1_fun/ppermute | solution.py:228
  40.7 1.2 %collective-permute-start.8 = (f32[16,2,128]{2,1,0:T(2,128)S(1)}, f32[16,2,128]{2,1,0:T(2,128)S(1)}, u32[]{:S(2)}, u32[]{:S(2)}) collective-permute-start(f32[16,2,128]{2,1,0:T(2,128)S(1)} %get-tuple-element.52), channel_id=1, source_target_pairs={{0,1},{1,0},{2,3},{3,2},{4,5},{5,4},{6,7},{7,6},{8,9},{9,8},{10,11... | collective-permute-start | bytes 49160 | tf_op jit(solution)/shard_map/ppermute | solution.py:290

commit v10 on v9

--- a/solution.py
+++ b/solution.py
@@ -158,14 +158,14 @@
         weight = jnp.exp2((scores[place] - largest) * scale)
         weights[place] = weight.astype(jnp.bfloat16)
         denominators = jnp.sum(weight, axis=1, keepdims=True)
-        rows_kept[place] = jnp.broadcast_to(denominators, (TILE, LANES))
+        rows_kept[place] = jnp.broadcast_to(1.0 / denominators, (TILE, LANES))
 
     def value_tile(place, step):
         values = [part(live, 2) for live in live_of(step)]
         total = jnp.dot(
             weights[place], jnp.concatenate(values, axis=0), preferred_element_type=jnp.float32
         )
-        out_ref[step] = (total / rows_kept[place]).astype(out_ref.dtype)
+        out_ref[step] = (total * rows_kept[place]).astype(out_ref.dtype)
 
     def some_tiles(first):
         for turn in range(together + 2 * APART):

time: 67.8 us -> 67.8 us (level)
  no operation moved by 1% of the time
where the time goes in v10:
time: 67.8 us; the launch traced here: 67.4 us
  starting transfers between devices  26.1 us (38%)
  blocking collectives  16.6 us (24%)
  waiting for transfers between devices  16.3 us (24%)
  Pallas kernels  4.64 us (7%)
  local copies, waits for them, and re-layouts  1.8 us (3%)
  other arithmetic  1.66 us (2%)
    ppermute x4, starting transfers between devices, swapped(): return lax.ppermute(held, ('seq', 'tp'), pairs)  18.9 us
    all_to_all x1, blocking collectives, local(): lax.all_to_all(results, 'seq', split_axis=0, concat_axis=0, tiled=True)  16.6 us
    ppermute x4, waiting for transfers between devices, swapped(): return lax.ppermute(held, ('seq', 'tp'), pairs)  10.5 us
    all_to_all x1, starting transfers between devices, local(): lax.all_to_all(outgoing, 'seq', split_axis=0, concat_axis=0, tiled=True)  7.19 us
    all_to_all x1, waiting for transfers between devices, local(): lax.all_to_all(outgoing, 'seq', split_axis=0, concat_axis=0, tiled=True)  5.65 us
    pallas_call x1, Pallas kernels, pack(): pl.pallas_call(pack_kernel, out_shape=jax.ShapeDtypeStruct(shape, query.d...  2.34 us
    pallas_call x1, Pallas kernels, attend(): pl.pallas_call(functools.partial(attend_kernel, most_live), out_shape=jax...  2.29 us
    reduce_sum x1, other arithmetic, squares_of(): jnp.sum(key * key, axis=1)  1.49 us
  transfers between devices with their start and end apart: 6, of which 6 were waited for; matrix products, arithmetic and copies ran while one was open for 2% of the time, Pallas kernels for 0%

profile of v10, /device:TPU:0, one launch (start us, length us, event | category | flops | bytes accessed | tf_op | source)
XLA Modules:
  0.0 67.4 jit_solution(14939947466943327552)
XLA Ops:
  0.0 0.0 copy-start
  0.0 2.3 %pack_heads.1 = bf16[16,3,128,128]{3,2,1,0:T(8,128)(2,1)} custom-call(bf16[128,2048]{1,0:T(8,128)(2,1)} %query_hbm.1, bf16[128,2048]{1,0:T(8,128)(2,1)} %key_hbm.1, bf16[128,2048]{1,0:T(8,128)(2,1)} %value_hbm.1), custom_call_target="tpu_custom_call" | custom-call | tf_op jit(solution)/shard_map/pack_heads/pallas_call | solution.py:52
  2.4 16.6 %conditional.2 = (f32[4,2,128]{2,1,0:T(2,128)S(1)}) conditional(s32[]{:T(128)} %convert_element_type.18, () %tuple.19, (bf16[128,2048]{1,0:T(8,128)(2,1)}, bf16[128,2048]{1,0:T(8,128)(2,1)}) %tuple.20), branch_computations={%region_0.1_spmd, %region_1.4_spmd} | conditional | flops 1576711 | bytes 1096868 | solution.py:265
  2.4 1.5 %multiply_reduce_fusion = (f32[128]{0:T(128)S(1)}, f32[128]{0:T(128)S(1)}) fusion(bf16[128,2048]{1,0:T(8,128)(2,1)} %get-tuple-element.23, bf16[128,2048]{1,0:T(8,128)(2,1)} %get-tuple-element.22), kind=kLoop, calls=%fused_computation | loop fusion | flops 1572608 | bytes 1049600 | tf_op jit(solution)/shard_map/cond/branch_1_fun/reduce_sum | solution.py:222
  3.9 5.9 %collective-permute-start = (f32[2,128]{1,0:T(2,128)S(1)}, f32[2,128]{1,0:T(2,128)S(1)}, u32[]{:S(2)}, u32[]{:S(2)}) collective-permute-start(f32[2,128]{1,0:T(2,128)S(1)} %pad_maximum_fusion.2), channel_id=1, source_target_pairs={{0,16},{2,18},{4,20},{6,22},{8,24},{10,26},{12,28},{14,30},{16,0},... | collective-permute-start | bytes 3080 | tf_op jit(solution)/shard_map/cond/branch_1_fun/ppermute | solution.py:228
  9.8 1.5 %collective-permute-done = f32[2,128]{1,0:T(2,128)S(1)} collective-permute-done((f32[2,128]{1,0:T(2,128)S(1)}, f32[2,128]{1,0:T(2,128)S(1)}, u32[]{:S(2)}, u32[]{:S(2)}) %collective-permute-start) | collective-permute-done | bytes 1056 | tf_op jit(solution)/shard_map/cond/branch_1_fun/ppermute | solution.py:228
  11.4 5.8 %collective-permute-start.1 = (f32[2,2,128]{2,1,0:T(2,128)S(1)}, f32[2,2,128]{2,1,0:T(2,128)S(1)}, u32[]{:S(2)}, u32[]{:S(2)}) collective-permute-start(f32[2,2,128]{2,1,0:T(2,128)S(1)} %pad_maximum_fusion.1), channel_id=1, source_target_pairs={{0,24},{2,26},{4,28},{6,30},{8,16},{10,18},{12,20},{14,22},{16,8},... | collective-permute-start | bytes 6152 | tf_op jit(solution)/shard_map/cond/branch_1_fun/ppermute | solution.py:228
  17.2 1.7 %collective-permute-done.1 = f32[2,2,128]{2,1,0:T(2,128)S(1)} collective-permute-done((f32[2,2,128]{2,1,0:T(2,128)S(1)}, f32[2,2,128]{2,1,0:T(2,128)S(1)}, u32[]{:S(2)}, u32[]{:S(2)}) %collective-permute-start.1) | collective-permute-done | bytes 2080 | tf_op jit(solution)/shard_map/cond/branch_1_fun/ppermute | solution.py:228
  18.9 0.0 copy-start.1
  19.0 0.0 copy-start.2
  19.0 0.0 copy-start.3
  19.0 0.0 copy-start.4
  19.0 7.2 %all-to-all-start = ((bf16[16,3,128,128]{3,2,1,0:T(8,128)(2,1)}), bf16[16,3,128,128]{3,2,1,0:T(8,128)(2,1)S(1)}, u32[]{:S(2)}, u32[]{:S(2)}) async-start(bf16[16,3,128,128]{3,2,1,0:T(8,128)(2,1)} %pack_heads.1), calls=%async_computation | async-start | bytes 3145728 | tf_op jit(solution)/shard_map/all_to_all | solution.py:269
  26.2 0.0 copy-done.1
  26.2 0.0 copy-done.2
  26.2 14.5 %conditional.3 = (f32[16,2,128]{2,1,0:T(2,128)S(1)}) conditional(s32[]{:T(128)} %convert_element_type.18, (s32[]{:T(128)}, bf16[128,2048]{1,0:T(8,128)(2,1)S(1)}, bf16[128,2048]{1,0:T(8,128)(2,1)S(1)}) %tuple.37, f32[4,2,128]{2,1,0:T(2,128)S(1)} %get-tuple-element.51), branch_computations={%region_4.7_spmd, %region_7.8_spmd} | conditional | flops 1591051 | bytes 1244448 | solution.py:289
  26.2 3.8 %collective-permute-start.6 = (f32[4,2,128]{2,1,0:T(2,128)S(1)}, f32[4,2,128]{2,1,0:T(2,128)S(1)}, u32[]{:S(2)}, u32[]{:S(2)}) collective-permute-start(f32[4,2,128]{2,1,0:T(2,128)S(1)} %param.3), channel_id=1, source_target_pairs={{0,4},{2,6},{4,0},{6,2},{8,12},{10,14},{12,8},{14,10},{16,20},{18,... | collective-permute-start | bytes 12296 | tf_op jit(solution)/shard_map/cond/branch_1_fun/ppermute | solution.py:228
  30.1 4.2 %collective-permute-done.6 = f32[4,2,128]{2,1,0:T(2,128)S(1)} collective-permute-done((f32[4,2,128]{2,1,0:T(2,128)S(1)}, f32[4,2,128]{2,1,0:T(2,128)S(1)}, u32[]{:S(2)}, u32[]{:S(2)}) %collective-permute-start.6) | collective-permute-done | bytes 4128 | tf_op jit(solution)/shard_map/cond/branch_1_fun/ppermute | solution.py:228
  34.3 3.3 %collective-permute-start.7 = (f32[4,2,2,128]{3,2,0,1:T(2,128)S(1)}, f32[4,2,2,128]{3,2,0,1:T(2,128)S(1)}, u32[]{:S(2)}, u32[]{:S(2)}) collective-permute-start(f32[4,2,2,128]{3,2,0,1:T(2,128)S(1)} %pad_maximum_fusion.9), channel_id=1, source_target_pairs={{0,2},{2,0},{4,6},{6,4},{8,10},{10,8},{12,14},{14,12},{16,18},{18,... | collective-permute-start | bytes 24584 | tf_op jit(solution)/shard_map/cond/branch_1_fun/ppermute | solution.py:228
  37.6 3.1 %collective-permute-done.7 = f32[4,2,2,128]{3,2,0,1:T(2,128)S(1)} collective-permute-done((f32[4,2,2,128]{3,2,0,1:T(2,128)S(1)}, f32[4,2,2,128]{3,2,0,1:T(2,128)S(1)}, u32[]{:S(2)}, u32[]{:S(2)}) %collective-permute-start.7) | collective-permute-done | bytes 8224 | tf_op jit(solution)/shard_map/cond/branch_1_fun/ppermute | solution.py:228
  40.7 0.1 collective-permute-start.8
  40.8 0.7 %fusion.2 = s32[16]{0:T(128)S(1)} fusion(s32[16,16]{1,0:T(8,128)} %param.17, s32[]{:T(128)S(6)} %select_n.107), kind=kLoop, calls=%fused_computation.38 | loop fusion | bytes 132 | tf_op jit(solution)/shard_map/jit(dynamic_index_in_dim)/squeeze | solution.py:300
  41.5 0.0 copy-done.3
  41.5 0.0 copy-done.4
  41.5 0.1 pad_add_fusion.counts_hbm
  41.6 0.1 copy.15
  41.7 0.1 reshape.28.lists_hbm
  41.8 0.2 collective-permute-done.8
  42.0 5.7 %all-to-all-done.gathered_ref = bf16[16,3,128,128]{3,2,1,0:T(8,128)(2,1)S(1)} async-done(((bf16[16,3,128,128]{3,2,1,0:T(8,128)(2,1)}), bf16[16,3,128,128]{3,2,1,0:T(8,128)(2,1)S(1)}, u32[]{:S(2)}, u32[]{:S(2)}) %all-to-all-start) | async-done | bytes 1572896 | tf_op jit(solution)/shard_map/all_to_all | solution.py:269
  47.6 2.3 %attend.1 = bf16[16,128,128]{2,1,0:T(8,128)(2,1)S(1)} custom-call(s32[64]{0:T(128)S(1)} %reshape.28.lists_hbm, s32[17]{0:T(128)S(1)} %pad_add_fusion.counts_hbm, f32[128,128]{1,0:T(8,128)S(1)} %pad.4.factors_ref, f32[2,128]{1,0:T(2,128)S(1)} %fusion.1.gains_ref, bf16[16,3,128,128]{3,2,1,0:T(8,128)(2,1)S(1)} %all-to-all-done.gathered_ref), custom_call_target="tpu_custom_call" | custom-call | tf_op jit(solution)/shard_map/attend/pallas_call | solution.py:199
  49.9 16.6 %all_to_all.10 = bf16[16,128,128]{2,1,0:T(8,128)(2,1)S(1)} all-to-all(bf16[16,128,128]{2,1,0:T(8,128)(2,1)S(1)} %attend.1), channel_id=1, replica_groups=mesh['seq'=16,'tp'=2] {'seq'}, dimensions={0} | all-to-all | bytes 1048576 | tf_op jit(solution)/shard_map/all_to_all | solution.py:310
  66.5 0.9 %copy_bitcast_fusion = bf16[128,2048]{1,0:T(8,128)(2,1)} fusion(bf16[16,128,128]{2,1,0:T(8,128)(2,1)S(1)} %all_to_all.10), kind=kLoop, calls=%fused_computation.30 | loop fusion | bytes 1048576 | tf_op jit(solution)/shard_map/reshape | solution.py:315
  (17 shorter events, 0.1 us)
Async XLA Ops:
  0.0 41.5 %copy-start = (s32[16,16,4]{1,2,0:T(4,128)S(1)}, s32[16,16,4]{1,2,0:T(4,128)}, u32[]{:S(2)}) copy-start(s32[16,16,4]{1,2,0:T(4,128)} %param.16) | copy-start | bytes 12292
  3.9 7.5 %collective-permute-start = (f32[2,128]{1,0:T(2,128)S(1)}, f32[2,128]{1,0:T(2,128)S(1)}, u32[]{:S(2)}, u32[]{:S(2)}) collective-permute-start(f32[2,128]{1,0:T(2,128)S(1)} %pad_maximum_fusion.2), channel_id=1, source_target_pairs={{0,16},{2,18},{4,20},{6,22},{8,24},{10,26},{12,28},{14,30},{16,0},... | collective-permute-start | bytes 3080 | tf_op jit(solution)/shard_map/cond/branch_1_fun/ppermute | solution.py:228
  11.4 7.5 %collective-permute-start.1 = (f32[2,2,128]{2,1,0:T(2,128)S(1)}, f32[2,2,128]{2,1,0:T(2,128)S(1)}, u32[]{:S(2)}, u32[]{:S(2)}) collective-permute-start(f32[2,2,128]{2,1,0:T(2,128)S(1)} %pad_maximum_fusion.1), channel_id=1, source_target_pairs={{0,24},{2,26},{4,28},{6,30},{8,16},{10,18},{12,20},{14,22},{16,8},... | collective-permute-start | bytes 6152 | tf_op jit(solution)/shard_map/cond/branch_1_fun/ppermute | solution.py:228
  18.9 7.3 %copy-start.1 = (bf16[128,2048]{1,0:T(8,128)(2,1)S(1)}, bf16[128,2048]{1,0:T(8,128)(2,1)}, u32[]{:S(2)}) copy-start(bf16[128,2048]{1,0:T(8,128)(2,1)} %query_hbm.1) | copy-start | bytes 1572868
  19.0 7.3 %copy-start.2 = (bf16[128,2048]{1,0:T(8,128)(2,1)S(1)}, bf16[128,2048]{1,0:T(8,128)(2,1)}, u32[]{:S(2)}) copy-start(bf16[128,2048]{1,0:T(8,128)(2,1)} %key_hbm.1) | copy-start | bytes 1572868
  19.0 22.5 %copy-start.3 = (f32[2048]{0:T(1024)S(1)}, f32[2048]{0:T(1024)}, u32[]{:S(2)}) copy-start(f32[2048]{0:T(1024)} %param.15) | copy-start | bytes 24580
  19.0 22.5 %copy-start.4 = (f32[2048]{0:T(1024)S(1)}, f32[2048]{0:T(1024)}, u32[]{:S(2)}) copy-start(f32[2048]{0:T(1024)} %param.14) | copy-start | bytes 24580
  19.0 28.6 %all-to-all-start = ((bf16[16,3,128,128]{3,2,1,0:T(8,128)(2,1)}), bf16[16,3,128,128]{3,2,1,0:T(8,128)(2,1)S(1)}, u32[]{:S(2)}, u32[]{:S(2)}) async-start(bf16[16,3,128,128]{3,2,1,0:T(8,128)(2,1)} %pack_heads.1), calls=%async_computation | async-start | bytes 3145728 | tf_op jit(solution)/shard_map/all_to_all | solution.py:269
  26.2 8.0 %collective-permute-start.6 = (f32[4,2,128]{2,1,0:T(2,128)S(1)}, f32[4,2,128]{2,1,0:T(2,128)S(1)}, u32[]{:S(2)}, u32[]{:S(2)}) collective-permute-start(f32[4,2,128]{2,1,0:T(2,128)S(1)} %param.3), channel_id=1, source_target_pairs={{0,4},{2,6},{4,0},{6,2},{8,12},{10,14},{12,8},{14,10},{16,20},{18,... | collective-permute-start | bytes 12296 | tf_op jit(solution)/shard_map/cond/branch_1_fun/ppermute | solution.py:228
  34.3 6.3 %collective-permute-start.7 = (f32[4,2,2,128]{3,2,0,1:T(2,128)S(1)}, f32[4,2,2,128]{3,2,0,1:T(2,128)S(1)}, u32[]{:S(2)}, u32[]{:S(2)}) collective-permute-start(f32[4,2,2,128]{3,2,0,1:T(2,128)S(1)} %pad_maximum_fusion.9), channel_id=1, source_target_pairs={{0,2},{2,0},{4,6},{6,4},{8,10},{10,8},{12,14},{14,12},{16,18},{18,... | collective-permute-start | bytes 24584 | tf_op jit(solution)/shard_map/cond/branch_1_fun/ppermute | solution.py:228
  40.7 1.2 %collective-permute-start.8 = (f32[16,2,128]{2,1,0:T(2,128)S(1)}, f32[16,2,128]{2,1,0:T(2,128)S(1)}, u32[]{:S(2)}, u32[]{:S(2)}) collective-permute-start(f32[16,2,128]{2,1,0:T(2,128)S(1)} %get-tuple-element.52), channel_id=1, source_target_pairs={{0,1},{1,0},{2,3},{3,2},{4,5},{5,4},{6,7},{7,6},{8,9},{9,8},{10,11... | collective-permute-start | bytes 49160 | tf_op jit(solution)/shard_map/ppermute | solution.py:290
